TPU v7x, 32 devices: a whole 2x2x4 slice. The times are simulated.
32 devices in a mesh: dp: 2 (over y), row: 4 (over z), col: 4 (over x, core).
Axes of the slice: x: 2, y: 2, z: 4, core: 2. Of those that a mesh axis runs over, the one named last changes fastest.
Arguments:
- hidden_in: bfloat16 [4096, 2048], P(('dp', 'row'), 'col'), may hold values from -6 to 6
- gain_attn: bfloat16 [2048], P('col'), may hold values from 0.5 to 1.5
- router_attn: bfloat16 [2048, 8], P('col'), may hold values from -0.09375 to 0.09375
- query_weight: bfloat16 [8, 2048, 2048], P(None, 'col', 'row'), may hold values from -0.125 to 0.125
- kv_weight: bfloat16 [2, 2048, 2048], P(None, 'col', 'row'), may hold values from -0.125 to 0.125
- out_weight: bfloat16 [8, 2048, 2048], P(None, 'row', 'col'), may hold values from -1.5 to 1.5
- gain_ffn: bfloat16 [2048], P('col'), may hold values from 0.5 to 1.5
- router_ffn: bfloat16 [2048, 8], P('col'), may hold values from -0.09375 to 0.09375
- gate_weight: bfloat16 [8, 2048, 5632], P(None, 'col', 'row'), may hold values from -0.125 to 0.125
- up_weight: bfloat16 [8, 2048, 5632], P(None, 'col', 'row'), may hold values from -0.125 to 0.125
- down_weight: bfloat16 [8, 5632, 2048], P(None, 'row', 'col'), may hold values from -0.078125 to 0.078125
- attn_routes: int32 [4096, 2], P('dp'), may hold values from 0 to 7, all different within a row
- ffn_routes: int32 [4096, 2], P('dp'), may hold values from 0 to 7, all different within a row
- attn_order: int32 [2, 4096], P('dp'), may hold values from 0 to 4095, each once within a row
- ffn_order: int32 [2, 4096], P('dp'), may hold values from 0 to 4095, each once within a row
- segment_ids: int32 [8, 512], P(('dp', 'col')), may hold values from 0 to 4, as said below
- d_out: bfloat16 [4096, 2048], P(('dp', 'row'), 'col'), may hold values from -6 to 6
Outputs:
- layer_out: bfloat16 [4096, 2048], P(('dp', 'row'), 'col')
- input_grad: float32 [4096, 2048], P(('dp', 'row'), 'col')
- gain_attn_grad: float32 [2048], P('col')
- router_attn_grad: float32 [2048, 8], P('col', 'dp')
- query_grad: float32 [8, 2048, 2048], P('dp', 'col', 'row')
- kv_grad: float32 [2, 2048, 2048], P('dp', 'col', 'row')
- out_grad: float32 [8, 2048, 2048], P('dp', 'row', 'col')
- gain_ffn_grad: float32 [2048], P('col')
- router_ffn_grad: float32 [2048, 8], P('col', 'dp')
- gate_grad: float32 [8, 2048, 5632], P('dp', 'col', 'row')
- up_grad: float32 [8, 2048, 5632], P('dp', 'col', 'row')
- down_grad: float32 [8, 5632, 2048], P('dp', 'row', 'col')
Inputs may be any that keep to these rules, and one draw needn't show every extreme that they name: `segment_ids`: in each group the prompt (segment 0) comes first and segments 1 to 4 follow in order, each at least one token long.
All inputs are finite; a program needn't handle non-finite values.
Results may differ from a plain program's by a relative error of at most 0.015.
Values may be sent and summed in bfloat16 or wider, within the bound.
No kernel may reach another device: no remote copies, remote signals or barrier semaphores. Data moves between devices by JAX's collectives and lax.ppermute only.
A program may use at most 448 MiB of HBM per device.

v0:
```python
import math

import jax
import jax.numpy as jnp
from jax import lax
from jax.sharding import PartitionSpec as P

D = 2048
HD = 128
SEQ = 512
CONT = 4


EPSILON = 1e-06
NEGATIVE = -1e30


def rotate_half(values):
    half_size = values.shape[-1] // 2
    return jnp.concatenate([-values[..., half_size:], values[..., :half_size]], axis=-1)


def rotary(values, cosine, sine_rows):
    return values * cosine + rotate_half(values) * sine_rows


def unrotary(values, cosine, sine_rows):
    return values * cosine - rotate_half(values) * sine_rows


def rope_tables(segment_ids):
    labels = jnp.arange(CONT + 1, dtype=jnp.int32)
    member = (segment_ids[:, :, None] == labels[None, None, :]).astype(jnp.int32)
    before = jnp.cumsum(member, axis=1) - member
    within = jnp.sum(before * member, axis=2)
    prompt = jnp.sum((segment_ids == 0).astype(jnp.int32), axis=1, keepdims=True)
    places = (within + jnp.where(segment_ids > 0, prompt, 0)).astype(jnp.float32).reshape(-1)
    frequency = jnp.exp(jnp.arange(HD // 2, dtype=jnp.float32) * (-2.0 * math.log(10000.0) / HD))
    angles = places[:, None] * frequency[None, :]
    angles = jnp.concatenate([angles, angles], axis=1)
    return (jnp.cos(angles), jnp.sin(angles))


def slot_tables(routes, pair_order, experts, capacity):
    flat_routes = routes.reshape(-1)
    chosen = jnp.take(flat_routes, pair_order, axis=0)
    labels = jnp.arange(experts, dtype=jnp.int32)
    member = (chosen[:, None] == labels[None, :]).astype(jnp.int32)
    ranked = jnp.sum((jnp.cumsum(member, axis=0) - member) * member, axis=1)
    slot_count = experts * capacity
    placed = jnp.where(ranked < capacity, chosen * capacity + ranked, slot_count)
    pair_slot = jnp.zeros(flat_routes.shape, jnp.int32).at[pair_order].set(placed)
    pair_ids = jnp.arange(flat_routes.shape[0], dtype=jnp.int32)
    slot_pair = (
        jnp.full((slot_count + 1,), flat_routes.shape[0], jnp.int32).at[pair_slot].set(pair_ids)
    )
    return (pair_slot, slot_pair[:slot_count])


def take_rows(source_rows, row_index):
    return jnp.take(source_rows, row_index, axis=0, mode="fill", fill_value=0)


def block_mask(segments, block_start, group_base, block_rows):
    place_query = block_start - group_base + jnp.arange(block_rows, dtype=jnp.int32)
    place_key = jnp.arange(SEQ, dtype=jnp.int32)
    causal = place_key[None, :] <= place_query[:, None]
    shared = (segments[None, :] == 0) | (segments[None, :] == segments[:, None])
    return causal & shared


def row_gather(values):
    return lax.all_gather(values, "row", axis=0, tiled=True)


def row_total(values):
    return lax.psum_scatter(values, "row", scatter_dimension=0, tiled=True)


def col_total(values):
    return lax.psum(values, "col")


def gate_total(values):
    return lax.psum(values, "row")


def data_total(first, second, third, fourth):
    return (
        lax.psum_scatter(first.astype(jnp.bfloat16), "dp", scatter_dimension=0, tiled=True).astype(
            jnp.float32
        ),
        lax.psum_scatter(second.astype(jnp.bfloat16), "dp", scatter_dimension=0, tiled=True).astype(
            jnp.float32
        ),
        lax.psum_scatter(third.astype(jnp.bfloat16), "dp", scatter_dimension=0, tiled=True).astype(
            jnp.float32
        ),
        lax.psum_scatter(fourth.astype(jnp.bfloat16), "dp", scatter_dimension=0, tiled=True).astype(
            jnp.float32
        ),
    )


def norm_forward(rows_in, gain_row):
    squares = col_total(jnp.sum(rows_in * rows_in, axis=1))
    factor = lax.rsqrt(squares / D + EPSILON)[:, None]
    return (factor, (rows_in * factor * gain_row).astype(jnp.bfloat16))


def norm_backward(rows_in, factor, gain_row, grad_in):
    scaled = grad_in * gain_row
    inner_sum = col_total(jnp.sum(scaled * rows_in, axis=1))[:, None]
    gain_grad = jnp.sum(grad_in * rows_in * factor, axis=0)
    return (factor * scaled - rows_in * factor**3 * inner_sum / D, gain_grad)


def gate_values(logits, routes):
    labels = jnp.arange(logits.shape[1], dtype=jnp.int32)
    member = (routes[:, :, None] == labels[None, None, :]).astype(jnp.float32)
    picked = jnp.sum(member * logits[:, None, :], axis=2)
    return (member, jax.nn.softmax(picked, axis=1))


def logit_grad(member, gate_prob, kept_mask, grad_in):
    masked = grad_in * kept_mask
    picked = gate_prob * (masked - jnp.sum(gate_prob * masked, axis=1, keepdims=True))
    return jnp.sum(member * picked[:, :, None], axis=1)


def attention_forward(queries, key_heads, values, segments):
    block_rows = min(512, SEQ)
    score_scale = HD ** (-0.5)
    starts = jnp.arange(queries.shape[0] // block_rows, dtype=jnp.int32) * block_rows

    def one_block(block_start):
        group_base = block_start // SEQ * SEQ
        allowed = block_mask(segments, block_start, group_base, block_rows)[:, None, None, :]
        scores = (
            jnp.einsum("qkhe,she->qkhs", queries, key_heads, preferred_element_type=jnp.float32)
            * score_scale
        )
        scores = jnp.where(allowed, scores, NEGATIVE)
        highest = jnp.max(scores, axis=-1, keepdims=True)
        weights = jnp.exp(scores - highest)
        totals = jnp.sum(weights, axis=-1, keepdims=True)
        prob_rows = (weights / totals).astype(jnp.bfloat16)
        mixed_rows = jnp.einsum(
            "qkhs,she->qkhe", prob_rows, values, preferred_element_type=jnp.float32
        )
        return (mixed_rows, (highest + jnp.log(totals))[..., 0])

    mixed_rows, log_sums = lax.map(one_block, starts)
    return (mixed_rows.reshape(queries.shape), log_sums.reshape(queries.shape[:3]))


def attention_backward(queries, key_heads, values, segments, grad_heads, log_sums):
    block_rows = min(512, SEQ)
    score_scale = HD ** (-0.5)
    starts = jnp.arange(queries.shape[0] // block_rows, dtype=jnp.int32) * block_rows

    def back_block(running, block_start):
        grad_keys, grad_values = running
        group_base = block_start // SEQ * SEQ
        allowed = block_mask(segments, block_start, group_base, block_rows)[:, None, None, :]
        scores = (
            jnp.einsum("qkhe,she->qkhs", queries, key_heads, preferred_element_type=jnp.float32)
            * score_scale
        )
        scores = jnp.where(allowed, scores, NEGATIVE)
        prob_rows = jnp.exp(scores - log_sums[..., None])
        value_part = jnp.einsum(
            "qkhs,qkhe->she",
            prob_rows.astype(jnp.bfloat16),
            grad_heads,
            preferred_element_type=jnp.float32,
        )
        grad_probs = jnp.einsum(
            "qkhe,she->qkhs", grad_heads, values, preferred_element_type=jnp.float32
        )
        centred = jnp.sum(prob_rows * grad_probs, axis=-1, keepdims=True)
        grad_scores = (prob_rows * (grad_probs - centred)).astype(jnp.bfloat16)
        query_part = (
            jnp.einsum("qkhs,she->qkhe", grad_scores, key_heads, preferred_element_type=jnp.float32)
            * score_scale
        )
        key_part = (
            jnp.einsum("qkhs,qkhe->she", grad_scores, queries, preferred_element_type=jnp.float32)
            * score_scale
        )
        grad_keys = grad_keys + key_part
        grad_values = grad_values + value_part
        return ((grad_keys, grad_values), query_part)

    empty = jnp.zeros(key_heads.shape, jnp.float32)
    (grad_keys, grad_values), grad_queries = lax.scan(back_block, (empty, empty), starts)
    return (grad_queries.reshape(queries.shape), grad_keys, grad_values)


def local(
    hidden_in,
    gain_attn,
    router_attn,
    query_weight,
    kv_weight,
    out_weight,
    gain_ffn,
    router_ffn,
    gate_weight,
    up_weight,
    down_weight,
    attn_routes,
    ffn_routes,
    attn_order,
    ffn_order,
    segment_ids,
    d_out,
):
    batch_rows = attn_routes.shape[0]
    col_rows = batch_rows // lax.axis_size("col")
    col_start = lax.axis_index("col") * col_rows
    row_rows = hidden_in.shape[0]
    row_start = lax.axis_index("row") * row_rows
    feature_cols = hidden_in.shape[1]
    attn_experts = query_weight.shape[0]
    ffn_experts = gate_weight.shape[0]
    attn_capacity = 5 * batch_rows // (2 * attn_experts)
    ffn_capacity = 5 * batch_rows // (2 * ffn_experts)
    head_width = query_weight.shape[2]
    head_count = head_width // HD
    hidden_cols = gate_weight.shape[2]
    attn_pair, attn_slot = slot_tables(attn_routes, attn_order[0], attn_experts, attn_capacity)
    ffn_pair, ffn_slot = slot_tables(ffn_routes, ffn_order[0], ffn_experts, ffn_capacity)
    attn_kept = (
        (attn_pair < attn_experts * attn_capacity).astype(jnp.float32).reshape(batch_rows, 2)
    )
    ffn_kept = (ffn_pair < ffn_experts * ffn_capacity).astype(jnp.float32).reshape(batch_rows, 2)
    attn_kept = lax.dynamic_slice_in_dim(attn_kept, col_start, col_rows, 0)
    ffn_kept = lax.dynamic_slice_in_dim(ffn_kept, col_start, col_rows, 0)
    attn_mine = lax.dynamic_slice_in_dim(attn_routes, col_start, col_rows, 0)
    ffn_mine = lax.dynamic_slice_in_dim(ffn_routes, col_start, col_rows, 0)
    cosine, sine_rows = rope_tables(segment_ids)
    segments = segment_ids.reshape(-1)
    rows_in = hidden_in.astype(jnp.float32)
    gain_a = gain_attn.astype(jnp.float32)
    factor_a, normed = norm_forward(rows_in, gain_a)
    normed_all = row_gather(normed)
    slots_a = take_rows(normed_all, attn_slot // 2).reshape(
        attn_experts, attn_capacity, feature_cols
    )
    query_slots = jnp.einsum(
        "ecd,edw->ecw", slots_a, query_weight, preferred_element_type=jnp.float32
    ).reshape(-1, head_width)
    query_pairs = take_rows(query_slots, attn_pair).reshape(batch_rows, 2, head_width)
    key_value = jnp.einsum("td,jdw->tjw", normed_all, kv_weight, preferred_element_type=jnp.float32)
    logit_part = jnp.dot(normed_all, router_attn, preferred_element_type=jnp.float32)
    query_sum, kv_sum, logits_a = (
        lax.psum_scatter(query_pairs, "col", scatter_dimension=0, tiled=True),
        lax.psum_scatter(key_value, "col", scatter_dimension=0, tiled=True),
        lax.psum_scatter(logit_part, "col", scatter_dimension=0, tiled=True),
    )
    member_a, gate_a = gate_values(logits_a, attn_mine)
    scaled_a = gate_a * attn_kept
    cos_query = cosine[:, None, None, :]
    sin_query = sine_rows[:, None, None, :]
    cos_key = cosine[:, None, :]
    sin_key = sine_rows[:, None, :]
    queries = rotary(query_sum.reshape(col_rows, 2, head_count, HD), cos_query, sin_query).astype(
        jnp.bfloat16
    )
    key_heads = rotary(kv_sum[:, 0].reshape(col_rows, head_count, HD), cos_key, sin_key).astype(
        jnp.bfloat16
    )
    value_heads = kv_sum[:, 1].reshape(col_rows, head_count, HD).astype(jnp.bfloat16)
    attended, log_sums = attention_forward(queries, key_heads, value_heads, segments)
    attended = attended.reshape(col_rows, 2, head_width)
    gated_out = (scaled_a[:, :, None] * attended).astype(jnp.bfloat16)
    gated_all = lax.all_gather(gated_out, "col", axis=0, tiled=True)
    out_slots = take_rows(gated_all.reshape(-1, head_width), attn_slot).reshape(
        attn_experts, attn_capacity, head_width
    )
    projected = jnp.einsum(
        "ecw,ewd->ecd", out_slots, out_weight, preferred_element_type=jnp.float32
    ).reshape(-1, feature_cols)
    attn_part = take_rows(projected, attn_pair).reshape(batch_rows, 2, feature_cols).sum(axis=1)
    middle = rows_in + row_total(attn_part)
    gain_f = gain_ffn.astype(jnp.float32)
    factor_f, normed_f = norm_forward(middle, gain_f)
    normed_f_all = row_gather(normed_f)
    slots_f = take_rows(normed_f_all, ffn_slot // 2).reshape(
        ffn_experts, ffn_capacity, feature_cols
    )
    gate_slots = jnp.einsum(
        "ecd,edf->ecf", slots_f, gate_weight, preferred_element_type=jnp.float32
    ).reshape(-1, hidden_cols)
    up_slots = jnp.einsum(
        "ecd,edf->ecf", slots_f, up_weight, preferred_element_type=jnp.float32
    ).reshape(-1, hidden_cols)
    gate_pairs = take_rows(gate_slots, ffn_pair).reshape(batch_rows, 2, hidden_cols)
    up_pairs = take_rows(up_slots, ffn_pair).reshape(batch_rows, 2, hidden_cols)
    flogit_part = jnp.dot(normed_f_all, router_ffn, preferred_element_type=jnp.float32)
    gate_sum, up_sum, logits_f = (
        lax.psum_scatter(gate_pairs, "col", scatter_dimension=0, tiled=True),
        lax.psum_scatter(up_pairs, "col", scatter_dimension=0, tiled=True),
        lax.psum_scatter(flogit_part, "col", scatter_dimension=0, tiled=True),
    )
    member_f, gate_f = gate_values(logits_f, ffn_mine)
    scaled_f = gate_f * ffn_kept
    sigmoid_gate = jax.nn.sigmoid(gate_sum)
    swish_gate = gate_sum * sigmoid_gate
    activation = swish_gate * up_sum
    gated_act = (activation * scaled_f[:, :, None]).astype(jnp.bfloat16)
    act_all = lax.all_gather(gated_act, "col", axis=0, tiled=True)
    down_slots_in = take_rows(act_all.reshape(-1, hidden_cols), ffn_slot).reshape(
        ffn_experts, ffn_capacity, hidden_cols
    )
    down_slots = jnp.einsum(
        "ecf,efd->ecd", down_slots_in, down_weight, preferred_element_type=jnp.float32
    ).reshape(-1, feature_cols)
    ffn_part = take_rows(down_slots, ffn_pair).reshape(batch_rows, 2, feature_cols).sum(axis=1)
    layer_out = (middle + row_total(ffn_part)).astype(jnp.bfloat16)
    grad_out_all = row_gather(d_out)
    grad_slots = take_rows(grad_out_all, ffn_slot // 2).reshape(
        ffn_experts, ffn_capacity, feature_cols
    )
    down_grad = jnp.einsum(
        "ecf,ecd->efd", down_slots_in, grad_slots, preferred_element_type=jnp.float32
    )
    act_grad_slots = jnp.einsum(
        "ecd,efd->ecf", grad_slots, down_weight, preferred_element_type=jnp.float32
    ).reshape(-1, hidden_cols)
    act_grad_pairs = take_rows(act_grad_slots, ffn_pair).reshape(batch_rows, 2, hidden_cols)
    grad_gated_act = lax.psum_scatter(act_grad_pairs, "col", scatter_dimension=0, tiled=True)
    ffn_gate_grad = gate_total(jnp.sum(grad_gated_act * activation, axis=2))
    ffn_logit_grad = logit_grad(member_f, gate_f, ffn_kept, ffn_gate_grad)
    grad_activation = grad_gated_act * scaled_f[:, :, None]
    swish_slope = sigmoid_gate * (1.0 + gate_sum * (1.0 - sigmoid_gate))
    grad_gate_pre = (grad_activation * up_sum * swish_slope).astype(jnp.bfloat16)
    grad_up_pre = (grad_activation * swish_gate).astype(jnp.bfloat16)
    gate_pre_all, up_pre_all, ffn_logit_all = (
        lax.all_gather(grad_gate_pre, "col", axis=0, tiled=True),
        lax.all_gather(grad_up_pre, "col", axis=0, tiled=True),
        lax.all_gather(ffn_logit_grad.astype(jnp.bfloat16), "col", axis=0, tiled=True),
    )
    gate_grad_slots = take_rows(gate_pre_all.reshape(-1, hidden_cols), ffn_slot).reshape(
        ffn_experts, ffn_capacity, hidden_cols
    )
    up_grad_slots = take_rows(up_pre_all.reshape(-1, hidden_cols), ffn_slot).reshape(
        ffn_experts, ffn_capacity, hidden_cols
    )
    gate_grad = jnp.einsum(
        "ecd,ecf->edf", slots_f, gate_grad_slots, preferred_element_type=jnp.float32
    )
    up_grad = jnp.einsum("ecd,ecf->edf", slots_f, up_grad_slots, preferred_element_type=jnp.float32)
    normed_f_slots = jnp.einsum(
        "ecf,edf->ecd", gate_grad_slots, gate_weight, preferred_element_type=jnp.float32
    )
    normed_f_slots = normed_f_slots + jnp.einsum(
        "ecf,edf->ecd", up_grad_slots, up_weight, preferred_element_type=jnp.float32
    )
    normed_f_part = (
        take_rows(normed_f_slots.reshape(-1, feature_cols), ffn_pair)
        .reshape(batch_rows, 2, feature_cols)
        .sum(axis=1)
    )
    router_ffn_grad = jnp.einsum(
        "te,td->ed", ffn_logit_all, normed_f_all, preferred_element_type=jnp.float32
    )
    ffn_logit_mine = lax.dynamic_slice_in_dim(ffn_logit_all, row_start, row_rows, 0)
    grad_normed_f = row_total(normed_f_part) + jnp.einsum(
        "te,de->td", ffn_logit_mine, router_ffn, preferred_element_type=jnp.float32
    )
    middle_norm_grad, gain_ffn_grad = norm_backward(middle, factor_f, gain_f, grad_normed_f)
    grad_middle = d_out.astype(jnp.float32) + middle_norm_grad
    grad_middle_all = row_gather(grad_middle.astype(jnp.bfloat16))
    attn_grad_slots = take_rows(grad_middle_all, attn_slot // 2).reshape(
        attn_experts, attn_capacity, feature_cols
    )
    out_grad = jnp.einsum(
        "ecw,ecd->ewd", out_slots, attn_grad_slots, preferred_element_type=jnp.float32
    )
    gated_grad_slots = jnp.einsum(
        "ecd,ewd->ecw", attn_grad_slots, out_weight, preferred_element_type=jnp.float32
    ).reshape(-1, head_width)
    gated_grad_pairs = take_rows(gated_grad_slots, attn_pair).reshape(batch_rows, 2, head_width)
    grad_gated = lax.psum_scatter(gated_grad_pairs, "col", scatter_dimension=0, tiled=True)
    attn_gate_grad = gate_total(jnp.sum(grad_gated * attended, axis=2))
    attn_logit_grad = logit_grad(member_a, gate_a, attn_kept, attn_gate_grad)
    grad_heads = (
        (grad_gated * scaled_a[:, :, None])
        .astype(jnp.bfloat16)
        .reshape(col_rows, 2, head_count, HD)
    )
    grad_queries, grad_keys, grad_values = attention_backward(
        queries, key_heads, value_heads, segments, grad_heads, log_sums
    )
    grad_queries = (
        unrotary(grad_queries, cos_query, sin_query)
        .reshape(col_rows, 2, head_width)
        .astype(jnp.bfloat16)
    )
    grad_keys = unrotary(grad_keys, cos_key, sin_key).reshape(col_rows, head_width)
    grad_kv = jnp.stack([grad_keys, grad_values.reshape(col_rows, head_width)], axis=1).astype(
        jnp.bfloat16
    )
    query_grad_all, kv_grad_all, attn_logit_all = (
        lax.all_gather(grad_queries, "col", axis=0, tiled=True),
        lax.all_gather(grad_kv, "col", axis=0, tiled=True),
        lax.all_gather(attn_logit_grad.astype(jnp.bfloat16), "col", axis=0, tiled=True),
    )
    query_grad_slots = take_rows(query_grad_all.reshape(-1, head_width), attn_slot).reshape(
        attn_experts, attn_capacity, head_width
    )
    query_grad = jnp.einsum(
        "ecd,ecw->edw", slots_a, query_grad_slots, preferred_element_type=jnp.float32
    )
    kv_grad = jnp.einsum("td,tjw->jdw", normed_all, kv_grad_all, preferred_element_type=jnp.float32)
    normed_slots = jnp.einsum(
        "ecw,edw->ecd", query_grad_slots, query_weight, preferred_element_type=jnp.float32
    ).reshape(-1, feature_cols)
    normed_part = (
        take_rows(normed_slots, attn_pair).reshape(batch_rows, 2, feature_cols).sum(axis=1)
    )
    normed_part = normed_part + jnp.einsum(
        "tjw,jdw->td", kv_grad_all, kv_weight, preferred_element_type=jnp.float32
    )
    router_attn_grad = jnp.einsum(
        "te,td->ed", attn_logit_all, normed_all, preferred_element_type=jnp.float32
    )
    attn_logit_mine = lax.dynamic_slice_in_dim(attn_logit_all, row_start, row_rows, 0)
    grad_normed = row_total(normed_part) + jnp.einsum(
        "te,de->td", attn_logit_mine, router_attn, preferred_element_type=jnp.float32
    )
    input_norm_grad, gain_attn_grad = norm_backward(rows_in, factor_a, gain_a, grad_normed)
    input_grad = grad_middle + input_norm_grad
    gain_attn_grad, gain_ffn_grad = lax.psum((gain_attn_grad, gain_ffn_grad), ("dp", "row"))
    gate_grad, up_grad, down_grad, router_ffn_grad = data_total(
        gate_grad, up_grad, down_grad, router_ffn_grad
    )
    query_grad, kv_grad, out_grad, router_attn_grad = data_total(
        query_grad, kv_grad, out_grad, router_attn_grad
    )
    return (
        layer_out,
        input_grad,
        gain_attn_grad,
        router_attn_grad.T,
        query_grad,
        kv_grad,
        out_grad,
        gain_ffn_grad,
        router_ffn_grad.T,
        gate_grad,
        up_grad,
        down_grad,
    )


def solution(mesh):
    in_specs = (
        P(("dp", "row"), "col"),
        P("col"),
        P("col", None),
        P(None, "col", "row"),
        P(None, "col", "row"),
        P(None, "row", "col"),
        P("col"),
        P("col", None),
        P(None, "col", "row"),
        P(None, "col", "row"),
        P(None, "row", "col"),
        P("dp", None),
        P("dp", None),
        P("dp", None),
        P("dp", None),
        P(("dp", "col"), None),
        P(("dp", "row"), "col"),
    )
    out_specs = (
        P(("dp", "row"), "col"),
        P(("dp", "row"), "col"),
        P("col"),
        P("col", "dp"),
        P("dp", "col", "row"),
        P("dp", "col", "row"),
        P("dp", "row", "col"),
        P("col"),
        P("col", "dp"),
        P("dp", "col", "row"),
        P("dp", "col", "row"),
        P("dp", "row", "col"),
    )
    return jax.shard_map(local, mesh=mesh, in_specs=in_specs, out_specs=out_specs, check_vma=False)
```

profile of v0, /device:TPU:0, one launch (start us, length us, event | category | flops | bytes accessed | tf_op | source)
XLA Modules:
  0.0 3634.8 jit_solution(12633805387707217922)
XLA Ops:
  20.8 46.4 %all-gather.11.cloned.1.call-done = bf16[2048,512]{1,0:T(8,128)(2,1)} async-done(((bf16[512,512]{1,0:T(8,128)(2,1)}), bf16[2048,512]{1,0:T(8,128)(2,1)}) %all-gather.11.cloned.1.call-update) | async-done | bytes 2097168 | tf_op jit(solution)/shard_map/all_gather | solution.py:73
  79.1 23.0 gather_fusion
  105.3 15.5 scatter_custom_fusion
  120.8 15.5 scatter_custom_fusion.1
  136.5 21.5 gather_fusion.1
  168.5 21.9 gather_fusion.2
  236.0 54.7 %reduce-scatter.20.cloned.1.call-done = f32[512,2,512]{0,2,1:T(8,128)} async-done(((f32[2048,2,512]{0,2,1:T(8,128)}), f32[512,2,512]{0,2,1:T(8,128)}) %reduce-scatter.20.cloned.1.call-update) | async-done | bytes 2097168 | tf_op jit(solution)/shard_map/reduce_scatter | solution.py:258
  304.0 34.4 all-gather.13.cloned.1.call-done
  356.7 24.3 gather_fusion.3
  391.5 21.9 gather_fusion.4
  429.9 15.5 reduce_sum.246
  447.2 75.2 %reduce-scatter.22.cloned.1.call-done = f32[512,512]{1,0:T(8,128)} async-done(((f32[2048,512]{1,0:T(8,128)}), f32[512,512]{1,0:T(8,128)}) %reduce-scatter.22.cloned.1.call-update) | async-done | bytes 1048592 | tf_op jit(solution)/shard_map/reduce_scatter | solution.py:77
  532.3 23.0 gather_fusion.5
  574.1 15.5 scatter_custom_fusion.3
  591.5 23.5 gather_fusion.11
  620.4 21.9 gather_fusion.6
  652.3 17.1 fusion.104
  669.4 35.0 gather_fusion.12
  704.4 18.7 fusion.101
  723.1 34.8 gather_fusion.8
  757.9 18.9 fusion.100
  776.8 34.8 gather_fusion.7
  811.7 44.1 %broadcast_select_fusion.5 = (f32[4096,1408]{1,0:T(8,128)}, f32[4096,1408]{1,0:T(8,128)}, f32[4096,1408]{1,0:T(8,128)}) fusion(f32[4096,1408]{1,0:T(8,128)} %gather_fusion.7, pred[4096]{0:T(1024)(128)(4,1)S(1)} %copy-done.58, f32[4096,1408]{1,0:T(8,128)} %gather_fusion.8, f32[4096,1408]{1,0:T(8,128)} %gather_fusion.12), kind=kLoop, calls=%fused_computation.32 | loop fusion | flops 17301504 | bytes 138416128 | tf_op jit(solution)/shard_map/jit(_take)/select_n | solution.py:61
  855.8 26.5 reshape.606
  882.4 26.9 reshape.608
  909.4 26.7 reshape.617
  940.8 330.2 %all-reduce.11.cloned.1.call-done = f32[2048,2,1408]{2,1,0:T(2,128)} async-done(((f32[2048,2,1408]{2,1,0:T(2,128)}), f32[2048,2,1408]{2,1,0:T(2,128)}) %all-reduce.11.cloned.1.call-update) | async-done | bytes 23068688
  1278.1 385.5 %all-reduce.13.cloned.1.call-done = f32[2048,2,1408]{2,1,0:T(2,128)} async-done(((f32[2048,2,1408]{2,1,0:T(2,128)}), f32[2048,2,1408]{2,1,0:T(2,128)}) %all-reduce.13.cloned.1.call-update) | async-done | bytes 23068688
  1670.7 385.3 %all-reduce.15.cloned.1.call-done = f32[2048,2,1408]{2,1,0:T(2,128)} async-done(((f32[2048,2,1408]{2,1,0:T(2,128)}), f32[2048,2,1408]{2,1,0:T(2,128)}) %all-reduce.15.cloned.1.call-update) | async-done | bytes 23068688
  2112.7 60.0 %all-gather.23.cloned.1.call-done = bf16[2048,2,1408]{2,1,0:T(2,128)(2,1)} async-done(((bf16[512,2,1408]{2,1,0:T(2,128)(2,1)}), bf16[2048,2,1408]{2,1,0:T(2,128)(2,1)}) %all-gather.23.cloned.1.call-update) | async-done | bytes 11534352 | tf_op jit(solution)/shard_map/all_gather | solution.py:342
  2172.7 24.1 reshape.620
  2196.8 35.2 gather_fusion.14
  2232.0 18.9 all-gather.21.cloned.1.call-done
  2250.9 24.1 reshape.618
  2275.0 35.2 gather_fusion.13
  2310.2 19.0 all-gather.17.cloned.1.call-done
  2329.2 23.8 reshape.611
  2352.9 35.3 gather_fusion.9
  2388.2 26.0 broadcast_select_fusion
  2414.2 17.9 fusion.103
  2432.1 21.9 gather_fusion.10
  2454.0 17.2 fusion.105
  2471.2 18.0 convolution_add_fusion
  2489.3 21.9 gather_fusion.15
  2533.4 15.5 reduce_sum.252
  2560.2 15.6 reduce_sum.251
  2581.1 44.7 %reduce-scatter.28.cloned.1.call-done = f32[512,512]{1,0:T(8,128)} async-done(((f32[2048,512]{1,0:T(8,128)}), f32[512,512]{1,0:T(8,128)}) %reduce-scatter.28.cloned.1.call-update) | async-done | bytes 1048592 | tf_op jit(solution)/shard_map/reduce_scatter | solution.py:77
  2635.0 70.8 %reduce-scatter.26.cloned.1.call-done = f32[512,512]{1,0:T(8,128)} async-done(((f32[2048,512]{1,0:T(8,128)}), f32[512,512]{1,0:T(8,128)}) %reduce-scatter.26.cloned.1.call-update) | async-done | bytes 1048592 | tf_op jit(solution)/shard_map/reduce_scatter | solution.py:77
  2709.1 46.6 %all-gather.25.cloned.1.call-done = bf16[2048,512]{1,0:T(8,128)(2,1)} async-done(((bf16[512,512]{1,0:T(8,128)(2,1)}), bf16[2048,512]{1,0:T(8,128)(2,1)}) %all-gather.25.cloned.1.call-update) | async-done | bytes 2097168 | tf_op jit(solution)/shard_map/all_gather | solution.py:73
  2755.6 23.5 gather_fusion.16
  2789.6 21.9 gather_fusion.17
  2841.8 69.9 %reduce-scatter.30.cloned.1.call-done = f32[512,2,512]{0,2,1:T(8,128)} async-done(((f32[2048,2,512]{0,2,1:T(8,128)}), f32[512,2,512]{0,2,1:T(8,128)}) %reduce-scatter.30.cloned.1.call-update) | async-done | bytes 2097168 | tf_op jit(solution)/shard_map/reduce_scatter | solution.py:386
  2949.6 16.0 convolution_convert_fusion
  2965.6 18.7 convolution_convert_fusion.2
  2984.4 18.8 convolution_convert_fusion.1
  3021.9 24.5 gather_fusion.18
  3069.9 22.2 gather_fusion.19
  3108.7 15.5 reduce_sum.258
  3149.4 42.4 %reduce-scatter.44.cloned.1.call-done = bf16[4,1408,512]{2,1,0:T(8,128)(2,1)} async-done(((bf16[8,1408,512]{2,1,0:T(8,128)(2,1)}), bf16[4,1408,512]{2,1,0:T(8,128)(2,1)}) %reduce-scatter.44.cloned.1.call-update) | async-done | bytes 5767184 | tf_op jit(solution)/shard_map/reduce_scatter | solution.py:96
  3200.5 127.3 %reduce-scatter.40.cloned.1.call-done = bf16[4,512,1408]{2,1,0:T(8,128)(2,1)} async-done(((bf16[8,512,1408]{2,1,0:T(8,128)(2,1)}), bf16[4,512,1408]{2,1,0:T(8,128)(2,1)}) %reduce-scatter.40.cloned.1.call-update) | async-done | bytes 5767184 | tf_op jit(solution)/shard_map/reduce_scatter | solution.py:90
  3335.7 127.8 %reduce-scatter.42.cloned.1.call-done = bf16[4,512,1408]{2,1,0:T(8,128)(2,1)} async-done(((bf16[8,512,1408]{2,1,0:T(8,128)(2,1)}), bf16[4,512,1408]{2,1,0:T(8,128)(2,1)}) %reduce-scatter.42.cloned.1.call-update) | async-done | bytes 5767184 | tf_op jit(solution)/shard_map/reduce_scatter | solution.py:93
  3498.6 67.5 %reduce-scatter.32.cloned.1.call-done = f32[512,512]{1,0:T(8,128)} async-done(((f32[2048,512]{1,0:T(8,128)}), f32[512,512]{1,0:T(8,128)}) %reduce-scatter.32.cloned.1.call-update) | async-done | bytes 1048592 | tf_op jit(solution)/shard_map/reduce_scatter | solution.py:77
  3568.1 21.8 all-reduce.5
  3598.6 25.0 reduce-scatter.34.cloned.1.call-done
  (425 shorter events, 544.7 us)
Async XLA Ops:
  7.2 63.0 %copy-start = (bf16[2,512,512]{2,1,0:T(8,128)(2,1)S(1)}, bf16[2,512,512]{2,1,0:T(8,128)(2,1)}, u32[]{:S(2)}) copy-start(bf16[2,512,512]{2,1,0:T(8,128)(2,1)} %param.33) | copy-start | bytes 3145732
  7.2 60.0 %all-gather.11.cloned.1.call-start = ((), (), s32[]{:S(2)}) async-start(), calls=%async_computation.15 | async-start | bytes 2621440 | tf_op jit(solution)/shard_map/all_gather | solution.py:73
  8.0 69.5 %copy-start.69 = (f32[512]{0:T(512)}, f32[512]{0:T(512)S(1)}, u32[]{:S(2)}) copy-start(f32[512]{0:T(512)S(1)} %convert_element_type.157) | copy-start | bytes 6148
  20.8 207.1 %reduce-scatter.16.cloned.1.call-start = ((), (), s32[]{:S(2)}) async-start(), calls=%async_computation.16 | async-start | bytes 81920 | tf_op jit(solution)/shard_map/reduce_scatter | solution.py:260
  70.1 159.2 %reduce-scatter.18.cloned.1.call-start = ((), (), s32[]{:S(2)}) async-start(), calls=%async_computation.17 | async-start | bytes 10485760 | tf_op jit(solution)/shard_map/reduce_scatter | solution.py:259
  77.5 213.1 %reduce-scatter.20.cloned.1.call-start = ((), (), s32[]{:S(2)}) async-start(), calls=%async_computation.18 | async-start | bytes 10485760 | tf_op jit(solution)/shard_map/reduce_scatter | solution.py:258
  79.1 57.4 %copy-start.1 = (bf16[2048,512]{1,0:T(8,128)(2,1)S(1)}, bf16[2048,512]{1,0:T(8,128)(2,1)}, u32[]{:S(2)}) copy-start(bf16[2048,512]{1,0:T(8,128)(2,1)} %all-gather.11.cloned.1.call-done) | copy-start | bytes 6291460
  120.8 270.7 %copy-start.35 = (s32[4096]{0:T(1024)}, s32[4096]{0:T(1024)S(1)}, u32[]{:S(2)}) copy-start(s32[4096]{0:T(1024)S(1)} %get-tuple-element.193) | copy-start | bytes 49156
  136.4 244.6 %copy-start.54 = (pred[5120]{0:T(1024)(128)(4,1)}, pred[5120]{0:T(1024)(128)(4,1)S(1)}, u32[]{:S(2)}) copy-start(pred[5120]{0:T(1024)(128)(4,1)S(1)} %get-tuple-element.183) | copy-start | bytes 15364
  136.5 276.9 %copy-start.48 = (pred[4096]{0:T(1024)(128)(4,1)}, pred[4096]{0:T(1024)(128)(4,1)S(1)}, u32[]{:S(2)}) copy-start(pred[4096]{0:T(1024)(128)(4,1)S(1)} %get-tuple-element.192) | copy-start | bytes 12292
  136.5 220.2 %copy-start.38 = (s32[5120]{0:T(1024)}, s32[5120]{0:T(1024)S(1)}, u32[]{:S(2)}) copy-start(s32[5120]{0:T(1024)S(1)} %get-tuple-element.185) | copy-start | bytes 61444
  220.0 118.3 %all-gather.13.cloned.1.call-start = ((), (), s32[]{:S(2)}) async-start(), calls=%async_computation.19 | async-start | bytes 5242880 | tf_op jit(solution)/shard_map/all_gather | solution.py:278
  226.9 67.3 %copy-start.22 = (f32[512,128]{0,1:T(8,128)}, f32[512,128]{0,1:T(8,128)S(1)}, u32[]{:S(2)}) copy-start(f32[512,128]{0,1:T(8,128)S(1)} %get-tuple-element.177) | copy-start | bytes 786436
  229.3 71.9 %copy-start.60 = (f32[512,2]{0,1:T(2,128)}, f32[512,2]{0,1:T(2,128)S(1)}, u32[]{:S(2)}) copy-start(f32[512,2]{0,1:T(2,128)S(1)} %get-tuple-element.158) | copy-start | bytes 12292
  231.2 61.5 %copy-start.30 = (f32[512,128]{0,1:T(8,128)S(1)}, f32[512,128]{0,1:T(8,128)}, u32[]{:S(2)}) copy-start(f32[512,128]{0,1:T(8,128)} %get-tuple-element.178) | copy-start | bytes 786436
  234.8 64.0 %copy-start.32 = (bf16[512,4,128]{2,1,0:T(4,128)(2,1)}, bf16[512,4,128]{2,1,0:T(4,128)(2,1)S(1)}, u32[]{:S(2)}) copy-start(bf16[512,4,128]{2,1,0:T(4,128)(2,1)S(1)} %convert_element_type.161) | copy-start | bytes 1572868
  303.7 218.6 %reduce-scatter.22.cloned.1.call-start = ((), (), s32[]{:S(2)}) async-start(), calls=%async_computation.20 | async-start | bytes 5242880 | tf_op jit(solution)/shard_map/reduce_scatter | solution.py:77
  445.4 76.9 %copy-start.18 = (bf16[512,512]{1,0:T(8,128)(2,1)S(1)}, bf16[512,512]{1,0:T(8,128)(2,1)}, u32[]{:S(2)}) copy-start(bf16[512,512]{1,0:T(8,128)(2,1)} %param.29) | copy-start | bytes 1572868
  445.4 86.9 %copy-start.47 = (s32[1,4096]{1,0:T(1,128)S(1)}, s32[1,4096]{1,0:T(1,128)}, u32[]{:S(2)}) copy-start(s32[1,4096]{1,0:T(1,128)} %param.43) | copy-start | bytes 49156
  445.5 146.0 %all-gather.19.cloned.1.call-start = ((), (), s32[]{:S(2)}) async-start(), calls=%async_computation.25 | async-start | bytes 2621440 | tf_op jit(solution)/shard_map/all_gather | solution.py:73
  446.2 171.1 %all-gather.15.cloned.1.call-start = ((), (), s32[]{:S(2)}) async-start(), calls=%async_computation.21 | async-start | bytes 2621440 | tf_op jit(solution)/shard_map/all_gather | solution.py:73
  446.3 109.1 %copy-start.78 = (f32[512]{0:T(512)}, f32[512]{0:T(512)S(1)}, u32[]{:S(2)}) copy-start(f32[512]{0:T(512)S(1)} %convert_element_type.169) | copy-start | bytes 6148
  532.2 407.7 %reduce-scatter.24.cloned.1.call-start = ((), (), s32[]{:S(2)}) async-start(), calls=%async_computation.22 | async-start | bytes 81920 | tf_op jit(solution)/shard_map/reduce_scatter | solution.py:305
  574.1 202.8 %copy-start.33 = (s32[4096]{0:T(1024)}, s32[4096]{0:T(1024)S(1)}, u32[]{:S(2)}) copy-start(s32[4096]{0:T(1024)S(1)} %get-tuple-element.189) | copy-start | bytes 49156
  620.3 650.6 %all-reduce.11.cloned.1.call-start = ((), (), s32[]{:S(2)}) async-start(), calls=%async_computation.40 | async-start | bytes 46137344
  882.3 781.2 %all-reduce.13.cloned.1.call-start = ((), (), s32[]{:S(2)}) async-start(), calls=%async_computation.41 | async-start | bytes 46137344
  909.3 1146.7 %all-reduce.15.cloned.1.call-start = ((), (), s32[]{:S(2)}) async-start(), calls=%async_computation.42 | async-start | bytes 46137344
  936.2 1236.5 %all-gather.23.cloned.1.call-start = ((), (), s32[]{:S(2)}) async-start(), calls=%async_computation.27 | async-start | bytes 14417920 | tf_op jit(solution)/shard_map/all_gather | solution.py:342
  940.0 338.1 %copy-start.67 = (s32[512,2]{0,1:T(2,128)}, s32[512,2]{0,1:T(2,128)S(1)}, u32[]{:S(2)}) copy-start(s32[512,2]{0,1:T(2,128)S(1)} %constant_dynamic-slice_fusion.1) | copy-start | bytes 12292
  2099.1 151.9 %all-gather.21.cloned.1.call-start = ((), (), s32[]{:S(2)}) async-start(), calls=%async_computation.26 | async-start | bytes 14417920 | tf_op jit(solution)/shard_map/all_gather | solution.py:341
  2105.5 223.7 %all-gather.17.cloned.1.call-start = ((), (), s32[]{:S(2)}) async-start(), calls=%async_computation.23 | async-start | bytes 14417920 | tf_op jit(solution)/shard_map/all_gather | solution.py:313
  2112.5 84.3 %copy-start.37 = (s32[5120]{0:T(1024)S(1)}, s32[5120]{0:T(1024)}, u32[]{:S(2)}) copy-start(s32[5120]{0:T(1024)} %get-tuple-element.181) | copy-start | bytes 61444
  2112.5 513.4 %reduce-scatter.28.cloned.1.call-start = ((), (), s32[]{:S(2)}) async-start(), calls=%async_computation.28 | async-start | bytes 5242880 | tf_op jit(solution)/shard_map/reduce_scatter | solution.py:77
  2548.9 156.9 %reduce-scatter.26.cloned.1.call-start = ((), (), s32[]{:S(2)}) async-start(), calls=%async_computation.24 | async-start | bytes 5242880 | tf_op jit(solution)/shard_map/reduce_scatter | solution.py:77
  2560.2 65.7 %copy-start.16 = (f32[512,512]{1,0:T(8,128)S(1)}, f32[512,512]{1,0:T(8,128)}, u32[]{:S(2)}) copy-start(f32[512,512]{1,0:T(8,128)} %copy-done.15) | copy-start | bytes 3145732
  2560.2 65.7 %copy-start.74 = (bf16[512,8]{0,1:T(8,128)(2,1)S(1)}, bf16[512,8]{0,1:T(8,128)(2,1)}, u32[]{:S(2)}) copy-start(bf16[512,8]{0,1:T(8,128)(2,1)} %param.36) | copy-start | bytes 24580
  2560.2 65.7 %copy-start.77 = (f32[512]{0:T(512)S(1)}, f32[512]{0:T(512)}, u32[]{:S(2)}) copy-start(f32[512]{0:T(512)} %copy-done.76) | copy-start | bytes 6148
  2560.2 65.7 %copy-start.79 = (f32[512]{0:T(512)S(1)}, f32[512]{0:T(512)}, u32[]{:S(2)}) copy-start(f32[512]{0:T(512)} %copy-done.78) | copy-start | bytes 6148
  2575.8 130.0 %copy-start.86 = (f32[512]{0:T(512)S(1)}, f32[512]{0:T(512)}, u32[]{:S(2)}) copy-start(f32[512]{0:T(512)} %get-tuple-element.209) | copy-start | bytes 6148
  2575.9 179.8 %copy-start.41 = (s32[5120]{0:T(1024)S(1)}, s32[5120]{0:T(1024)}, u32[]{:S(2)}) copy-start(s32[5120]{0:T(1024)} %copy-done.40) | copy-start | bytes 61444
  2575.9 179.7 %all-gather.25.cloned.1.call-start = ((), (), s32[]{:S(2)}) async-start(), calls=%async_computation.29 | async-start | bytes 2621440 | tf_op jit(solution)/shard_map/all_gather | solution.py:73
  2581.1 197.9 %copy-start.42 = (bf16[2048,8]{0,1:T(8,128)(2,1)}, bf16[2048,8]{0,1:T(8,128)(2,1)S(1)}, u32[]{:S(2)}) copy-start(bf16[2048,8]{0,1:T(8,128)(2,1)S(1)} %all_gather.43) | copy-start | bytes 98308
  2709.0 70.1 %copy-start.57 = (pred[5120]{0:T(1024)(128)(4,1)S(1)}, pred[5120]{0:T(1024)(128)(4,1)}, u32[]{:S(2)}) copy-start(pred[5120]{0:T(1024)(128)(4,1)} %copy-done.56) | copy-start | bytes 15364
  2709.0 202.7 %reduce-scatter.30.cloned.1.call-start = ((), (), s32[]{:S(2)}) async-start(), calls=%async_computation.30 | async-start | bytes 10485760 | tf_op jit(solution)/shard_map/reduce_scatter | solution.py:386
  2841.1 70.6 %copy-start.14 = (f32[512,2,4,128]{0,3,2,1:T(8,128)S(1)}, f32[512,2,4,128]{0,3,2,1:T(8,128)}, u32[]{:S(2)}) copy-start(f32[512,2,4,128]{0,3,2,1:T(8,128)} %copy-done.13) | copy-start | bytes 6291460
  2841.1 70.6 %copy-start.61 = (f32[512,2]{0,1:T(2,128)S(1)}, f32[512,2]{0,1:T(2,128)}, u32[]{:S(2)}) copy-start(f32[512,2]{0,1:T(2,128)} %copy-done.60) | copy-start | bytes 12292
  2841.1 162.2 %all-gather.27.cloned.1.call-start = ((), (), s32[]{:S(2)}) async-start(), calls=%async_computation.31 | async-start | bytes 5242880 | tf_op jit(solution)/shard_map/all_gather | solution.py:407
  2928.3 118.1 %all-gather.29.cloned.1.call-start = ((), (), s32[]{:S(2)}) async-start(), calls=%async_computation.32 | async-start | bytes 5242880 | tf_op jit(solution)/shard_map/all_gather | solution.py:408
  2940.0 205.0 %reduce-scatter.38.cloned.1.call-start = ((), (), s32[]{:S(2)}) async-start(), calls=%async_computation.36 | async-start | bytes 6291456 | tf_op jit(solution)/shard_map/reduce_scatter | solution.py:96
  2949.5 242.3 %reduce-scatter.44.cloned.1.call-start = ((), (), s32[]{:S(2)}) async-start(), calls=%async_computation.39 | async-start | bytes 17301504 | tf_op jit(solution)/shard_map/reduce_scatter | solution.py:96
  2965.6 362.3 %reduce-scatter.40.cloned.1.call-start = ((), (), s32[]{:S(2)}) async-start(), calls=%async_computation.37 | async-start | bytes 17301504 | tf_op jit(solution)/shard_map/reduce_scatter | solution.py:90
  2984.4 479.1 %reduce-scatter.42.cloned.1.call-start = ((), (), s32[]{:S(2)}) async-start(), calls=%async_computation.38 | async-start | bytes 17301504 | tf_op jit(solution)/shard_map/reduce_scatter | solution.py:93
  3003.3 493.1 %reduce-scatter.36.cloned.1.call-start = ((), (), s32[]{:S(2)}) async-start(), calls=%async_computation.35 | async-start | bytes 1572864 | tf_op jit(solution)/shard_map/reduce_scatter | solution.py:93
  3059.1 507.0 %reduce-scatter.32.cloned.1.call-start = ((), (), s32[]{:S(2)}) async-start(), calls=%async_computation.33 | async-start | bytes 5242880 | tf_op jit(solution)/shard_map/reduce_scatter | solution.py:77
  3132.2 491.4 %reduce-scatter.34.cloned.1.call-start = ((), (), s32[]{:S(2)}) async-start(), calls=%async_computation.34 | async-start | bytes 6291456 | tf_op jit(solution)/shard_map/reduce_scatter | solution.py:90
  3335.7 135.6 %copy-start.83 = (f32[512,2]{0,1:T(2,128)S(1)}, f32[512,2]{0,1:T(2,128)}, u32[]{:S(2)}) copy-start(f32[512,2]{0,1:T(2,128)} %get-tuple-element.165) | copy-start | bytes 12292
  3335.7 147.3 %copy-start.63 = (f32[512,2]{0,1:T(2,128)S(1)}, f32[512,2]{0,1:T(2,128)}, u32[]{:S(2)}) copy-start(f32[512,2]{0,1:T(2,128)} %copy-done.62) | copy-start | bytes 12292
  3335.7 147.3 %copy-start.64 = (f32[512,2]{0,1:T(2,128)S(1)}, f32[512,2]{0,1:T(2,128)}, u32[]{:S(2)}) copy-start(f32[512,2]{0,1:T(2,128)} %get-tuple-element.159) | copy-start | bytes 12292
  3335.7 147.3 %copy-start.66 = (s32[512,2]{0,1:T(2,128)S(1)}, s32[512,2]{0,1:T(2,128)}, u32[]{:S(2)}) copy-start(s32[512,2]{0,1:T(2,128)} %copy-done.65) | copy-start | bytes 12292
  3335.7 230.4 %copy-start.70 = (f32[512]{0:T(512)S(1)}, f32[512]{0:T(512)}, u32[]{:S(2)}) copy-start(f32[512]{0:T(512)} %copy-done.69) | copy-start | bytes 6148
  3335.7 230.4 %copy-start.72 = (f32[512]{0:T(512)S(1)}, f32[512]{0:T(512)}, u32[]{:S(2)}) copy-start(f32[512]{0:T(512)} %copy-done.71) | copy-start | bytes 6148
  3335.7 230.4 %copy-start.75 = (bf16[512,8]{0,1:T(8,128)(2,1)S(1)}, bf16[512,8]{0,1:T(8,128)(2,1)}, u32[]{:S(2)}) copy-start(bf16[512,8]{0,1:T(8,128)(2,1)} %param.31) | copy-start | bytes 24580
  3471.3 96.8 %copy-start.87 = (f32[512]{0:T(512)S(1)}, f32[512]{0:T(512)}, u32[]{:S(2)}) copy-start(f32[512]{0:T(512)} %get-tuple-element.141) | copy-start | bytes 6148
  3471.3 124.7 %copy-start.85 = (f32[512]{0:T(512)S(1)}, f32[512]{0:T(512)}, u32[]{:S(2)}) copy-start(f32[512]{0:T(512)} %get-tuple-element.207) | copy-start | bytes 6148
  (57 other events, 505.1 us)
Sparse Core Ops, SparseCore 0:
  20.9 46.2 all-gather.10
  70.2 18.1 reduce-scatter.15
  91.7 71.7 reduce-scatter.17
  220.1 70.4 reduce-scatter.19
  303.9 34.4 all-gather.12
  445.6 76.7 reduce-scatter.21
  524.0 46.4 all-gather.18
  572.6 44.6 all-gather.14
  620.5 18.0 reduce-scatter.23
  882.5 388.4 all-reduce.10
  1273.6 389.8 all-reduce.12
  1666.1 389.8 all-reduce.14
  2099.2 73.4 all-gather.22
  2174.7 76.1 all-gather.20
  2253.0 76.1 all-gather.16
  2549.1 76.7 reduce-scatter.27
  2628.6 77.2 reduce-scatter.25
  2709.1 46.4 all-gather.24
  2841.2 70.4 reduce-scatter.29
  2928.4 34.4 all-gather.26
  2964.5 34.4 all-gather.28
  3001.3 54.3 reduce-scatter.37
  3058.6 133.1 reduce-scatter.43
  3194.6 133.1 reduce-scatter.39
  3330.2 133.1 reduce-scatter.41
  3466.2 20.3 reduce-scatter.35
  3489.3 76.7 reduce-scatter.31
  3568.5 55.0 reduce-scatter.33
where the time goes:
time: 3650 us; the launch traced here: 3630 us
  waiting for transfers between devices  2040 us (56%)
  local copies, waits for them, and re-layouts  933 us (26%)
  other arithmetic  297 us (8%)
  matrix products  259 us (7%)
  blocking collectives  91.2 us (2%)
    unnamed x31, waiting for transfers between devices  1100 us
    gather x18, local copies, waits for them, and re-layouts, take_rows(): return jnp.take(source_rows, row_index, axis=0, mode='fill', fill_value=0)  481 us
    reduce_scatter x4, waiting for transfers between devices, row_total(): return lax.psum_scatter(values, 'row', scatter_dimension=0, tiled=True)  258 us
    reduce_scatter x2, waiting for transfers between devices, data_total(): lax.psum_scatter(first.astype(jnp.bfloat16), 'dp', scatter_dimension=0, t...  152 us
    select_n x12, other arithmetic, take_rows(): return jnp.take(source_rows, row_index, axis=0, mode='fill', fill_value=0)  137 us
    reduce_scatter x2, waiting for transfers between devices, data_total(): lax.psum_scatter(second.astype(jnp.bfloat16), 'dp', scatter_dimension=0,...  128 us
    all_gather x4, waiting for transfers between devices, row_gather(): return lax.all_gather(values, 'row', axis=0, tiled=True)  95.3 us
  transfers between devices with their start and end apart: 28, of which 20 were waited for; matrix products, arithmetic and copies ran while one was open for 27% of the time, Pallas kernels for 0%

commit v1 on v0

v1 whole, which is shorter than its diff:
```python
import functools
import math

import jax
import jax.numpy as jnp
from jax import lax
from jax.experimental import pallas as pl
from jax.experimental.pallas import tpu as pltpu
from jax.sharding import PartitionSpec as P

D = 2048
HD = 128
SEQ = 512
CONT = 4

EPSILON = 1e-06
NEGATIVE = -1e30
VMEM_BYTES = 56 * 1024 * 1024
TILE = 128
WINDOW = TILE + 16
BF = jnp.bfloat16
F32 = jnp.float32


def after(value, *others):
    return lax.optimization_barrier((value,) + others)[0]


def rope_tables(segment_ids):
    labels = jnp.arange(CONT + 1, dtype=jnp.int32)
    member = (segment_ids[:, :, None] == labels[None, None, :]).astype(jnp.int32)
    before = jnp.cumsum(member, axis=1) - member
    within = jnp.sum(before * member, axis=2)
    prompt = jnp.sum((segment_ids == 0).astype(jnp.int32), axis=1, keepdims=True)
    places = (within + jnp.where(segment_ids > 0, prompt, 0)).astype(F32).reshape(-1)
    frequency = jnp.exp(jnp.arange(HD // 2, dtype=F32) * (-2.0 * math.log(10000.0) / HD))
    angles = places[:, None] * frequency[None, :]
    cosine, sine = jnp.cos(angles), jnp.sin(angles)
    return (
        jnp.concatenate([cosine, cosine], axis=1),
        jnp.concatenate([-sine, sine], axis=1),
    )


def kept_pairs(routes, pair_order, experts, capacity):
    pairs = pair_order.shape[0]
    side = 64
    digits = jnp.arange(side, dtype=jnp.int32)[None, :]
    high = (pair_order[:, None] // side == jnp.arange(pairs // side, dtype=jnp.int32)[None, :])
    high = high.astype(BF)
    low = (pair_order[:, None] % side == digits).astype(BF)
    table = routes.reshape(pairs // side, side).astype(BF)
    chosen = jnp.sum(jnp.dot(high, table, preferred_element_type=F32) * low, axis=1)
    labels = jnp.arange(experts, dtype=F32)
    member = (chosen[:, None] == labels[None, :]).astype(jnp.int32)
    ranked = jnp.sum((jnp.cumsum(member, axis=0) - member) * member, axis=1)
    placed = (ranked < capacity).astype(BF)
    kept = lax.dot_general(
        high * placed[:, None], low, (((0,), (0,)), ((), ())), preferred_element_type=F32
    )
    return kept.reshape(routes.shape).astype(jnp.int32)


def token_slots(routes, kept, labels, slots):
    member = (routes[:, :, None] == labels[None, None, :]).astype(jnp.int32)
    member = jnp.sum(member * kept[:, :, None], axis=1)
    ranked = jnp.cumsum(member, axis=0)
    starts = (ranked - member)[::TILE] // 16 * 16
    return (ranked * member - 1, jnp.minimum(starts, slots - WINDOW))


def pick_kernel(extra, transposed, blocks_ref, routes_ref, x_ref, w_ref, *rest):
    outs = rest[-2:]
    rows = x_ref[...]
    experts = w_ref.shape[0]
    width = w_ref.shape[1] if transposed else w_ref.shape[2]
    contract = (((1,), (1 if transposed else 0,)), ((), ()))
    first = jnp.broadcast_to(routes_ref[:, 0:1], (rows.shape[0], width))
    second = jnp.broadcast_to(routes_ref[:, 1:2], (rows.shape[0], width))
    picked = [jnp.zeros((rows.shape[0], width), F32) for _ in range(2)]
    for expert in range(experts):
        product = lax.dot_general(rows, w_ref[expert], contract, preferred_element_type=F32)
        picked[0] = jnp.where(first == expert, product, picked[0])
        picked[1] = jnp.where(second == expert, product, picked[1])
    for place in range(extra):
        picked.append(
            lax.dot_general(rows, rest[0][place], contract, preferred_element_type=F32)
        )
    picked = [item.astype(BF) for item in picked]
    for block, o_ref in enumerate(outs):

        @pl.when(pl.program_id(0) == block)
        def _():
            for place, item in enumerate(picked):
                o_ref[:, place * width : (place + 1) * width] = item


def pick_matmul(blocks, routes, rows, weight, extra_weight, block_rows, transposed):
    experts = weight.shape[0]
    depth = rows.shape[1]
    width = weight.shape[1] if transposed else weight.shape[2]
    tile = min(256, block_rows)
    tiles = block_rows // tile
    extra = 0 if extra_weight is None else extra_weight.shape[0]
    total = (2 + extra) * width
    in_specs = [
        pl.BlockSpec((tile, 2), lambda b, i, s: (s[b] * tiles + i, 0)),
        pl.BlockSpec((tile, depth), lambda b, i, s: (s[b] * tiles + i, 0)),
        pl.BlockSpec(weight.shape, lambda b, i, s: (0, 0, 0)),
    ]
    operands = [routes, rows, weight]
    if extra:
        in_specs.append(pl.BlockSpec(extra_weight.shape, lambda b, i, s: (0, 0, 0)))
        operands.append(extra_weight)
    flops = 4 * block_rows * depth * width * (experts + extra)
    return pl.pallas_call(
        functools.partial(pick_kernel, extra, transposed),
        out_shape=[jax.ShapeDtypeStruct((block_rows, total), BF)] * 2,
        grid_spec=pltpu.PrefetchScalarGridSpec(
            num_scalar_prefetch=1,
            grid=(2, tiles),
            in_specs=in_specs,
            out_specs=[
                pl.BlockSpec((tile, total), lambda b, i, s: (jnp.where(b == 0, i, tiles - 1), 0)),
                pl.BlockSpec((tile, total), lambda b, i, s: (jnp.where(b == 0, 0, i), 0)),
            ],
        ),
        compiler_params=pltpu.CompilerParams(vmem_limit_bytes=VMEM_BYTES),
        cost_estimate=pl.CostEstimate(
            flops=flops,
            bytes_accessed=2 * (weight.size + 2 * block_rows * (depth + total)),
            transcendentals=0,
        ),
    )(blocks, *operands)


def mixed_rows(routes_ref, rows_ref, expert):
    first = (routes_ref[:, 0:1] == expert).astype(F32).astype(BF)
    second = (routes_ref[:, 1:2] == expert).astype(F32).astype(BF)
    return rows_ref[0] * first + rows_ref[1] * second


def merge_kernel(extra, transposed, routes_ref, rows_ref, w_ref, *rest):
    o_ref = rest[-1]
    experts = w_ref.shape[0]
    contract = (((1,), (1 if transposed else 0,)), ((), ()))
    total = jnp.zeros(o_ref.shape, F32)
    for expert in range(experts):
        mixed = mixed_rows(routes_ref, rows_ref, expert)
        total += lax.dot_general(mixed, w_ref[expert], contract, preferred_element_type=F32)
    if extra:
        logits_ref, pair_ref, router_ref = rest[:3]
        for place in range(2):
            total += lax.dot_general(
                rows_ref[2 + place], pair_ref[place], contract, preferred_element_type=F32
            )
        total += lax.dot_general(
            logits_ref[...], router_ref[...], contract, preferred_element_type=F32
        )
    o_ref[...] = total.astype(o_ref.dtype)


def merge_matmul(routes, rows, weight, extras, transposed):
    parts, count, width = rows.shape
    depth = weight.shape[1] if transposed else weight.shape[2]
    tile = min(256, count)
    in_specs = [
        pl.BlockSpec((tile, 2), lambda i: (i, 0)),
        pl.BlockSpec((parts, tile, width), lambda i: (0, i, 0)),
        pl.BlockSpec(weight.shape, lambda i: (0, 0, 0)),
    ]
    if extras:
        in_specs.append(pl.BlockSpec((tile, extras[0].shape[1]), lambda i: (i, 0)))
        in_specs.append(pl.BlockSpec(extras[1].shape, lambda i: (0, 0, 0)))
        in_specs.append(pl.BlockSpec(extras[2].shape, lambda i: (0, 0)))
    flops = 2 * count * depth * width * (weight.shape[0] + len(extras))
    return pl.pallas_call(
        functools.partial(merge_kernel, len(extras), transposed),
        out_shape=jax.ShapeDtypeStruct((count, depth), BF),
        grid=(count // tile,),
        in_specs=in_specs,
        out_specs=pl.BlockSpec((tile, depth), lambda i: (i, 0)),
        compiler_params=pltpu.CompilerParams(vmem_limit_bytes=VMEM_BYTES),
        cost_estimate=pl.CostEstimate(
            flops=flops,
            bytes_accessed=2 * (weight.size + rows.size + count * depth),
            transcendentals=0,
        ),
    )(routes, rows, weight, *extras)


def right_grad_kernel(base_ref, routes_ref, left_ref, rows_ref, o_ref):
    expert = base_ref[0] + pl.program_id(0)
    mixed = mixed_rows(routes_ref, rows_ref, expert)
    product = jnp.dot(left_ref[...], mixed, preferred_element_type=F32)
    o_ref[0] = product.astype(o_ref.dtype)


def left_grad_kernel(base_ref, routes_ref, left_ref, rows_ref, o_ref):
    expert = base_ref[0] + pl.program_id(0)
    first = (routes_ref[0:1, :] == expert).astype(F32).astype(BF)
    second = (routes_ref[1:2, :] == expert).astype(F32).astype(BF)
    mixed = left_ref[0] * first + left_ref[1] * second
    product = jnp.dot(mixed, rows_ref[...], preferred_element_type=F32)
    o_ref[0] = product.astype(o_ref.dtype)


def expert_grads(kernel, base, count, routes, left, rows, shape, dtype):
    tokens = rows.shape[-2]
    whole = lambda array: pl.BlockSpec(array.shape, lambda i, s: (0,) * array.ndim)
    return pl.pallas_call(
        kernel,
        out_shape=jax.ShapeDtypeStruct((count,) + shape, dtype),
        grid_spec=pltpu.PrefetchScalarGridSpec(
            num_scalar_prefetch=1,
            grid=(count,),
            in_specs=[whole(routes), whole(left), whole(rows)],
            out_specs=pl.BlockSpec((1,) + shape, lambda i, s: (i, 0, 0)),
        ),
        compiler_params=pltpu.CompilerParams(vmem_limit_bytes=VMEM_BYTES),
        cost_estimate=pl.CostEstimate(
            flops=2 * count * shape[0] * shape[1] * tokens,
            bytes_accessed=2 * (left.size + rows.size) + 4 * count * shape[0] * shape[1],
            transcendentals=0,
        ),
    )(base, routes, left, rows)


def spread_kernel(groups, starts_ref, places_ref, rows_ref, *refs):
    outs, totals = refs[: len(groups)], refs[len(groups) :]
    blocks = [bits for group in groups for bits in group]
    tokens = rows_ref.shape[0]
    for total_ref in totals:
        total_ref[...] = jnp.zeros(total_ref.shape, F32)
    slot = lax.broadcasted_iota(jnp.int32, (WINDOW, TILE), 0)
    for index in range(tokens // TILE):
        span = slice(index * TILE, (index + 1) * TILE)
        rows = rows_ref[span, :]
        for bits, total_ref in zip(blocks, totals):
            start = pl.multiple_of(starts_ref[bits, index], 16)
            hot = (slot == places_ref[bits : bits + 1, span] - start).astype(F32).astype(BF)
            product = jnp.dot(hot, rows, preferred_element_type=F32)
            total_ref[pl.ds(start, WINDOW), :] += product
    place = 0
    for group, o_ref in zip(groups, outs):
        for lead in range(len(group)):
            value = totals[place][...].astype(BF)
            if len(group) == 1:
                o_ref[...] = value
            else:
                o_ref[lead] = value
            place += 1


def spread_rows(starts, places, rows, slots, groups):
    tokens, width = rows.shape
    shapes = [
        (slots, width) if len(group) == 1 else (len(group), slots, width) for group in groups
    ]
    count = sum(len(group) for group in groups)
    return pl.pallas_call(
        functools.partial(spread_kernel, groups),
        out_shape=[jax.ShapeDtypeStruct(shape, BF) for shape in shapes],
        grid_spec=pltpu.PrefetchScalarGridSpec(
            num_scalar_prefetch=1,
            grid=(1,),
            in_specs=[
                pl.BlockSpec(places.shape, lambda i, s: (0, 0)),
                pl.BlockSpec((tokens, width), lambda i, s: (0, 0)),
            ],
            out_specs=[
                pl.BlockSpec(shape, lambda i, s, n=len(shape): (0,) * n) for shape in shapes
            ],
            scratch_shapes=[pltpu.VMEM((slots, width), F32) for _ in range(count)],
        ),
        compiler_params=pltpu.CompilerParams(vmem_limit_bytes=VMEM_BYTES),
        cost_estimate=pl.CostEstimate(
            flops=4 * count * WINDOW * tokens * width,
            bytes_accessed=2 * (tokens + count * slots) * width,
            transcendentals=0,
        ),
    )(starts, places, rows)


def gather_kernel(tiles, starts_ref, places_ref, *refs):
    o_ref = refs[-1]
    slot = lax.broadcasted_iota(jnp.int32, (TILE, WINDOW), 1)
    for index in range(tiles):
        span = slice(index * TILE, (index + 1) * TILE)
        total = jnp.zeros((TILE, o_ref.shape[1]), F32)
        for block, block_ref in enumerate(refs[:-1]):
            start = pl.multiple_of(starts_ref[block, pl.program_id(0) * tiles + index], 16)
            hot = (slot == places_ref[span, block : block + 1] - start).astype(F32).astype(BF)
            total += jnp.dot(
                hot, block_ref[pl.ds(start, WINDOW), :], preferred_element_type=F32
            )
        o_ref[span, :] = total.astype(o_ref.dtype)


def gather_slots(starts, places, blocks):
    tokens = places.shape[0]
    slots, width = blocks[0].shape
    tiles = 4
    tile = tiles * TILE
    return pl.pallas_call(
        functools.partial(gather_kernel, tiles),
        out_shape=jax.ShapeDtypeStruct((tokens, width), BF),
        grid_spec=pltpu.PrefetchScalarGridSpec(
            num_scalar_prefetch=1,
            grid=(tokens // tile,),
            in_specs=[pl.BlockSpec((tile, places.shape[1]), lambda i, s: (i, 0))]
            + [pl.BlockSpec((slots, width), lambda i, s: (0, 0)) for _ in blocks],
            out_specs=pl.BlockSpec((tile, width), lambda i, s: (i, 0)),
        ),
        compiler_params=pltpu.CompilerParams(vmem_limit_bytes=VMEM_BYTES),
        cost_estimate=pl.CostEstimate(
            flops=4 * WINDOW * tokens * width * len(blocks),
            bytes_accessed=2 * (tokens + slots * len(blocks)) * width,
            transcendentals=0,
        ),
    )(starts, places, *blocks)


def dots_kernel(transposed, lead, terms, *refs):
    count = (len(refs) - terms) // (terms + 1)
    outs = refs[len(refs) - count :]
    contract = (((1,), (1 if transposed else 0,)), ((), ()))
    operands = [ref[0] if flag else ref[...] for ref, flag in zip(refs, lead)]
    for place, o_ref in enumerate(outs):
        total = None
        for term in range(terms):
            right = operands[terms * (1 + place) + term]
            product = lax.dot_general(
                operands[term], right, contract, preferred_element_type=F32
            )
            total = product if total is None else total + product
        o_ref[...] = total.astype(o_ref.dtype)


def dots(lefts, right_lists, transposed, dtype):
    operands, specs, lead = [], [], []
    rows = lefts[0][0].shape[1] if isinstance(lefts[0], tuple) else lefts[0].shape[0]
    tile = rows // 2 if rows % 32 == 0 else rows
    flops, size = 0, 0
    for side, items in enumerate([lefts] + list(right_lists)):
        for item in items:
            array, place = item if isinstance(item, tuple) else (item, None)
            shape = array.shape[-2:]
            block = (tile, shape[1]) if side == 0 else shape
            if place is None:
                specs.append(
                    pl.BlockSpec(block, (lambda i: (i, 0)) if side == 0 else (lambda i: (0, 0)))
                )
            elif side == 0:
                specs.append(pl.BlockSpec((1,) + block, lambda i, p=place: (p, i, 0)))
            else:
                specs.append(pl.BlockSpec((1,) + block, lambda i, p=place: (p, 0, 0)))
            operands.append(array)
            lead.append(place is not None)
            size += 2 * shape[0] * shape[1]
            if side:
                flops += 2 * rows * shape[0] * shape[1]
    width = shape[0] if transposed else shape[1]
    count = len(right_lists)
    return pl.pallas_call(
        functools.partial(dots_kernel, transposed, lead, len(lefts)),
        out_shape=[jax.ShapeDtypeStruct((rows, width), dtype)] * count,
        grid=(rows // tile,),
        in_specs=specs,
        out_specs=[pl.BlockSpec((tile, width), lambda i: (i, 0))] * count,
        compiler_params=pltpu.CompilerParams(vmem_limit_bytes=VMEM_BYTES),
        cost_estimate=pl.CostEstimate(
            flops=2 * flops, bytes_accessed=size + 2 * count * rows * width, transcendentals=0
        ),
    )(*operands)


def turned_kernel(count, lead, *refs):
    contract = (((0,), (0,)), ((), ()))
    outs = refs[len(refs) - count :]
    refs = refs[: len(refs) - count]
    lefts = [ref[0] if flag else ref[...] for ref, flag in zip(refs[:2], lead[:2])]
    for place, o_ref in enumerate(outs):
        rights = refs[2 + 2 * place : 4 + 2 * place]
        flags = lead[2 + 2 * place : 4 + 2 * place]
        total = None
        for left, ref, flag in zip(lefts, rights, flags):
            right = ref[0] if flag else ref[...]
            product = lax.dot_general(left, right, contract, preferred_element_type=F32)
            total = product if total is None else total + product
        o_ref[...] = total.astype(o_ref.dtype)


def turned_dots(lefts, rights, dtypes):
    operands, specs, lead = [], [], []
    flops = 0
    shapes = []
    for item in list(lefts) + [each for pair in rights for each in pair]:
        array, place = item if isinstance(item, tuple) else (item, None)
        shape = array.shape[-2:]
        if place is None:
            specs.append(pl.BlockSpec(shape, lambda i: (0, 0)))
        else:
            specs.append(pl.BlockSpec((1,) + shape, lambda i, p=place: (p, 0, 0)))
        operands.append(array)
        lead.append(place is not None)
        shapes.append(shape)
    depth = shapes[0][1]
    outs = []
    for place, dtype in enumerate(dtypes):
        width = shapes[2 + 2 * place][1]
        flops += 4 * shapes[0][0] * depth * width
        outs.append(jax.ShapeDtypeStruct((depth, width), dtype))
    return pl.pallas_call(
        functools.partial(turned_kernel, len(outs), lead),
        out_shape=outs,
        grid=(1,),
        in_specs=specs,
        out_specs=[pl.BlockSpec(out.shape, lambda i: (0, 0)) for out in outs],
        compiler_params=pltpu.CompilerParams(vmem_limit_bytes=VMEM_BYTES),
        cost_estimate=pl.CostEstimate(
            flops=flops, bytes_accessed=flops // 300, transcendentals=0
        ),
    )(*operands)


def expert_kernel(count, owner_ref, other_ref, own_ref, sent_ref, *refs):
    rows_refs, gate_refs = refs[:count], refs[count : 2 * count]
    up_refs, router_refs = refs[2 * count : 3 * count], refs[3 * count : 4 * count]
    act_ref, gate_out, up_out, logit_out = refs[4 * count :]
    gate_pre = up_pre = logits = None
    for index in range(count):
        rows = rows_refs[index][...]
        gate_part = jnp.dot(rows, gate_refs[index][...], preferred_element_type=F32)
        up_part = jnp.dot(rows, up_refs[index][...], preferred_element_type=F32)
        logit_part = jnp.dot(rows, router_refs[index][...], preferred_element_type=F32)
        gate_pre = gate_part if index == 0 else gate_pre + gate_part
        up_pre = up_part if index == 0 else up_pre + up_part
        logits = logit_part if index == 0 else logits + logit_part
    lane = lax.broadcasted_iota(jnp.int32, logits.shape, 1)
    signs = (lane == owner_ref[0]).astype(F32) - (lane == other_ref[...]).astype(F32)
    gate = jax.nn.sigmoid(jnp.sum(logits * signs, axis=1, keepdims=True))
    grad_act = own_ref[...] + sent_ref[...].astype(F32)
    sigmoid_gate = jax.nn.sigmoid(gate_pre)
    swish_gate = gate_pre * sigmoid_gate
    activation = swish_gate * up_pre
    act_ref[...] = (activation * gate).astype(BF)
    share = jnp.sum(grad_act * activation, axis=1, keepdims=True) * gate * (1.0 - gate)
    logit_out[...] = (share * signs).astype(BF)
    grad_activation = grad_act * gate
    swish_slope = sigmoid_gate * (1.0 + gate_pre * (1.0 - sigmoid_gate))
    gate_out[...] = (grad_activation * up_pre * swish_slope).astype(BF)
    up_out[...] = (grad_activation * swish_gate).astype(BF)


def expert_forward(owner, other, own, sent, rows, gates, ups, routers):
    slots, depth = rows[0].shape
    hidden = gates[0].shape[1]
    lanes = routers[0].shape[1]
    tile = slots // 2 if slots % 32 == 0 else slots
    row_spec = lambda width: pl.BlockSpec((tile, width), lambda i, s: (i, 0))
    whole = lambda array: pl.BlockSpec(array.shape, lambda i, s: (0, 0))
    out_shapes = [jax.ShapeDtypeStruct((slots, hidden), BF)] * 3
    out_shapes.append(jax.ShapeDtypeStruct((slots, lanes), BF))
    return pl.pallas_call(
        functools.partial(expert_kernel, len(rows)),
        out_shape=out_shapes,
        grid_spec=pltpu.PrefetchScalarGridSpec(
            num_scalar_prefetch=1,
            grid=(slots // tile,),
            in_specs=[row_spec(1), row_spec(hidden), row_spec(hidden)]
            + [row_spec(depth) for _ in rows]
            + [whole(item) for item in list(gates) + list(ups) + list(routers)],
            out_specs=[row_spec(item.shape[1]) for item in out_shapes],
        ),
        compiler_params=pltpu.CompilerParams(vmem_limit_bytes=VMEM_BYTES),
        cost_estimate=pl.CostEstimate(
            flops=4 * len(rows) * slots * depth * hidden,
            bytes_accessed=4 * len(rows) * depth * hidden + 12 * slots * hidden,
            transcendentals=slots * hidden,
        ),
    )(owner.reshape(1), other, own, sent, *rows, *gates, *ups, *routers)


def assemble_kernel(blocks_ref, *refs):
    for block, ref in enumerate(refs[:-1]):

        @pl.when(pl.program_id(0) == block)
        def _():
            refs[-1][0] = ref[...].astype(F32)


def assemble(order, blocks):
    count = len(blocks)
    rows, width = blocks[0].shape
    tiles = 2 if rows % 32 == 0 else 1

    def spec(place):
        return pl.BlockSpec(
            (rows // tiles, width),
            lambda b, i, s: (jnp.where(b == place, i, jnp.where(b < place, 0, tiles - 1)), 0),
        )

    return pl.pallas_call(
        assemble_kernel,
        out_shape=jax.ShapeDtypeStruct((count, rows, width), F32),
        grid_spec=pltpu.PrefetchScalarGridSpec(
            num_scalar_prefetch=1,
            grid=(count, tiles),
            in_specs=[spec(place) for place in range(count)],
            out_specs=pl.BlockSpec(
                (1, rows // tiles, width), lambda b, i, s: (s[b], i, 0)
            ),
        ),
        compiler_params=pltpu.CompilerParams(vmem_limit_bytes=VMEM_BYTES),
        cost_estimate=pl.CostEstimate(
            flops=0, bytes_accessed=7 * count * rows * width, transcendentals=0
        ),
    )(order, *blocks)


def allowed_keys(row_segments, column_segments):
    length = row_segments.shape[0]
    query = lax.broadcasted_iota(jnp.int32, (length, length), 0)
    key = lax.broadcasted_iota(jnp.int32, (length, length), 1)
    same = (column_segments == 0) | (column_segments == row_segments)
    return same & (key <= query)


def weights_of(query, key, allowed):
    scores = lax.dot_general(query, key, (((1,), (1,)), ((), ())), preferred_element_type=F32)
    scores = jnp.where(allowed, scores * HD ** (-0.5), NEGATIVE)
    weights = jnp.exp(scores - jnp.max(scores, axis=1, keepdims=True))
    return weights / jnp.sum(weights, axis=1, keepdims=True)


def attend_kernel(gates_ref, rows_ref, columns_ref, cos_ref, sin_ref, *refs):
    parts, (saved_ref, mixed_ref, gated_ref) = refs[:12], refs[12:]
    summed = [
        parts[place][...].astype(F32)
        + parts[4 + place][...].astype(F32)
        + parts[8 + place][...].astype(F32)
        for place in range(4)
    ]
    cosine, sine = cos_ref[...], sin_ref[...]
    turned = [
        (item * cosine + pltpu.roll(item, HD // 2, 1) * sine).astype(BF) for item in summed[:3]
    ]
    turned.append(summed[3].astype(BF))
    for place in range(4):
        saved_ref[place] = turned[place]
    allowed = allowed_keys(rows_ref[...], columns_ref[...])
    for place in range(2):
        probs = weights_of(turned[place], turned[2], allowed).astype(BF)
        mixed = jnp.dot(probs, turned[3], preferred_element_type=F32)
        mixed_ref[place] = mixed
        gated_ref[place] = (mixed * gates_ref[:, place : place + 1]).astype(BF)


def attend(gates, segments, cosine, sine, parts):
    length = gates.shape[0]
    heads = parts[0].shape[1] // (4 * HD)
    whole = lambda array: pl.BlockSpec(array.shape, lambda h: (0, 0))
    part_specs = [
        pl.BlockSpec((length, HD), lambda h, p=place: (0, p * heads + h))
        for _ in parts
        for place in range(4)
    ]
    small = [gates, segments.reshape(length, 1), segments.reshape(1, length), cosine, sine]
    return pl.pallas_call(
        attend_kernel,
        out_shape=[
            jax.ShapeDtypeStruct((4, length, heads * HD), BF),
            jax.ShapeDtypeStruct((2, length, heads * HD), F32),
            jax.ShapeDtypeStruct((2, length, heads * HD), BF),
        ],
        grid=(heads,),
        in_specs=[whole(item) for item in small] + part_specs,
        out_specs=[
            pl.BlockSpec((count, length, HD), lambda h: (0, 0, h)) for count in (4, 2, 2)
        ],
        compiler_params=pltpu.CompilerParams(vmem_limit_bytes=VMEM_BYTES),
        cost_estimate=pl.CostEstimate(
            flops=16 * heads * length * length * HD,
            bytes_accessed=12 * length * heads * HD * 4,
            transcendentals=2 * heads * length * length,
        ),
    )(*small, *[part for part in parts for _ in range(4)])


def attend_back_kernel(
    gates_ref, rows_ref, columns_ref, cos_ref, sin_ref, saved_ref, mixed_ref, *refs
):
    parts, (out_ref, share_ref) = refs[:6], refs[6:]
    allowed = allowed_keys(rows_ref[...], columns_ref[...])
    key, value = saved_ref[2], saved_ref[3]
    cosine, sine = cos_ref[...], sin_ref[...]
    scale = HD ** (-0.5)
    over_rows = (((0,), (0,)), ((), ()))
    over_last = (((1,), (1,)), ((), ()))

    def unturn(item):
        return (item * cosine - pltpu.roll(item, HD // 2, 1) * sine).astype(BF)

    @pl.when(pl.program_id(0) == 0)
    def _():
        share_ref[...] = jnp.zeros(share_ref.shape, F32)

    grad_key = grad_value = 0.0
    for place in range(2):
        grad = (
            parts[place][...].astype(F32)
            + parts[2 + place][...].astype(F32)
            + parts[4 + place][...].astype(F32)
        )
        share_ref[place] += jnp.sum(grad * mixed_ref[place], axis=1, keepdims=True)
        grad = (grad * gates_ref[:, place : place + 1]).astype(BF)
        query = saved_ref[place]
        probs = weights_of(query, key, allowed)
        grad_value += lax.dot_general(
            probs.astype(BF), grad, over_rows, preferred_element_type=F32
        )
        grad_probs = lax.dot_general(grad, value, over_last, preferred_element_type=F32)
        centred = jnp.sum(probs * grad_probs, axis=1, keepdims=True)
        grad_scores = (probs * (grad_probs - centred)).astype(BF)
        grad_query = jnp.dot(grad_scores, key, preferred_element_type=F32) * scale
        out_ref[place] = unturn(grad_query)
        grad_key += lax.dot_general(
            grad_scores, query, over_rows, preferred_element_type=F32
        )
    out_ref[2] = unturn(grad_key * scale)
    out_ref[3] = grad_value.astype(BF)


def attend_back(gates, segments, cosine, sine, saved, mixed, parts):
    length = gates.shape[0]
    heads = saved.shape[2] // HD
    whole = lambda array: pl.BlockSpec(array.shape, lambda h: (0, 0))
    part_specs = [
        pl.BlockSpec((length, HD), lambda h, p=place: (0, p * heads + h))
        for _ in parts
        for place in range(2)
    ]
    small = [gates, segments.reshape(length, 1), segments.reshape(1, length), cosine, sine]
    return pl.pallas_call(
        attend_back_kernel,
        out_shape=[
            jax.ShapeDtypeStruct((4, length, heads * HD), BF),
            jax.ShapeDtypeStruct((2, length, 1), F32),
        ],
        grid=(heads,),
        in_specs=[whole(item) for item in small]
        + [pl.BlockSpec((count, length, HD), lambda h: (0, 0, h)) for count in (4, 2)]
        + part_specs,
        out_specs=[
            pl.BlockSpec((4, length, HD), lambda h: (0, 0, h)),
            pl.BlockSpec((2, length, 1), lambda h: (0, 0, 0)),
        ],
        compiler_params=pltpu.CompilerParams(vmem_limit_bytes=VMEM_BYTES),
        cost_estimate=pl.CostEstimate(
            flops=40 * heads * length * length * HD,
            bytes_accessed=20 * length * heads * HD * 4,
            transcendentals=2 * heads * length * length,
        ),
    )(*small, saved, mixed, *[part for part in parts for _ in range(2)])


def swap(value, axes, bits, size):
    if bits == 0:
        return value
    return lax.ppermute(value, axes, [(i, i ^ bits) for i in range(size)])


def row_gather(values):
    return lax.all_gather(values, "row", axis=0, tiled=True)


def row_total(values):
    return lax.psum_scatter(values, "row", scatter_dimension=0, tiled=True).astype(F32)


def col_total(values):
    return lax.psum(values, "col")


def small_total(value, axes):
    for axis in axes:
        size = lax.axis_size(axis)
        bits = 1
        while bits < size:
            value = value + swap(value, axis, bits, size)
            bits *= 2
    return value


def norm_factor(rows_in):
    squares = col_total(jnp.sum(rows_in * rows_in, axis=1))
    return lax.rsqrt(squares / D + EPSILON)


def norm_backward(rows_in, factor, gain_row, grad_in):
    scaled = grad_in * gain_row
    inner_sum = col_total(jnp.sum(scaled * rows_in, axis=1))[:, None]
    gain_grad = jnp.sum(grad_in * rows_in * factor, axis=0)
    return (factor * scaled - rows_in * factor**3 * inner_sum / D, gain_grad)


def local(
    hidden_in,
    gain_attn,
    router_attn,
    query_weight,
    kv_weight,
    out_weight,
    gain_ffn,
    router_ffn,
    gate_weight,
    up_weight,
    down_weight,
    attn_routes,
    ffn_routes,
    attn_order,
    ffn_order,
    segment_ids,
    d_out,
):
    dp_count, col_count = lax.axis_size("dp"), lax.axis_size("col")
    dp_index, col_index = lax.axis_index("dp"), lax.axis_index("col")
    owners = dp_count * col_count
    owner = dp_index * col_count + col_index
    batch_rows = attn_routes.shape[0]
    group_rows = batch_rows // col_count
    features = hidden_in.shape[1]
    attn_experts = query_weight.shape[0]
    ffn_experts = gate_weight.shape[0]
    half_experts = attn_experts // dp_count
    attn_capacity = 5 * batch_rows // (2 * attn_experts)
    slots = 5 * batch_rows // (2 * ffn_experts)
    head_width = query_weight.shape[2]
    pair_axes = ("dp", "col")

    def at_owner(array, bits):
        return lax.dynamic_index_in_dim(array, owner ^ bits, 0, keepdims=False)

    def expert_weight(weight, *waits):
        blocks = {bits: at_owner(weight, bits) for bits in (2, 3, 1, 0)}
        for bits in blocks:
            block = after(blocks[bits], *waits) if waits else blocks[bits]
            blocks[bits] = swap(block, "col", bits, col_count)
        return [blocks[bits] for bits in range(col_count)]

    def col_gather(block, axis):
        blocks = {0: block, 2: swap(block, "col", 2, col_count)}
        blocks[1] = swap(block, "col", 1, col_count)
        blocks[3] = swap(blocks[2], "col", 1, col_count)
        shape = list(block.shape)
        shape[axis] *= col_count
        result = jnp.zeros(shape, block.dtype)
        for bits in (0, 1, 2, 3):
            start = (col_index ^ bits) * block.shape[axis]
            result = lax.dynamic_update_slice_in_dim(result, blocks[bits], start, axis)
        return result

    hidden_all = row_gather(hidden_in)
    gate_blocks = expert_weight(gate_weight)
    rows_in = hidden_in.astype(F32)
    factor_a = norm_factor(rows_in)
    factor_a_all = row_gather(factor_a)
    attn_order, ffn_order = lax.optimization_barrier((attn_order, ffn_order, factor_a_all))[:2]

    lane_router_f = jnp.pad(router_ffn, ((0, 0), (0, 128 - ffn_experts)))
    router_blocks = [swap(lane_router_f, "col", bits, col_count) for bits in range(col_count)]

    offsets = owner ^ jnp.arange(owners, dtype=jnp.int32)
    ffn_kept = kept_pairs(ffn_routes, ffn_order[0], ffn_experts, slots)
    owner_places, owner_starts = token_slots(ffn_routes, ffn_kept, offsets, slots)
    owner_starts, owner_rows = owner_starts.T, owner_places.T
    hidden_all, owner_rows, owner_starts, owner_places = lax.optimization_barrier(
        (hidden_all, owner_rows, owner_starts, owner_places, gate_blocks[2])
    )[:4]
    grad_out_all = row_gather(after(d_out, hidden_all))

    gain_a = gain_attn.astype(F32)
    normed_all = (hidden_all.astype(F32) * factor_a_all[:, None] * gain_a).astype(BF)
    near_blocks = jnp.stack([col_index, col_index ^ 1]).astype(jnp.int32)
    far_blocks = jnp.stack([col_index ^ 2, col_index ^ 3]).astype(jnp.int32)

    def col_scatter(rows, weight, extra_weight, transposed, waits):
        def part(blocks, rows):
            kept, sent = pick_matmul(
                blocks, attn_routes, rows, weight, extra_weight, group_rows, transposed
            )
            return kept, swap(sent, "col", 1, col_count)

        kept, received = part(far_blocks, rows)
        far = (kept.astype(F32) + received.astype(F32)).astype(BF)
        far = swap(after(far, *waits), "col", 2, col_count)
        kept, received = part(near_blocks, after(rows, received))
        return [kept, received, far]

    def group_block(array, bits, axis):
        start = (col_index ^ bits) * group_rows
        return lax.dynamic_slice_in_dim(array, start, group_rows, axis)

    logits_all = lax.dot_general(
        router_attn, normed_all, (((0,), (1,)), ((), ())), preferred_element_type=F32
    )
    logits_a = sum(
        swap(group_block(logits_all, bits, 1), "col", bits, col_count)
        for bits in range(col_count)
    )
    projected = col_scatter(
        normed_all, query_weight, kv_weight, False, [logits_a] + gate_blocks[1:]
    )
    attn_order = after(attn_order, projected[1])
    attn_kept = kept_pairs(attn_routes, attn_order[0], attn_experts, attn_capacity)
    kept_a = group_block(attn_kept, 0, 0).astype(F32)
    routes_a = group_block(attn_routes, 0, 0)
    member_a = (
        routes_a[:, :, None] == jnp.arange(attn_experts, dtype=jnp.int32)[None, None, :]
    ).astype(F32)
    gate_a = jax.nn.softmax(jnp.sum(member_a * logits_a.T[:, None, :], axis=2), axis=1)
    scaled_a = gate_a * kept_a
    cosine, sine_rows = rope_tables(segment_ids)
    segments = segment_ids.reshape(-1)

    half_bits = (0, 1, col_count, col_count + 1)
    grad_groups = spread_rows(
        owner_starts,
        owner_rows,
        after(grad_out_all, projected[1]),
        slots,
        [(bits, bits ^ 2) for bits in half_bits],
    )
    route_sums = jnp.sum(ffn_routes, axis=1).astype(BF)
    route_sums = jnp.broadcast_to(route_sums[:, None], (batch_rows, 128))
    near_sums, far_sums = spread_rows(
        owner_starts, owner_rows, route_sums, slots, [(0,), (col_count,)]
    )
    far_sums = swap(far_sums[:, 0:8], pair_axes, col_count, owners)
    slot_other = [item[:, 0:1].astype(jnp.int32) - owner for item in (near_sums, far_sums)]
    grad_pairs = [
        swap(group, pair_axes, bits, owners) for bits, group in zip(half_bits, grad_groups)
    ]
    down_pairs = [
        swap(
            jnp.stack([at_owner(down_weight, bits), at_owner(down_weight, bits ^ 2)]),
            "col",
            bits,
            col_count,
        )
        for bits in (0, 1)
    ]
    scaled_a, cosine, sine_rows = lax.optimization_barrier(
        (scaled_a, cosine, sine_rows, *grad_groups, *slot_other)
    )[:3]
    saved, attended, gated_out = attend(scaled_a, segments, cosine, sine_rows, projected)
    gated_all = col_gather(gated_out, 1)
    up_blocks = expert_weight(up_weight, gated_all)
    attn_part = merge_matmul(attn_routes, gated_all, out_weight, (), False)

    def grad_act_part(batch, lead, dtype):
        return dots(
            [(grad_pairs[2 * batch + near], lead) for near in (0, 1)],
            [[(down_pairs[near], lead) for near in (0, 1)]],
            True,
            dtype,
        )[0]

    grad_pairs = [after(pair, gated_all) for pair in grad_pairs]
    grad_act_out = [grad_act_part(batch, 1, BF) for batch in (0, 1)]
    attn_sum = row_total(attn_part)
    attn_sum = after(attn_sum, up_blocks[2], *grad_act_out)
    grad_act_sent = [swap(part, "col", 2, col_count) for part in grad_act_out]
    grad_act_own = [grad_act_part(batch, 0, F32) for batch in (0, 1)]
    middle = rows_in + attn_sum

    gain_f = gain_ffn.astype(F32)
    factor_f = norm_factor(middle)[:, None]
    normed_f = (middle * factor_f * gain_f).astype(BF)
    normed_f_all = row_gather(normed_f)
    normed_f_all = after(normed_f_all, up_blocks[3], grad_act_sent[0], *grad_act_own)
    order = [(2,), (3,), (6,), (7,)], [(4,), (5,), (1,), (0,)]
    slots_f = {}
    for part in order:
        blocks = spread_rows(owner_starts, owner_rows, normed_f_all, slots, part)
        for group, block in zip(part, blocks):
            slots_f[group[0]] = swap(block, pair_axes, group[0], owners)
        normed_f_all = after(normed_f_all, *blocks)
    acts, grad_gates, grad_ups, grad_logits = [], [], [], []
    for batch in (0, 1):
        act, grad_gate, grad_up, grad_logit = expert_forward(
            owner.astype(jnp.int32),
            slot_other[batch],
            grad_act_own[batch],
            grad_act_sent[batch],
            [slots_f[batch * col_count + bits] for bits in range(col_count)],
            gate_blocks,
            up_blocks,
            router_blocks,
        )
        acts.append(act)
        grad_gates.append(grad_gate)
        grad_ups.append(grad_up)
        grad_logits.append(grad_logit)

    back_blocks = {}
    for pair in ((2, 3), (6, 7), (4, 5), (1, 0)):
        batch = pair[0] // col_count
        blocks = dots(
            [grad_gates[batch], grad_ups[batch], grad_logits[batch]],
            [
                [gate_blocks[bits % col_count], up_blocks[bits % col_count], router_blocks[bits % col_count]]
                for bits in pair
            ],
            True,
            BF,
        )
        for bits, block in zip(pair, blocks):
            back_blocks[bits] = swap(block, pair_axes, bits, owners)
    back_sent = blocks[0]

    gate_grads, up_grads, router_parts = {}, {}, {}
    for bits in (2, 3, 1, 0):
        dtype = BF if bits else F32
        gate_part, up_part, router_part = turned_dots(
            [after(slots_f[bits], back_sent), slots_f[bits + col_count]],
            [grad_gates, grad_ups, grad_logits],
            [dtype, dtype, F32],
        )
        gate_grads[bits], up_grads[bits] = gate_part, up_part
        router_parts[bits] = router_part[:, :ffn_experts].T
    back_blocks = [after(back_blocks[bits], *gate_grads.values()) for bits in range(owners)]
    grad_normed_f_part = gather_slots(owner_starts, owner_places, back_blocks)

    acts = [after(act, grad_normed_f_part) for act in acts]
    act_pairs = [(act, swap(act, "col", 2, col_count)) for act in acts]
    grad_normed_f = row_total(grad_normed_f_part)
    grad_normed_f = after(grad_normed_f, act_pairs[0][1])

    middle_norm_grad, gain_ffn_grad = norm_backward(middle, factor_f, gain_f, grad_normed_f)
    grad_middle = d_out.astype(F32) + middle_norm_grad
    grad_middle_all = row_gather(grad_middle.astype(BF))
    gate_grads = {
        bits: swap(after(gate_grads[bits], act_pairs[1][1]), "col", bits, col_count)
        for bits in (2, 3, 1, 0)
    }
    grad_middle_all = after(grad_middle_all, act_pairs[1][1])

    grad_gated = col_scatter(grad_middle_all, out_weight, None, True, [gate_grads[2]])

    down_blocks = {}
    for slot, bits in enumerate(half_bits):
        pair = jnp.stack(
            [
                jnp.dot(
                    act_pairs[slot // 2][lead],
                    down_pairs[slot % 2][lead],
                    preferred_element_type=F32,
                ).astype(BF)
                for lead in (0, 1)
            ]
        )
        pair = swap(pair, pair_axes, bits, owners)
        down_blocks[bits], down_blocks[bits ^ 2] = pair[0], pair[1]

    pieces, shares = attend_back(
        scaled_a, segments, cosine, sine_rows, saved, attended, grad_gated
    )
    pieces_all = col_gather(pieces, 1)
    shares = shares[:, :, 0] * kept_a.T * (gate_a[:, 0] * gate_a[:, 1])
    grad_logits_a = (shares[0] - shares[1])[:, None] * (member_a[:, 0] - member_a[:, 1])
    grad_logits_a = jnp.pad(grad_logits_a, ((0, 0), (0, 128 - attn_experts))).astype(BF)
    logits_back = col_gather(grad_logits_a, 0)
    lane_router = jnp.pad(router_attn, ((0, 0), (0, 128 - attn_experts)))
    normed_part = merge_matmul(
        attn_routes, pieces_all, query_weight, (logits_back, kv_weight, lane_router), True
    )
    grad_normed = row_total(normed_part)
    input_norm_grad, gain_attn_grad = norm_backward(
        rows_in, factor_a[:, None], gain_a, grad_normed
    )
    input_grad = grad_middle + input_norm_grad

    ffn_part = gather_slots(
        owner_starts, owner_places, [down_blocks[bits] for bits in range(owners)]
    )
    layer_out = (middle + row_total(ffn_part)).astype(BF)
    down_near = [
        turned_dots(
            [act_pairs[0][lead], act_pairs[1][lead]],
            [[(grad_pairs[0], lead), (grad_pairs[2], lead)]],
            [F32],
        )[0]
        for lead in (0, 1)
    ]
    down_away = [
        swap(
            turned_dots(
                [act_pairs[0][lead], act_pairs[1][lead]],
                [[(grad_pairs[1], lead), (grad_pairs[3], lead)]],
                [BF],
            )[0],
            "col",
            1,
            col_count,
        )
        for lead in (0, 1)
    ]
    expert_order = (col_index ^ jnp.arange(col_count, dtype=jnp.int32)).astype(jnp.int32)
    down_grad = assemble(expert_order, [down_near[0], down_away[0], down_near[1], down_away[1]])
    gate_grad = assemble(expert_order, [gate_grads[bits] for bits in range(col_count)])
    up_grads = {
        bits: swap(after(up_grads[bits], pieces_all), "col", bits, col_count)
        for bits in (2, 3, 1, 0)
    }
    up_grad = assemble(expert_order, [up_grads[bits] for bits in range(col_count)])
    router_ffn_grad = sum(
        swap(router_parts[bits], "col", bits, col_count) for bits in range(col_count)
    )

    own_base = (dp_index * half_experts).astype(jnp.int32).reshape(1)
    away_base = ((1 - dp_index) * half_experts).astype(jnp.int32).reshape(1)

    def dp_grads(kernel, routes, left, rows, shape):
        away = expert_grads(kernel, away_base, half_experts, routes, left, rows, shape, BF)
        away = swap(away, "dp", 1, dp_count)
        own = expert_grads(kernel, own_base, half_experts, routes, left, rows, shape, F32)
        return own + away.astype(F32)

    out_grad = dp_grads(
        left_grad_kernel,
        attn_routes.T,
        jnp.swapaxes(gated_all, 1, 2),
        grad_middle_all,
        (head_width, features),
    )
    normed_turned = normed_all.T
    query_grad = dp_grads(
        right_grad_kernel, attn_routes, normed_turned, pieces_all[:2], (features, head_width)
    )
    kv_own = lax.dynamic_index_in_dim(pieces_all, 2 + dp_index, 0, keepdims=False)
    kv_away = lax.dynamic_index_in_dim(pieces_all, 3 - dp_index, 0, keepdims=False)
    kv_away = jnp.dot(normed_turned, kv_away, preferred_element_type=F32).astype(BF)
    kv_away = swap(kv_away, "dp", 1, dp_count).astype(F32)
    kv_grad = (jnp.dot(normed_turned, kv_own, preferred_element_type=F32) + kv_away)[None]
    router_attn_grad = jnp.dot(normed_turned, logits_back, preferred_element_type=F32)
    router_attn_grad = router_attn_grad[:, :attn_experts].T
    ffn_small = jnp.concatenate([router_ffn_grad, gain_ffn_grad[None]], axis=0)
    ffn_small = small_total(ffn_small, ("row", "dp"))
    router_attn_grad = small_total(router_attn_grad, ("row", "dp"))
    gain_attn_grad = small_total(gain_attn_grad, ("row", "dp"))
    gain_ffn_grad = ffn_small[ffn_experts]
    router_attn_grad = lax.dynamic_slice_in_dim(
        router_attn_grad, dp_index * half_experts, half_experts, 0
    ).T
    ffn_half = ffn_experts // dp_count
    router_ffn_grad = lax.dynamic_slice_in_dim(ffn_small, dp_index * ffn_half, ffn_half, 0).T
    return (
        layer_out,
        input_grad,
        gain_attn_grad,
        router_attn_grad,
        query_grad,
        kv_grad,
        out_grad,
        gain_ffn_grad,
        router_ffn_grad,
        gate_grad,
        up_grad,
        down_grad,
    )


def solution(mesh):
    in_specs = (
        P(("dp", "row"), "col"),
        P("col"),
        P("col", None),
        P(None, "col", "row"),
        P(None, "col", "row"),
        P(None, "row", "col"),
        P("col"),
        P("col", None),
        P(None, "col", "row"),
        P(None, "col", "row"),
        P(None, "row", "col"),
        P("dp", None),
        P("dp", None),
        P("dp", None),
        P("dp", None),
        P(("dp", "col"), None),
        P(("dp", "row"), "col"),
    )
    out_specs = (
        P(("dp", "row"), "col"),
        P(("dp", "row"), "col"),
        P("col"),
        P("col", "dp"),
        P("dp", "col", "row"),
        P("dp", "col", "row"),
        P("dp", "row", "col"),
        P("col"),
        P("col", "dp"),
        P("dp", "col", "row"),
        P("dp", "col", "row"),
        P("dp", "row", "col"),
    )
    return jax.shard_map(local, mesh=mesh, in_specs=in_specs, out_specs=out_specs, check_vma=False)
```

time: 3650 us -> 1270 us (0.35)
  waiting for transfers between devices: 2040 us -> 554 us
  local copies, waits for them, and re-layouts: 933 us -> 90.5 us
  Pallas kernels: 0 us -> 386 us
  other arithmetic: 297 us -> 55.3 us
  matrix products: 259 us -> 35.7 us
  starting transfers between devices: 1.98 us -> 62.2 us
    unnamed x31 -> x8, waiting for transfers between devices: 1100 us -> 0.13 us
    reduce_scatter x15 -> x4, waiting for transfers between devices: 705 us -> 34.9 us  [row_total(): lax.psum_scatter(values, 'row', scatter_dimension=0, tiled=True).astype(F32)]
    gather x20 -> x0, local copies, waits for them, and re-layouts: 527 us -> none  [the longest x18 481 us: take_rows(): return jnp.take(source_rows, row_index, axis=0, mode='fill', fill_value=0)]
    ppermute x0 -> x76, waiting for transfers between devices: none -> 473 us  [swap(): return lax.ppermute(value, axes, [(i, i ^ bits) for i in range(size)])]
    pallas_call x0 -> x39, Pallas kernels: none -> 386 us  [the longest x8 64 us: turned_dots(): pl.pallas_call(functools.partial(turned_kernel, len(outs), lead), out_sha...]
    reshape x20 -> x0, local copies, waits for them, and re-layouts: 260 us -> none  [the longest x1 26.9 us: local(): up_pairs = take_rows(up_slots, ffn_pair).reshape(batch_rows, 2, hidden_cols)]
    dot_general x30 -> x16, matrix products: 259 us -> 35.7 us  [the longest x8 22.8 us: local(): jnp.dot(act_pairs[slot // 2][lead], down_pairs[slot % 2][lead], preferred...]
    select_n x18 -> x2, other arithmetic: 137 us -> 0.04 us  [kept_pairs(): low = (pair_order[:, None] % side == digits).astype(BF)]
  transfers between devices with their start and end apart: 28 -> 84, of which waited for: 20 -> 31; matrix products, arithmetic and copies ran while one was open for 27% -> 12% of each run, Pallas kernels for 0% -> 25%
where the time goes in v1:
time: 1270 us; the launch traced here: 1260 us
  waiting for transfers between devices  554 us (44%)
  Pallas kernels  386 us (30%)
  local copies, waits for them, and re-layouts  90.5 us (7%)
  blocking collectives  65 us (5%)
  starting transfers between devices  62.2 us (5%)
  other arithmetic  55.3 us (4%)
  matrix products  35.7 us (3%)
  between operations  15.6 us (1%)
    ppermute x76, waiting for transfers between devices, swap(): return lax.ppermute(value, axes, [(i, i ^ bits) for i in range(size)])  473 us
    pallas_call x8, Pallas kernels, turned_dots(): pl.pallas_call(functools.partial(turned_kernel, len(outs), lead), out_sha...  64 us
    ppermute x76, starting transfers between devices, swap(): return lax.ppermute(value, axes, [(i, i ^ bits) for i in range(size)])  61.2 us
    pallas_call x8, Pallas kernels, dots(): pl.pallas_call(functools.partial(dots_kernel, transposed, lead, len(lefts...  59.2 us
    psum x4, blocking collectives, col_total(): return lax.psum(values, 'col')  53 us
    all_gather x4, waiting for transfers between devices, row_gather(): return lax.all_gather(values, 'row', axis=0, tiled=True)  45.8 us
    pallas_call x4, Pallas kernels, pick_matmul(): pl.pallas_call(functools.partial(pick_kernel, extra, transposed), out_sha...  44.7 us
    pallas_call x2, Pallas kernels, expert_forward(): pl.pallas_call(functools.partial(expert_kernel, len(rows)), out_shape=out...  38.1 us
  transfers between devices with their start and end apart: 84, of which 31 were waited for; matrix products, arithmetic and copies ran while one was open for 12% of the time, Pallas kernels for 25%

profile of v1, /device:TPU:0, one launch (start us, length us, event | category | flops | bytes accessed | tf_op | source)
XLA Modules:
  0.0 1264.1 jit_solution(17933996807384710266)
XLA Ops:
  17.9 34.6 %psum.28 = f32[512]{0:T(512)S(1)} all-reduce(f32[512]{0:T(512)S(1)} %fusion.52), channel_id=1, replica_groups=mesh['dp'=2,'row'=4,'col'=4] {'col'}, use_global_device_ids=true, to_apply=%region_1.2 | all-reduce | flops 512 | bytes 4096 | tf_op jit(solution)/shard_map/psum | solution.py:683
  53.1 12.0 all-gather
  88.0 12.2 shard_map.259
  109.3 12.3 shard_map.260
  160.1 10.5 shard_map.261
  170.6 24.8 %collective-permute-done.9.refs_8_.refs_9_.refs_10_.refs_11_ = bf16[512,2048]{1,0:T(8,128)(2,1)S(1)} collective-permute-done((bf16[512,2048]{1,0:T(8,128)(2,1)}, bf16[512,2048]{1,0:T(8,128)(2,1)S(1)}, u32[]{:S(2)}, u32[]{:S(2)}) %collective-permute-start.9) | collective-permute-done | bytes 2097184 | tf_op jit(solution)/shard_map/ppermute | solution.py:671
  196.7 15.9 %shard_map.263 = (bf16[4,512,512]{2,1,0:T(8,128)(2,1)}, f32[2,512,512]{2,1,0:T(8,128)}, bf16[2,512,512]{2,1,0:T(8,128)(2,1)}) custom-call(f32[512,2]{1,0:T(8,128)} %get-tuple-element.135.gates_ref, s32[512,1]{1,0:T(8,128)} %copy.221.rows_ref, s32[1,512]{1,0:T(1,128)} %columns_ref.3, f32[512,128]{1,0:T(8,128)} %get-tuple-element.136.cos_ref, ...), custom_call_target="tpu_custom_call" | custom-call | flops 2147483648 | bytes 12582912 | tf_op jit(solution)/shard_map/pallas_call | solution.py:570
  214.7 24.2 %collective-permute-done.11 = bf16[2,512,512]{1,2,0:T(8,128)(2,1)S(1)} collective-permute-done((bf16[2,512,512]{1,2,0:T(8,128)(2,1)S(1)}, bf16[2,512,512]{1,2,0:T(8,128)(2,1)S(1)}, u32[]{:S(2)}, u32[]{:S(2)}) %collective-permute-start.11) | collective-permute-done | bytes 1048608 | tf_op jit(solution)/shard_map/ppermute | solution.py:671
  245.6 6.2 copy.226.rows_ref
  251.8 15.6 %shard_map.264 = bf16[2048,512]{1,0:T(8,128)(2,1)} custom-call(s32[2048,2]{1,0:T(8,128)} %copy.225.routes_ref, bf16[2,2048,512]{2,1,0:T(8,128)(2,1)} %copy.226.rows_ref, bf16[8,512,512]{2,1,0:T(8,128)(2,1)} %w_ref.10), custom_call_target="tpu_custom_call" | custom-call | flops 8589934592 | bytes 10485760 | tf_op jit(solution)/shard_map/pallas_call | solution.py:177
  282.7 22.3 %collective-permute-done.16.refs_0_.refs_3_ = bf16[2,640,512]{2,1,0:T(8,128)(2,1)S(1)} collective-permute-done((bf16[2,640,512]{2,1,0:T(8,128)(2,1)S(1)}, bf16[2,640,512]{2,1,0:T(8,128)(2,1)S(1)}, u32[]{:S(2)}, u32[]{:S(2)}) %collective-permute-start.16) | collective-permute-done | bytes 1310752 | tf_op jit(solution)/shard_map/ppermute | solution.py:671
  305.0 27.2 %collective-permute-done.17.refs_1_.refs_3_ = bf16[2,640,512]{2,1,0:T(8,128)(2,1)S(1)} collective-permute-done((bf16[2,640,512]{2,1,0:T(8,128)(2,1)S(1)}, bf16[2,640,512]{2,1,0:T(8,128)(2,1)S(1)}, u32[]{:S(2)}, u32[]{:S(2)}) %collective-permute-start.17) | collective-permute-done | bytes 1310752 | tf_op jit(solution)/shard_map/ppermute | solution.py:671
  345.5 6.1 psum.29
  356.3 5.7 shard_map.268.own_ref
  362.0 5.7 shard_map.267.own_ref
  367.7 56.3 %collective-permute-done.19.refs_11_.refs_7_ = bf16[512,1408]{1,0:T(8,128)(2,1)} collective-permute-done((bf16[512,1408]{1,0:T(8,128)(2,1)}, bf16[512,1408]{1,0:T(8,128)(2,1)}, u32[]{:S(2)}, u32[]{:S(2)}) %collective-permute-start.19) | collective-permute-done | bytes 1441824 | tf_op jit(solution)/shard_map/ppermute | solution.py:671
  424.0 6.9 shard_map.269
  430.8 7.0 shard_map.270
  442.0 31.6 %collective-permute-done.25.refs_14_.refs_5_ = bf16[512,128]{1,0:T(8,128)(2,1)S(1)} collective-permute-done((bf16[512,128]{1,0:T(8,128)(2,1)S(1)}, bf16[512,128]{1,0:T(8,128)(2,1)S(1)}, u32[]{:S(2)}, u32[]{:S(2)}) %collective-permute-start.25) | collective-permute-done | bytes 131104 | tf_op jit(solution)/shard_map/ppermute | solution.py:671
  479.6 19.1 %shard_map.271 = (bf16[640,1408]{1,0:T(8,128)(2,1)}, bf16[640,1408]{1,0:T(8,128)(2,1)}, bf16[640,1408]{1,0:T(8,128)(2,1)}, bf16[640,128]{1,0:T(8,128)(2,1)}) custom-call(s32[1]{0:T(128)} %bitcast.39.owner_ref, s32[640,1]{1,0:T(8,128)} %convert_subtract_fusion.1.other_ref, f32[640,1408]{1,0:T(8,128)} %shard_map.267.own_ref, ...), custom_call_target="tpu_custom_call" | custom-call | flops 7381975040 | bytes 22347776 | tf_op jit(solution)/shard_map/pallas_call | solution.py:465
  498.8 9.1 shard_map.272
  507.9 9.2 collective-permute-done.28.sent_ref
  517.1 14.9 %collective-permute-done.27.refs_2_.refs_1_ = bf16[640,512]{1,0:T(8,128)(2,1)S(1)} collective-permute-done((bf16[640,512]{1,0:T(8,128)(2,1)}, bf16[640,512]{1,0:T(8,128)(2,1)S(1)}, u32[]{:S(2)}, u32[]{:S(2)}) %collective-permute-start.27) | collective-permute-done | bytes 655392 | tf_op jit(solution)/shard_map/ppermute | solution.py:671
  532.1 12.6 collective-permute-done.31.refs_3_.refs_1_
  544.6 18.9 %shard_map.273 = (bf16[640,1408]{1,0:T(8,128)(2,1)}, bf16[640,1408]{1,0:T(8,128)(2,1)}, bf16[640,1408]{1,0:T(8,128)(2,1)}, bf16[640,128]{1,0:T(8,128)(2,1)}) custom-call(s32[1]{0:T(128)} %bitcast.39.owner_ref, s32[640,1]{1,0:T(8,128)} %convert_subtract_fusion.other_ref, f32[640,1408]{1,0:T(8,128)} %shard_map.268.own_ref, bf16[640,1408]{1,0:T(8,128)(2,1)} %copy-done.51, ...), custom_call_target="tpu_custom_call" | custom-call | flops 7381975040 | bytes 22347776 | tf_op jit(solution)/shard_map/pallas_call | solution.py:465
  563.6 9.3 shard_map.280
  575.8 9.1 shard_map.278
  586.3 9.7 shard_map.274
  596.0 9.7 shard_map.275
  605.7 9.5 shard_map.279
  617.3 9.7 shard_map.276
  627.0 10.1 shard_map.277
  637.1 9.4 collective-permute-done.36.refs_5_
  648.8 9.4 shard_map.281
  668.9 31.6 %collective-permute-done.39.refs_0_ = bf16[640,1408]{1,0:T(8,128)(2,1)} collective-permute-done((bf16[640,1408]{1,0:T(8,128)(2,1)S(1)}, bf16[640,1408]{1,0:T(8,128)(2,1)}, u32[]{:S(2)}, u32[]{:S(2)}) %collective-permute-start.39) | collective-permute-done | bytes 1802272 | tf_op jit(solution)/shard_map/ppermute | solution.py:671
  703.8 34.5 %collective-permute-done.41.refs_1_ = bf16[640,1408]{1,0:T(8,128)(2,1)} collective-permute-done((bf16[640,1408]{1,0:T(8,128)(2,1)}, bf16[640,1408]{1,0:T(8,128)(2,1)}, u32[]{:S(2)}, u32[]{:S(2)}) %collective-permute-start.41) | collective-permute-done | bytes 1802272 | tf_op jit(solution)/shard_map/ppermute | solution.py:671
  753.5 19.1 %collective-permute-done.43 = bf16[2,640,512]{2,1,0:T(8,128)(2,1)S(1)} collective-permute-done((bf16[2,640,512]{2,1,0:T(8,128)(2,1)S(1)}, bf16[2,640,512]{2,1,0:T(8,128)(2,1)S(1)}, u32[]{:S(2)}, u32[]{:S(2)}) %collective-permute-start.43) | collective-permute-done | bytes 1310752 | tf_op jit(solution)/shard_map/ppermute | solution.py:671
  773.8 26.1 %collective-permute-done.42 = bf16[2,640,512]{2,1,0:T(8,128)(2,1)S(1)} collective-permute-done((bf16[2,640,512]{2,1,0:T(8,128)(2,1)S(1)}, bf16[2,640,512]{2,1,0:T(8,128)(2,1)S(1)}, u32[]{:S(2)}, u32[]{:S(2)}) %collective-permute-start.42) | collective-permute-done | bytes 1310752 | tf_op jit(solution)/shard_map/ppermute | solution.py:671
  801.0 9.4 shard_map.282
  812.1 6.0 psum.30
  818.1 34.9 %reduce-scatter.7.cloned.1.call-done = bf16[512,512]{1,0:T(8,128)(2,1)} async-done(((bf16[2048,512]{1,0:T(8,128)(2,1)}), bf16[512,512]{1,0:T(8,128)(2,1)}) %reduce-scatter.7.cloned.1.call-update) | async-done | bytes 524304 | tf_op jit(solution)/shard_map/reduce_scatter | solution.py:679
  857.3 43.8 %all-gather.12.cloned.1.call-done.x_ref.rows_ref = bf16[2048,512]{1,0:T(8,128)(2,1)} async-done(((bf16[512,512]{1,0:T(8,128)(2,1)}), bf16[2048,512]{1,0:T(8,128)(2,1)}) %all-gather.12.cloned.1.call-update) | async-done | bytes 2097168 | tf_op jit(solution)/shard_map/all_gather | solution.py:675
  901.2 10.1 shard_map.283
  917.3 10.1 shard_map.284
  927.5 13.6 %collective-permute-done.47.refs_4_.refs_5_ = bf16[512,1024]{1,0:T(8,128)(2,1)S(1)} collective-permute-done((bf16[512,1024]{1,0:T(8,128)(2,1)S(1)}, bf16[512,1024]{1,0:T(8,128)(2,1)S(1)}, u32[]{:S(2)}, u32[]{:S(2)}) %collective-permute-start.47) | collective-permute-done | bytes 1048608 | tf_op jit(solution)/shard_map/ppermute | solution.py:671
  942.4 14.6 %shard_map.285 = (bf16[4,512,512]{2,1,0:T(8,128)(2,1)}, f32[2,512,1]{2,1,0:T(8,128)}) custom-call(f32[512,2]{1,0:T(8,128)} %get-tuple-element.135.gates_ref, s32[512,1]{1,0:T(8,128)} %copy.221.rows_ref, s32[1,512]{1,0:T(1,128)} %columns_ref.3, f32[512,128]{1,0:T(8,128)} %get-tuple-element.136.cos_ref, f32[512,128]{1,0:T(8,128)} %get-tuple-element.137.sin_ref, ...), custom_call_target="tpu_custom_call" | custom-call | flops 5368709120 | bytes 20971520 | tf_op jit(solution)/shard_map/pallas_call | solution.py:645
  964.8 46.7 %collective-permute-done.64 = f32[8,512]{0,1:T(8,128)S(1)} collective-permute-done((f32[8,512]{0,1:T(8,128)S(1)}, f32[8,512]{0,1:T(8,128)S(1)}, u32[]{:S(2)}, u32[]{:S(2)}) %collective-permute-start.64) | collective-permute-done | bytes 16416 | tf_op jit(solution)/shard_map/ppermute | solution.py:671
  1015.5 5.9 shard_map.294
  1021.5 6.0 shard_map.296
  1054.2 18.4 %shard_map.286 = bf16[2048,512]{1,0:T(8,128)(2,1)} custom-call(s32[2048,2]{1,0:T(8,128)} %copy.225.routes_ref, bf16[4,2048,512]{2,1,0:T(8,128)(2,1)} %constant_dynamic-update-slice_fusion.4.rows_ref, bf16[8,512,512]{2,1,0:T(8,128)(2,1)} %w_ref.11, bf16[2048,128]{1,0:T(8,128)(2,1)} %copy-done.19, bf16[2,512,512]{2,1,0:T(8,128)(2,1)} %rest_1_.1, ...), custom_call_target="tpu_custom_call" | custom-call | flops 11811160064 | bytes 14680064 | tf_op jit(solution)/shard_map/pallas_call | solution.py:177
  1072.7 9.1 shard_map.290
  1085.1 6.4 shard_map.293.refs_0_
  1092.2 6.5 shard_map.295.refs_2_
  1098.6 10.1 shard_map.291
  1108.8 11.2 shard_map.297
  1119.9 10.4 collective-permute-done.68
  1140.8 9.7 shard_map.288
  1151.9 9.0 shard_map.289
  1166.2 30.5 %collective-permute-done.59 = f32[8,512]{1,0:T(8,128)S(1)} collective-permute-done((f32[8,512]{1,0:T(8,128)S(1)}, f32[8,512]{1,0:T(8,128)S(1)}, u32[]{:S(2)}, u32[]{:S(2)}) %collective-permute-start.59) | collective-permute-done | bytes 16416 | tf_op jit(solution)/shard_map/ppermute | solution.py:671
  1201.5 10.0 shard_map.287
  1215.5 10.8 collective-permute-done.73.refs_3_
  1226.3 10.1 shard_map.292
  1239.7 5.6 convert_add_fusion.1
  1246.4 6.3 psum.31
  (463 shorter events, 265.3 us)
Async XLA Ops:
  7.2 76.1 %all-gather.6.cloned.1.call-start = ((), (), s32[]{:S(2)}) async-start(), calls=%async_computation.4 | async-start | bytes 2621440 | tf_op jit(solution)/shard_map/all_gather | solution.py:675
  9.3 140.9 %all-gather.8.cloned.1.call-start = ((), (), s32[]{:S(2)}) async-start(), calls=%async_computation.5 | async-start | bytes 2621440 | tf_op jit(solution)/shard_map/all_gather | solution.py:675
  14.8 68.5 %collective-permute-start = (bf16[512,1408]{1,0:T(8,128)(2,1)}, bf16[512,1408]{1,0:T(8,128)(2,1)}, u32[]{:S(2)}, u32[]{:S(2)}) collective-permute-start(bf16[512,1408]{1,0:T(8,128)(2,1)} %get-tuple-element.266), channel_id=1, source_target_pairs={{0,2},{1,3},{2,0},{3,1},{4,6},{5,7},{6,4},{7,5},{8,10},{9,11},{10,... | collective-permute-start | bytes 4325384 | tf_op jit(solution)/shard_map/ppermute | solution.py:671
  100.2 47.0 %collective-permute-start.7 = (bf16[512,1408]{1,0:T(8,128)(2,1)}, bf16[512,1408]{1,0:T(8,128)(2,1)}, u32[]{:S(2)}, u32[]{:S(2)}) collective-permute-start(bf16[512,1408]{1,0:T(8,128)(2,1)} %get-tuple-element.265), channel_id=1, source_target_pairs={{0,1},{1,0},{2,3},{3,2},{4,5},{5,4},{6,7},{7,6},{8,9},{9,8},{10,11... | collective-permute-start | bytes 4325384 | tf_op jit(solution)/shard_map/ppermute | solution.py:671
  100.7 46.5 %collective-permute-start.8 = (bf16[512,1408]{1,0:T(8,128)(2,1)}, bf16[512,1408]{1,0:T(8,128)(2,1)}, u32[]{:S(2)}, u32[]{:S(2)}) collective-permute-start(bf16[512,1408]{1,0:T(8,128)(2,1)} %get-tuple-element.267), channel_id=1, source_target_pairs={{0,3},{1,2},{2,1},{3,0},{4,7},{5,6},{6,5},{7,4},{8,11},{9,10},{10,... | collective-permute-start | bytes 4325384 | tf_op jit(solution)/shard_map/ppermute | solution.py:671
  104.2 239.8 %reduce-scatter.5.cloned.1.call-start = ((), (), s32[]{:S(2)}) async-start(), calls=%async_computation.6 | async-start | bytes 2621440 | tf_op jit(solution)/shard_map/reduce_scatter | solution.py:679
  121.6 26.6 %collective-permute-start.5 = (bf16[512,2048]{1,0:T(8,128)(2,1)}, bf16[512,2048]{1,0:T(8,128)(2,1)}, u32[]{:S(2)}, u32[]{:S(2)}) collective-permute-start(bf16[512,2048]{1,0:T(8,128)(2,1)} %get-tuple-element.123), channel_id=1, source_target_pairs={{0,1},{1,0},{2,3},{3,2},{4,5},{5,4},{6,7},{7,6},{8,9},{9,8},{10,11... | collective-permute-start | bytes 6291464 | tf_op jit(solution)/shard_map/ppermute | solution.py:671
  147.2 48.2 %collective-permute-start.9 = (bf16[512,2048]{1,0:T(8,128)(2,1)}, bf16[512,2048]{1,0:T(8,128)(2,1)S(1)}, u32[]{:S(2)}, u32[]{:S(2)}) collective-permute-start(bf16[512,2048]{1,0:T(8,128)(2,1)} %add_convert_fusion), channel_id=1, source_target_pairs={{0,2},{1,3},{2,0},{3,1},{4,6},{5,7},{6,4},{7,5},{8,10},{9,11},{10,... | collective-permute-start | bytes 6291464 | tf_op jit(solution)/shard_map/ppermute | solution.py:671
  214.6 27.8 %collective-permute-start.10 = (bf16[2,512,512]{1,2,0:T(8,128)(2,1)S(1)}, bf16[2,512,512]{1,2,0:T(8,128)(2,1)S(1)}, u32[]{:S(2)}, u32[]{:S(2)}) collective-permute-start(bf16[2,512,512]{1,2,0:T(8,128)(2,1)S(1)} %copy.222), channel_id=1, source_target_pairs={{0,1},{1,0},{2,3},{3,2},{4,5},{5,4},{6,7},{7,6},{8,9},{9,8},{10,11... | collective-permute-start | bytes 3145736 | tf_op jit(solution)/shard_map/ppermute | solution.py:671
  267.4 156.6 %all-gather.10.cloned.1.call-start = ((), (), s32[]{:S(2)}) async-start(), calls=%async_computation.7 | async-start | bytes 2621440 | tf_op jit(solution)/shard_map/all_gather | solution.py:675
  270.8 61.3 %collective-permute-start.15 = (bf16[2,1408,512]{2,1,0:T(8,128)(2,1)S(1)}, bf16[2,1408,512]{2,1,0:T(8,128)(2,1)}, u32[]{:S(2)}, u32[]{:S(2)}) collective-permute-start(bf16[2,1408,512]{2,1,0:T(8,128)(2,1)S(1)} %pad_maximum_fusion.1), channel_id=1, source_target_pairs={{0,1},{1,0},{2,3},{3,2},{4,5},{5,4},{6,7},{7,6},{8,9},{9,8},{10,11... | collective-permute-start | bytes 8650760 | tf_op jit(solution)/shard_map/ppermute | solution.py:671
  273.4 31.6 %collective-permute-start.16 = (bf16[2,640,512]{2,1,0:T(8,128)(2,1)S(1)}, bf16[2,640,512]{2,1,0:T(8,128)(2,1)S(1)}, u32[]{:S(2)}, u32[]{:S(2)}) collective-permute-start(bf16[2,640,512]{2,1,0:T(8,128)(2,1)S(1)} %copy-done.53), channel_id=1, source_target_pairs={{0,16},{1,17},{2,18},{3,19},{16,0},{17,1},{18,2},{19,3},{4,20},{5,... | collective-permute-start | bytes 3932168 | tf_op jit(solution)/shard_map/ppermute | solution.py:671
  275.0 57.2 %collective-permute-start.17 = (bf16[2,640,512]{2,1,0:T(8,128)(2,1)S(1)}, bf16[2,640,512]{2,1,0:T(8,128)(2,1)S(1)}, u32[]{:S(2)}, u32[]{:S(2)}) collective-permute-start(bf16[2,640,512]{2,1,0:T(8,128)(2,1)S(1)} %copy-done.52), channel_id=1, source_target_pairs={{0,17},{1,16},{2,19},{3,18},{16,1},{17,0},{18,3},{19,2},{4,21},{5,... | collective-permute-start | bytes 3932168 | tf_op jit(solution)/shard_map/ppermute | solution.py:671
  280.7 64.6 %collective-permute-start.13 = (bf16[512,1408]{1,0:T(8,128)(2,1)}, bf16[512,1408]{1,0:T(8,128)(2,1)}, u32[]{:S(2)}, u32[]{:S(2)}) collective-permute-start(bf16[512,1408]{1,0:T(8,128)(2,1)} %get-tuple-element.142), channel_id=1, source_target_pairs={{0,2},{1,3},{2,0},{3,1},{4,6},{5,7},{6,4},{7,5},{8,10},{9,11},{10,... | collective-permute-start | bytes 4325384 | tf_op jit(solution)/shard_map/ppermute | solution.py:671
  352.5 458.0 %reduce-scatter.9.cloned.1.call-start = ((), (), s32[]{:S(2)}) async-start(), calls=%async_computation.9 | async-start | bytes 2621440 | tf_op jit(solution)/shard_map/reduce_scatter | solution.py:679
  352.6 71.4 %collective-permute-start.18 = (bf16[640,1408]{1,0:T(8,128)(2,1)}, bf16[640,1408]{1,0:T(8,128)(2,1)}, u32[]{:S(2)}, u32[]{:S(2)}) collective-permute-start(bf16[640,1408]{1,0:T(8,128)(2,1)} %shard_map.265), channel_id=1, source_target_pairs={{0,2},{1,3},{2,0},{3,1},{4,6},{5,7},{6,4},{7,5},{8,10},{9,11},{10,... | collective-permute-start | bytes 5406728 | tf_op jit(solution)/shard_map/ppermute | solution.py:671
  354.3 69.7 %collective-permute-start.19 = (bf16[512,1408]{1,0:T(8,128)(2,1)}, bf16[512,1408]{1,0:T(8,128)(2,1)}, u32[]{:S(2)}, u32[]{:S(2)}) collective-permute-start(bf16[512,1408]{1,0:T(8,128)(2,1)} %get-tuple-element.149), channel_id=1, source_target_pairs={{0,3},{1,2},{2,1},{3,0},{4,7},{5,6},{6,5},{7,4},{8,11},{9,10},{10,... | collective-permute-start | bytes 4325384 | tf_op jit(solution)/shard_map/ppermute | solution.py:671
  354.5 86.7 %collective-permute-start.26 = (bf16[512,128]{1,0:T(8,128)(2,1)S(1)}, bf16[512,128]{1,0:T(8,128)(2,1)S(1)}, u32[]{:S(2)}, u32[]{:S(2)}) collective-permute-start(bf16[512,128]{1,0:T(8,128)(2,1)S(1)} %pad.12.refs_12_.refs_8_.refs_5_), channel_id=1, source_target_pairs={{0,3},{1,2},{2,1},{3,0},{4,7},{5,6},{6,5},{7,4},{8,11},{9,10},{10,... | collective-permute-start | bytes 393224 | tf_op jit(solution)/shard_map/ppermute | solution.py:671
  356.3 118.9 %collective-permute-start.23 = (bf16[512,1408]{1,0:T(8,128)(2,1)S(1)}, bf16[512,1408]{1,0:T(8,128)(2,1)}, u32[]{:S(2)}, u32[]{:S(2)}) collective-permute-start(bf16[512,1408]{1,0:T(8,128)(2,1)S(1)} %copy-done.22), channel_id=1, source_target_pairs={{0,1},{1,0},{2,3},{3,2},{4,5},{5,4},{6,7},{7,6},{8,9},{9,8},{10,11... | collective-permute-start | bytes 4325384 | tf_op jit(solution)/shard_map/ppermute | solution.py:671
  437.8 40.1 %collective-permute-start.20 = (bf16[640,512]{1,0:T(8,128)(2,1)}, bf16[640,512]{1,0:T(8,128)(2,1)S(1)}, u32[]{:S(2)}, u32[]{:S(2)}) collective-permute-start(bf16[640,512]{1,0:T(8,128)(2,1)} %get-tuple-element.157), channel_id=1, source_target_pairs={{0,1},{1,0},{2,3},{3,2},{16,17},{17,16},{18,19},{19,18},{4,5},{5,4... | collective-permute-start | bytes 1966088 | tf_op jit(solution)/shard_map/ppermute | solution.py:671
  439.9 38.0 %collective-permute-start.21 = (bf16[640,512]{1,0:T(8,128)(2,1)}, bf16[640,512]{1,0:T(8,128)(2,1)}, u32[]{:S(2)}, u32[]{:S(2)}) collective-permute-start(bf16[640,512]{1,0:T(8,128)(2,1)} %get-tuple-element.151), channel_id=1, source_target_pairs={{0,2},{1,3},{2,0},{3,1},{16,18},{17,19},{18,16},{19,17},{4,6},{5,7... | collective-permute-start | bytes 1966088 | tf_op jit(solution)/shard_map/ppermute | solution.py:671
  440.1 38.8 %collective-permute-start.22 = (bf16[640,512]{1,0:T(8,128)(2,1)}, bf16[640,512]{1,0:T(8,128)(2,1)}, u32[]{:S(2)}, u32[]{:S(2)}) collective-permute-start(bf16[640,512]{1,0:T(8,128)(2,1)} %get-tuple-element.152), channel_id=1, source_target_pairs={{0,3},{1,2},{2,1},{3,0},{16,19},{17,18},{18,17},{19,16},{4,7},{5,6... | collective-permute-start | bytes 1966088 | tf_op jit(solution)/shard_map/ppermute | solution.py:671
  441.2 32.3 %collective-permute-start.25 = (bf16[512,128]{1,0:T(8,128)(2,1)S(1)}, bf16[512,128]{1,0:T(8,128)(2,1)S(1)}, u32[]{:S(2)}, u32[]{:S(2)}) collective-permute-start(bf16[512,128]{1,0:T(8,128)(2,1)S(1)} %pad.12.refs_12_.refs_8_.refs_5_), channel_id=1, source_target_pairs={{0,2},{1,3},{2,0},{3,1},{4,6},{5,7},{6,4},{7,5},{8,10},{9,11},{10,... | collective-permute-start | bytes 393224 | tf_op jit(solution)/shard_map/ppermute | solution.py:671
  474.9 42.2 %collective-permute-start.28 = (bf16[640,1408]{1,0:T(8,128)(2,1)S(1)}, bf16[640,1408]{1,0:T(8,128)(2,1)S(1)}, u32[]{:S(2)}, u32[]{:S(2)}) collective-permute-start(bf16[640,1408]{1,0:T(8,128)(2,1)S(1)} %copy-done.50), channel_id=1, source_target_pairs={{0,2},{1,3},{2,0},{3,1},{4,6},{5,7},{6,4},{7,5},{8,10},{9,11},{10,... | collective-permute-start | bytes 5406728 | tf_op jit(solution)/shard_map/ppermute | solution.py:671
  475.2 56.8 %collective-permute-start.27 = (bf16[640,512]{1,0:T(8,128)(2,1)}, bf16[640,512]{1,0:T(8,128)(2,1)S(1)}, u32[]{:S(2)}, u32[]{:S(2)}) collective-permute-start(bf16[640,512]{1,0:T(8,128)(2,1)} %get-tuple-element.153), channel_id=1, source_target_pairs={{0,18},{1,19},{2,16},{3,17},{16,2},{17,3},{18,0},{19,1},{4,22},{5,... | collective-permute-start | bytes 1966088 | tf_op jit(solution)/shard_map/ppermute | solution.py:671
  477.9 66.7 %collective-permute-start.31 = (bf16[640,512]{1,0:T(8,128)(2,1)}, bf16[640,512]{1,0:T(8,128)(2,1)}, u32[]{:S(2)}, u32[]{:S(2)}) collective-permute-start(bf16[640,512]{1,0:T(8,128)(2,1)} %get-tuple-element.154), channel_id=1, source_target_pairs={{0,19},{1,18},{2,17},{3,16},{16,3},{17,2},{18,1},{19,0},{4,23},{5,... | collective-permute-start | bytes 1966088 | tf_op jit(solution)/shard_map/ppermute | solution.py:671
  477.9 39.2 %collective-permute-start.29 = (bf16[640,512]{1,0:T(8,128)(2,1)}, bf16[640,512]{1,0:T(8,128)(2,1)S(1)}, u32[]{:S(2)}, u32[]{:S(2)}) collective-permute-start(bf16[640,512]{1,0:T(8,128)(2,1)} %get-tuple-element.167), channel_id=1, source_target_pairs={{0,16},{1,17},{2,18},{3,19},{16,0},{17,1},{18,2},{19,3},{4,20},{5,... | collective-permute-start | bytes 1966088 | tf_op jit(solution)/shard_map/ppermute | solution.py:671
  478.9 38.2 %collective-permute-start.30 = (bf16[640,512]{1,0:T(8,128)(2,1)}, bf16[640,512]{1,0:T(8,128)(2,1)S(1)}, u32[]{:S(2)}, u32[]{:S(2)}) collective-permute-start(bf16[640,512]{1,0:T(8,128)(2,1)} %get-tuple-element.168), channel_id=1, source_target_pairs={{0,17},{1,16},{2,19},{3,18},{16,1},{17,0},{18,3},{19,2},{4,21},{5,... | collective-permute-start | bytes 1966088 | tf_op jit(solution)/shard_map/ppermute | solution.py:671
  517.1 129.4 %collective-permute-start.32 = (bf16[640,512]{1,0:T(8,128)(2,1)}, bf16[640,512]{1,0:T(8,128)(2,1)S(1)}, u32[]{:S(2)}, u32[]{:S(2)}) collective-permute-start(bf16[640,512]{1,0:T(8,128)(2,1)} %get-tuple-element.165), channel_id=1, source_target_pairs={{0,1},{1,0},{2,3},{3,2},{16,17},{17,16},{18,19},{19,18},{4,5},{5,4... | collective-permute-start | bytes 1966088 | tf_op jit(solution)/shard_map/ppermute | solution.py:671
  572.9 42.3 %collective-permute-start.37 = (bf16[640,512]{1,0:T(8,128)(2,1)}, bf16[640,512]{1,0:T(8,128)(2,1)S(1)}, u32[]{:S(2)}, u32[]{:S(2)}) collective-permute-start(bf16[640,512]{1,0:T(8,128)(2,1)} %get-tuple-element.189), channel_id=1, source_target_pairs={{0,18},{1,19},{2,16},{3,17},{16,2},{17,3},{18,0},{19,1},{4,22},{5,... | collective-permute-start | bytes 1966088 | tf_op jit(solution)/shard_map/ppermute | solution.py:671
  573.2 42.6 %collective-permute-start.38 = (bf16[640,512]{1,0:T(8,128)(2,1)}, bf16[640,512]{1,0:T(8,128)(2,1)S(1)}, u32[]{:S(2)}, u32[]{:S(2)}) collective-permute-start(bf16[640,512]{1,0:T(8,128)(2,1)} %get-tuple-element.191), channel_id=1, source_target_pairs={{0,19},{1,18},{2,17},{3,16},{16,3},{17,2},{18,1},{19,0},{4,23},{5,... | collective-permute-start | bytes 1966088 | tf_op jit(solution)/shard_map/ppermute | solution.py:671
  584.8 61.7 %collective-permute-start.33 = (bf16[640,512]{1,0:T(8,128)(2,1)}, bf16[640,512]{1,0:T(8,128)(2,1)S(1)}, u32[]{:S(2)}, u32[]{:S(2)}) collective-permute-start(bf16[640,512]{1,0:T(8,128)(2,1)} %get-tuple-element.181), channel_id=1, source_target_pairs={{0,2},{1,3},{2,0},{3,1},{16,18},{17,19},{18,16},{19,17},{4,6},{5,7... | collective-permute-start | bytes 1966088 | tf_op jit(solution)/shard_map/ppermute | solution.py:671
  585.1 61.4 %collective-permute-start.34 = (bf16[640,512]{1,0:T(8,128)(2,1)}, bf16[640,512]{1,0:T(8,128)(2,1)S(1)}, u32[]{:S(2)}, u32[]{:S(2)}) collective-permute-start(bf16[640,512]{1,0:T(8,128)(2,1)} %get-tuple-element.183), channel_id=1, source_target_pairs={{0,3},{1,2},{2,1},{3,0},{16,19},{17,18},{18,17},{19,16},{4,7},{5,6... | collective-permute-start | bytes 1966088 | tf_op jit(solution)/shard_map/ppermute | solution.py:671
  615.2 31.3 %collective-permute-start.35 = (bf16[640,512]{1,0:T(8,128)(2,1)}, bf16[640,512]{1,0:T(8,128)(2,1)S(1)}, u32[]{:S(2)}, u32[]{:S(2)}) collective-permute-start(bf16[640,512]{1,0:T(8,128)(2,1)} %get-tuple-element.185), channel_id=1, source_target_pairs={{0,16},{1,17},{2,18},{3,19},{16,0},{17,1},{18,2},{19,3},{4,20},{5,... | collective-permute-start | bytes 1966088 | tf_op jit(solution)/shard_map/ppermute | solution.py:671
  615.8 30.7 %collective-permute-start.36 = (bf16[640,512]{1,0:T(8,128)(2,1)}, bf16[640,512]{1,0:T(8,128)(2,1)S(1)}, u32[]{:S(2)}, u32[]{:S(2)}) collective-permute-start(bf16[640,512]{1,0:T(8,128)(2,1)} %get-tuple-element.187), channel_id=1, source_target_pairs={{0,17},{1,16},{2,19},{3,18},{16,1},{17,0},{18,3},{19,2},{4,21},{5,... | collective-permute-start | bytes 1966088 | tf_op jit(solution)/shard_map/ppermute | solution.py:671
  658.2 42.3 %collective-permute-start.39 = (bf16[640,1408]{1,0:T(8,128)(2,1)S(1)}, bf16[640,1408]{1,0:T(8,128)(2,1)}, u32[]{:S(2)}, u32[]{:S(2)}) collective-permute-start(bf16[640,1408]{1,0:T(8,128)(2,1)S(1)} %copy-done.6), channel_id=1, source_target_pairs={{0,2},{1,3},{2,0},{3,1},{4,6},{5,7},{6,4},{7,5},{8,10},{9,11},{10,... | collective-permute-start | bytes 5406728 | tf_op jit(solution)/shard_map/ppermute | solution.py:671
  658.4 79.9 %collective-permute-start.41 = (bf16[640,1408]{1,0:T(8,128)(2,1)}, bf16[640,1408]{1,0:T(8,128)(2,1)}, u32[]{:S(2)}, u32[]{:S(2)}) collective-permute-start(bf16[640,1408]{1,0:T(8,128)(2,1)} %get-tuple-element.195.refs_1_), channel_id=1, source_target_pairs={{0,2},{1,3},{2,0},{3,1},{4,6},{5,7},{6,4},{7,5},{8,10},{9,11},{10,... | collective-permute-start | bytes 5406728 | tf_op jit(solution)/shard_map/ppermute | solution.py:671
  660.3 192.7 %reduce-scatter.7.cloned.1.call-start = ((), (), s32[]{:S(2)}) async-start(), calls=%async_computation.8 | async-start | bytes 2621440 | tf_op jit(solution)/shard_map/reduce_scatter | solution.py:679
  703.7 48.6 %collective-permute-start.40 = (bf16[2,640,512]{2,1,0:T(8,128)(2,1)S(1)}, bf16[2,640,512]{2,1,0:T(8,128)(2,1)S(1)}, u32[]{:S(2)}, u32[]{:S(2)}) collective-permute-start(bf16[2,640,512]{2,1,0:T(8,128)(2,1)S(1)} %pad_maximum_fusion.2), channel_id=1, source_target_pairs={{0,1},{1,0},{2,3},{3,2},{16,17},{17,16},{18,19},{19,18},{4,5},{5,4... | collective-permute-start | bytes 3932168 | tf_op jit(solution)/shard_map/ppermute | solution.py:671
  741.5 31.1 %collective-permute-start.43 = (bf16[2,640,512]{2,1,0:T(8,128)(2,1)S(1)}, bf16[2,640,512]{2,1,0:T(8,128)(2,1)S(1)}, u32[]{:S(2)}, u32[]{:S(2)}) collective-permute-start(bf16[2,640,512]{2,1,0:T(8,128)(2,1)S(1)} %pad_maximum_fusion.4), channel_id=1, source_target_pairs={{0,17},{1,16},{2,19},{3,18},{16,1},{17,0},{18,3},{19,2},{4,21},{5,... | collective-permute-start | bytes 3932168 | tf_op jit(solution)/shard_map/ppermute | solution.py:671
  745.6 54.3 %collective-permute-start.42 = (bf16[2,640,512]{2,1,0:T(8,128)(2,1)S(1)}, bf16[2,640,512]{2,1,0:T(8,128)(2,1)S(1)}, u32[]{:S(2)}, u32[]{:S(2)}) collective-permute-start(bf16[2,640,512]{2,1,0:T(8,128)(2,1)S(1)} %pad_maximum_fusion.3), channel_id=1, source_target_pairs={{0,16},{1,17},{2,18},{3,19},{16,0},{17,1},{18,2},{19,3},{4,20},{5,... | collective-permute-start | bytes 3932168 | tf_op jit(solution)/shard_map/ppermute | solution.py:671
  810.4 90.7 %all-gather.12.cloned.1.call-start = ((), (), s32[]{:S(2)}) async-start(), calls=%async_computation.10 | async-start | bytes 2621440 | tf_op jit(solution)/shard_map/all_gather | solution.py:675
  855.8 380.6 %reduce-scatter.11.cloned.1.call-start = ((), (), s32[]{:S(2)}) async-start(), calls=%async_computation.11 | async-start | bytes 2621440 | tf_op jit(solution)/shard_map/reduce_scatter | solution.py:679
  855.8 60.0 %collective-permute-start.46 = (bf16[512,1408]{1,0:T(8,128)(2,1)}, bf16[512,1408]{1,0:T(8,128)(2,1)S(1)}, u32[]{:S(2)}, u32[]{:S(2)}) collective-permute-start(bf16[512,1408]{1,0:T(8,128)(2,1)} %get-tuple-element.205), channel_id=1, source_target_pairs={{0,2},{1,3},{2,0},{3,1},{4,6},{5,7},{6,4},{7,5},{8,10},{9,11},{10,... | collective-permute-start | bytes 4325384 | tf_op jit(solution)/shard_map/ppermute | solution.py:671
  915.8 25.3 %collective-permute-start.47 = (bf16[512,1024]{1,0:T(8,128)(2,1)S(1)}, bf16[512,1024]{1,0:T(8,128)(2,1)S(1)}, u32[]{:S(2)}, u32[]{:S(2)}) collective-permute-start(bf16[512,1024]{1,0:T(8,128)(2,1)S(1)} %add_convert_fusion.1), channel_id=1, source_target_pairs={{0,2},{1,3},{2,0},{3,1},{4,6},{5,7},{6,4},{7,5},{8,10},{9,11},{10,... | collective-permute-start | bytes 3145736 | tf_op jit(solution)/shard_map/ppermute | solution.py:671
  957.1 57.5 %collective-permute-start.49 = (bf16[4,512,512]{2,1,0:T(8,128)(2,1)}, bf16[4,512,512]{2,1,0:T(8,128)(2,1)S(1)}, u32[]{:S(2)}, u32[]{:S(2)}) collective-permute-start(bf16[4,512,512]{2,1,0:T(8,128)(2,1)} %get-tuple-element.207), channel_id=1, source_target_pairs={{0,2},{1,3},{2,0},{3,1},{4,6},{5,7},{6,4},{7,5},{8,10},{9,11},{10,... | collective-permute-start | bytes 6291464 | tf_op jit(solution)/shard_map/ppermute | solution.py:671
  961.2 50.3 %collective-permute-start.64 = (f32[8,512]{0,1:T(8,128)S(1)}, f32[8,512]{0,1:T(8,128)S(1)}, u32[]{:S(2)}, u32[]{:S(2)}) collective-permute-start(f32[8,512]{0,1:T(8,128)S(1)} %slice_bitcast_fusion.21), channel_id=1, source_target_pairs={{0,2},{1,3},{2,0},{3,1},{4,6},{5,7},{6,4},{7,5},{8,10},{9,11},{10,... | collective-permute-start | bytes 49160 | tf_op jit(solution)/shard_map/ppermute | solution.py:671
  961.8 52.6 %collective-permute-start.65 = (f32[8,512]{0,1:T(8,128)S(1)}, f32[8,512]{0,1:T(8,128)S(1)}, u32[]{:S(2)}, u32[]{:S(2)}) collective-permute-start(f32[8,512]{0,1:T(8,128)S(1)} %slice_bitcast_fusion.20), channel_id=1, source_target_pairs={{0,3},{1,2},{2,1},{3,0},{4,7},{5,6},{6,5},{7,4},{8,11},{9,10},{10,... | collective-permute-start | bytes 49160 | tf_op jit(solution)/shard_map/ppermute | solution.py:671
  962.9 51.5 %collective-permute-start.63 = (f32[8,512]{0,1:T(8,128)S(1)}, f32[8,512]{0,1:T(8,128)S(1)}, u32[]{:S(2)}, u32[]{:S(2)}) collective-permute-start(f32[8,512]{0,1:T(8,128)S(1)} %slice_bitcast_fusion.22), channel_id=1, source_target_pairs={{0,1},{1,0},{2,3},{3,2},{4,5},{5,4},{6,7},{7,6},{8,9},{9,8},{10,11... | collective-permute-start | bytes 49160 | tf_op jit(solution)/shard_map/ppermute | solution.py:671
  964.7 80.3 %collective-permute-start.48 = (bf16[4,512,512]{2,1,0:T(8,128)(2,1)}, bf16[4,512,512]{2,1,0:T(8,128)(2,1)}, u32[]{:S(2)}, u32[]{:S(2)}) collective-permute-start(bf16[4,512,512]{2,1,0:T(8,128)(2,1)} %get-tuple-element.207), channel_id=1, source_target_pairs={{0,1},{1,0},{2,3},{3,2},{4,5},{5,4},{6,7},{7,6},{8,9},{9,8},{10,11... | collective-permute-start | bytes 6291464 | tf_op jit(solution)/shard_map/ppermute | solution.py:671
  1014.6 35.1 %collective-permute-start.50 = (bf16[4,512,512]{2,1,0:T(8,128)(2,1)S(1)}, bf16[4,512,512]{2,1,0:T(8,128)(2,1)}, u32[]{:S(2)}, u32[]{:S(2)}) collective-permute-start(bf16[4,512,512]{2,1,0:T(8,128)(2,1)S(1)} %collective-permute-done.49), channel_id=1, source_target_pairs={{0,1},{1,0},{2,3},{3,2},{4,5},{5,4},{6,7},{7,6},{8,9},{9,8},{10,11... | collective-permute-start | bytes 6291464 | tf_op jit(solution)/shard_map/ppermute | solution.py:671
  1021.4 87.4 %collective-permute-start.74 = (bf16[1408,512]{1,0:T(8,128)(2,1)}, bf16[1408,512]{1,0:T(8,128)(2,1)}, u32[]{:S(2)}, u32[]{:S(2)}) collective-permute-start(bf16[1408,512]{1,0:T(8,128)(2,1)} %shard_map.294), channel_id=1, source_target_pairs={{0,1},{1,0},{2,3},{3,2},{4,5},{5,4},{6,7},{7,6},{8,9},{9,8},{10,11... | collective-permute-start | bytes 4325384 | tf_op jit(solution)/shard_map/ppermute | solution.py:671
  1041.4 50.1 %collective-permute-start.69 = (bf16[512,1408]{1,0:T(8,128)(2,1)}, bf16[512,1408]{1,0:T(8,128)(2,1)}, u32[]{:S(2)}, u32[]{:S(2)}) collective-permute-start(bf16[512,1408]{1,0:T(8,128)(2,1)} %get-tuple-element.214), channel_id=1, source_target_pairs={{0,1},{1,0},{2,3},{3,2},{4,5},{5,4},{6,7},{7,6},{8,9},{9,8},{10,11... | collective-permute-start | bytes 4325384 | tf_op jit(solution)/shard_map/ppermute | solution.py:671
  1044.4 54.2 %collective-permute-start.70 = (bf16[512,1408]{1,0:T(8,128)(2,1)}, bf16[512,1408]{1,0:T(8,128)(2,1)}, u32[]{:S(2)}, u32[]{:S(2)}) collective-permute-start(bf16[512,1408]{1,0:T(8,128)(2,1)} %get-tuple-element.215), channel_id=1, source_target_pairs={{0,3},{1,2},{2,1},{3,0},{4,7},{5,6},{6,5},{7,4},{8,11},{9,10},{10,... | collective-permute-start | bytes 4325384 | tf_op jit(solution)/shard_map/ppermute | solution.py:671
  1045.0 63.8 %collective-permute-start.75 = (bf16[1408,512]{1,0:T(8,128)(2,1)}, bf16[1408,512]{1,0:T(8,128)(2,1)}, u32[]{:S(2)}, u32[]{:S(2)}) collective-permute-start(bf16[1408,512]{1,0:T(8,128)(2,1)} %shard_map.296), channel_id=1, source_target_pairs={{0,1},{1,0},{2,3},{3,2},{4,5},{5,4},{6,7},{7,6},{8,9},{9,8},{10,11... | collective-permute-start | bytes 4325384 | tf_op jit(solution)/shard_map/ppermute | solution.py:671
  1049.7 32.0 %collective-permute-start.67 = (f32[9,512]{1,0:T(8,128)S(1)}, f32[9,512]{1,0:T(8,128)S(1)}, u32[]{:S(2)}, u32[]{:S(2)}) collective-permute-start(f32[9,512]{1,0:T(8,128)S(1)} %fusion.113), channel_id=1, source_target_pairs={{0,8},{4,12},{8,0},{12,4},{1,9},{5,13},{9,1},{13,5},{2,10},{6,14},... | collective-permute-start | bytes 55304 | tf_op jit(solution)/shard_map/ppermute | solution.py:671
  1081.7 81.2 %collective-permute-start.62 = (bf16[4,512,512]{2,1,0:T(8,128)(2,1)}, bf16[4,512,512]{2,1,0:T(8,128)(2,1)S(1)}, u32[]{:S(2)}, u32[]{:S(2)}) collective-permute-start(bf16[4,512,512]{2,1,0:T(8,128)(2,1)} %shard_map.290), channel_id=1, source_target_pairs={{0,16},{16,0},{1,17},{17,1},{2,18},{18,2},{3,19},{19,3},{4,20},{20... | collective-permute-start | bytes 6291464 | tf_op jit(solution)/shard_map/ppermute | solution.py:671
  1091.5 38.8 %collective-permute-start.68 = (f32[9,512]{1,0:T(8,128)S(1)}, f32[9,512]{1,0:T(8,128)S(1)}, u32[]{:S(2)}, u32[]{:S(2)}) collective-permute-start(f32[9,512]{1,0:T(8,128)S(1)} %add.248), channel_id=1, source_target_pairs={{0,16},{16,0},{1,17},{17,1},{2,18},{18,2},{3,19},{19,3},{4,20},{20... | collective-permute-start | bytes 55304 | tf_op jit(solution)/shard_map/ppermute | solution.py:671
  1134.7 26.1 %collective-permute-start.58 = (f32[8,512]{1,0:T(8,128)S(1)}, f32[8,512]{1,0:T(8,128)S(1)}, u32[]{:S(2)}, u32[]{:S(2)}) collective-permute-start(f32[8,512]{1,0:T(8,128)S(1)} %add.234), channel_id=1, source_target_pairs={{0,8},{4,12},{8,0},{12,4},{1,9},{5,13},{9,1},{13,5},{2,10},{6,14},... | collective-permute-start | bytes 49160 | tf_op jit(solution)/shard_map/ppermute | solution.py:671
  1150.4 89.3 %collective-permute-start.60 = (bf16[4,512,512]{2,1,0:T(8,128)(2,1)}, bf16[4,512,512]{2,1,0:T(8,128)(2,1)}, u32[]{:S(2)}, u32[]{:S(2)}) collective-permute-start(bf16[4,512,512]{2,1,0:T(8,128)(2,1)} %shard_map.288), channel_id=1, source_target_pairs={{0,16},{16,0},{1,17},{17,1},{2,18},{18,2},{3,19},{19,3},{4,20},{20... | collective-permute-start | bytes 6291464 | tf_op jit(solution)/shard_map/ppermute | solution.py:671
  1160.9 35.8 %collective-permute-start.59 = (f32[8,512]{1,0:T(8,128)S(1)}, f32[8,512]{1,0:T(8,128)S(1)}, u32[]{:S(2)}, u32[]{:S(2)}) collective-permute-start(f32[8,512]{1,0:T(8,128)S(1)} %add.235), channel_id=1, source_target_pairs={{0,16},{16,0},{1,17},{17,1},{2,18},{18,2},{3,19},{19,3},{4,20},{20... | collective-permute-start | bytes 49160 | tf_op jit(solution)/shard_map/ppermute | solution.py:671
  1161.5 53.9 %collective-permute-start.71 = (bf16[512,1408]{1,0:T(8,128)(2,1)}, bf16[512,1408]{1,0:T(8,128)(2,1)S(1)}, u32[]{:S(2)}, u32[]{:S(2)}) collective-permute-start(bf16[512,1408]{1,0:T(8,128)(2,1)} %get-tuple-element.219), channel_id=1, source_target_pairs={{0,1},{1,0},{2,3},{3,2},{4,5},{5,4},{6,7},{7,6},{8,9},{9,8},{10,11... | collective-permute-start | bytes 4325384 | tf_op jit(solution)/shard_map/ppermute | solution.py:671
  1161.5 54.0 %collective-permute-start.72 = (bf16[512,1408]{1,0:T(8,128)(2,1)}, bf16[512,1408]{1,0:T(8,128)(2,1)S(1)}, u32[]{:S(2)}, u32[]{:S(2)}) collective-permute-start(bf16[512,1408]{1,0:T(8,128)(2,1)} %get-tuple-element.221), channel_id=1, source_target_pairs={{0,2},{1,3},{2,0},{3,1},{4,6},{5,7},{6,4},{7,5},{8,10},{9,11},{10,... | collective-permute-start | bytes 4325384 | tf_op jit(solution)/shard_map/ppermute | solution.py:671
  1163.0 63.3 %collective-permute-start.73 = (bf16[512,1408]{1,0:T(8,128)(2,1)}, bf16[512,1408]{1,0:T(8,128)(2,1)}, u32[]{:S(2)}, u32[]{:S(2)}) collective-permute-start(bf16[512,1408]{1,0:T(8,128)(2,1)} %get-tuple-element.223), channel_id=1, source_target_pairs={{0,3},{1,2},{2,1},{3,0},{4,7},{5,6},{6,5},{7,4},{8,11},{9,10},{10,... | collective-permute-start | bytes 4325384 | tf_op jit(solution)/shard_map/ppermute | solution.py:671
  (91 other events, 1335.9 us)
Sparse Core Ops, SparseCore 0:
  10.2 48.6 all-gather.5
  104.3 45.8 all-gather.7
  267.5 42.6 reduce-scatter.4
  352.6 45.5 all-gather.9
  660.4 41.4 reduce-scatter.8
  810.6 42.3 reduce-scatter.6
  855.9 45.2 all-gather.11
  1072.7 44.1 reduce-scatter.10

commit v2 on v1

v2 whole, which is shorter than its diff:
```python
import functools
import math

import jax
import jax.numpy as jnp
from jax import lax
from jax.experimental import pallas as pl
from jax.experimental.pallas import tpu as pltpu
from jax.sharding import PartitionSpec as P

D = 2048
HD = 128
SEQ = 512

EPSILON = 1e-06
NEGATIVE = -1e30
VMEM_BYTES = 56 * 1024 * 1024
TILE = 128
WINDOW = TILE + 16
COST = 1 << 20
ASSEMBLE = 2
BF = jnp.bfloat16
F32 = jnp.float32


def cost(flops, size, scale=COST):
    return pl.CostEstimate(flops=flops // scale, bytes_accessed=size // scale, transcendentals=0)


def after(value, *others):
    return lax.optimization_barrier((value,) + others)[0]


def rope_lines(row_segments, column_segments):
    length = row_segments.shape[0]
    query = lax.broadcasted_iota(jnp.int32, (length, length), 0)
    key = lax.broadcasted_iota(jnp.int32, (length, length), 1)
    before = (column_segments == row_segments) & (key < query)
    within = jnp.sum(before.astype(F32), axis=1, keepdims=True)
    prompt = jnp.sum((column_segments == 0).astype(F32), axis=1, keepdims=True)
    places = within + jnp.where(row_segments > 0, prompt, 0.0)
    lane = lax.broadcasted_iota(jnp.int32, (1, HD), 1)
    step = jnp.where(lane < HD // 2, lane, lane - HD // 2).astype(F32)
    frequency = jnp.exp(step * (-2.0 * math.log(10000.0) / HD))
    angles = places * frequency
    sine = jnp.sin(angles)
    return jnp.cos(angles), jnp.where(lane < HD // 2, -sine, sine)


def kept_table(capacity, experts, order_ref, table_ref, turned_ref):
    lines, lanes = table_ref.shape
    pairs = order_ref.shape[1]
    order = order_ref[...]
    token = order // 2
    line = (order % 2) * (lines // 2) + token // lanes
    high = (lax.broadcasted_iota(jnp.int32, (lines, pairs), 0) == line).astype(F32).astype(BF)
    low = lax.broadcasted_iota(jnp.int32, (lanes, pairs), 0) == token % lanes
    low = low.astype(F32).astype(BF)
    chosen = jnp.dot(turned_ref[...].astype(BF), high, preferred_element_type=F32)
    chosen = jnp.sum(chosen * low.astype(F32), axis=0, keepdims=True)
    label = lax.broadcasted_iota(jnp.int32, (experts, pairs), 0).astype(F32)
    member = (label == chosen).astype(F32)
    step = 256
    row = lax.broadcasted_iota(jnp.int32, (step, step), 0)
    upto = row <= lax.broadcasted_iota(jnp.int32, (step, step), 1)
    upto = upto.astype(F32).astype(BF)
    carry = jnp.zeros((experts, 1), F32)
    placed = []
    for start in range(0, pairs, step):
        part = member[:, start : start + step]
        count = jnp.dot(part.astype(BF), upto, preferred_element_type=F32) + carry
        carry = count[:, step - 1 : step]
        ranked = jnp.sum(count * part, axis=0, keepdims=True)
        placed.append((ranked <= capacity).astype(F32))
    placed = jnp.concatenate(placed, axis=1)
    return lax.dot_general(
        high * placed.astype(BF), low, (((1,), (1,)), ((), ())), preferred_element_type=F32
    )


def kept_kernel(capacity, experts, order_ref, table_ref, turned_ref, kept_ref):
    kept_ref[...] = kept_table(capacity, experts, order_ref, table_ref, turned_ref)


def slots_kernel(
    capacity, experts, labels_ref, order_ref, table_ref, turned_ref, places_ref, starts_ref
):
    kept = kept_table(capacity, experts, order_ref, table_ref, turned_ref)
    lines, lanes = table_ref.shape
    tiles = lines // 2
    row = lax.broadcasted_iota(jnp.int32, (lanes, lanes), 0)
    upto = (row <= lax.broadcasted_iota(jnp.int32, (lanes, lanes), 1)).astype(F32).astype(BF)
    first = lax.broadcasted_iota(jnp.int32, (tiles, tiles), 0)
    second = lax.broadcasted_iota(jnp.int32, (tiles, tiles), 1)
    above = (second < first).astype(F32).astype(BF)
    before = (first < second).astype(F32).astype(BF)
    ones = jnp.ones((8, lanes), BF)
    table = table_ref[...]
    for place in range(places_ref.shape[0]):
        member = (table == labels_ref[place].astype(F32)).astype(F32) * kept
        member = member[:tiles] + member[tiles:]
        inside = jnp.dot(member.astype(BF), upto, preferred_element_type=F32)
        past = jnp.dot(above, inside.astype(BF), preferred_element_type=F32)
        count = inside + past[:, lanes - 1 : lanes]
        slot = (count * member - 1.0).astype(jnp.int32)
        for tile in range(tiles):
            places_ref[place : place + 1, tile * lanes : (tile + 1) * lanes] = slot[tile : tile + 1]
        sums = lax.dot_general(
            ones, member.astype(BF), (((1,), (1,)), ((), ())), preferred_element_type=F32
        )
        start = jnp.dot(sums.astype(BF), before, preferred_element_type=F32)[0:1]
        start = start.astype(jnp.int32) // 16 * 16
        starts_ref[place : place + 1, :] = jnp.minimum(start, capacity - WINDOW)


def route_table(routes):
    return routes.astype(F32).T.reshape(-1, TILE)


def kept_pairs(routes, pair_order, experts, capacity):
    table = route_table(routes)
    return pl.pallas_call(
        functools.partial(kept_kernel, capacity, experts),
        out_shape=jax.ShapeDtypeStruct(table.shape, F32),
        compiler_params=pltpu.CompilerParams(vmem_limit_bytes=VMEM_BYTES),
        cost_estimate=cost(0, 0),
    )(pair_order, table, table.T)


def token_slots(routes, pair_order, labels, experts, capacity):
    table = route_table(routes)
    whole = lambda array: pl.BlockSpec(array.shape, lambda i, s: (0, 0))
    tiles = table.shape[0] // 2
    shapes = [(labels.shape[0], routes.shape[0]), (labels.shape[0], tiles)]
    return pl.pallas_call(
        functools.partial(slots_kernel, capacity, experts),
        out_shape=[jax.ShapeDtypeStruct(shape, jnp.int32) for shape in shapes],
        grid_spec=pltpu.PrefetchScalarGridSpec(
            num_scalar_prefetch=1,
            grid=(1,),
            in_specs=[whole(pair_order), whole(table), whole(table.T)],
            out_specs=[pl.BlockSpec(shape, lambda i, s: (0, 0)) for shape in shapes],
        ),
        compiler_params=pltpu.CompilerParams(vmem_limit_bytes=VMEM_BYTES),
        cost_estimate=cost(0, 0),
    )(labels, pair_order, table, table.T)


def copy_kernel(index_ref, block_ref, o_ref):
    o_ref[...] = block_ref[...]


def take_blocks(array, index, start, step, count):
    shape = array.shape[1:]
    return pl.pallas_call(
        copy_kernel,
        out_shape=jax.ShapeDtypeStruct((count,) + shape, array.dtype),
        grid_spec=pltpu.PrefetchScalarGridSpec(
            num_scalar_prefetch=1,
            grid=(count,),
            in_specs=[pl.BlockSpec((1,) + shape, lambda i, s: (s[start + step * i], 0, 0))],
            out_specs=pl.BlockSpec((1,) + shape, lambda i, s: (i, 0, 0)),
        ),
        compiler_params=pltpu.CompilerParams(vmem_limit_bytes=VMEM_BYTES),
        cost_estimate=cost(0, 0),
    )(index, array)


def lead_block(array, place):
    shape = (1,) + array.shape[1:]
    return pl.pallas_call(
        lead_kernel,
        out_shape=jax.ShapeDtypeStruct(shape, array.dtype),
        grid=(1,),
        in_specs=[pl.BlockSpec(shape, lambda i: (place, 0, 0))],
        out_specs=pl.BlockSpec(shape, lambda i: (0, 0, 0)),
        compiler_params=pltpu.CompilerParams(vmem_limit_bytes=VMEM_BYTES),
        cost_estimate=cost(0, 0),
    )(array)


def lead_kernel(block_ref, o_ref):
    o_ref[...] = block_ref[...]


def join_kernel(kept_ref, *refs):
    o_ref = refs[-1]
    start = 0
    for ref in refs[:-1]:
        span = slice(start, start + ref.shape[1])
        o_ref[:, span] = (kept_ref[:, span].astype(F32) + ref[...].astype(F32)).astype(BF)
        start += ref.shape[1]


def join_halves(kept, halves):
    rows, width = kept.shape
    tile = rows // 4 if rows % 64 == 0 else rows
    spec = lambda array: pl.BlockSpec((tile, array.shape[1]), lambda i: (i, 0))
    return pl.pallas_call(
        join_kernel,
        out_shape=jax.ShapeDtypeStruct(kept.shape, BF),
        grid=(rows // tile,),
        in_specs=[spec(kept)] + [spec(half) for half in halves],
        out_specs=spec(kept),
        compiler_params=pltpu.CompilerParams(vmem_limit_bytes=VMEM_BYTES),
        cost_estimate=cost(0, 0),
    )(kept, *halves)


def tip_kernel(rows_ref, o_ref):
    o_ref[...] = rows_ref[...].astype(BF)


def tip(rows):
    lead = rows.ndim - 2
    block = (None,) * lead + (16, 128)
    return pl.pallas_call(
        tip_kernel,
        out_shape=jax.ShapeDtypeStruct((16, 128), BF),
        grid=(1,),
        in_specs=[pl.BlockSpec(block, lambda i: (0,) * rows.ndim)],
        out_specs=pl.BlockSpec((16, 128), lambda i: (0, 0)),
        compiler_params=pltpu.CompilerParams(vmem_limit_bytes=VMEM_BYTES),
        cost_estimate=cost(0, 0),
    )(rows)


def add_kernel(own_ref, away_ref, o_ref):
    o_ref[...] = own_ref[...] + away_ref[...].astype(F32)


def add_wide(own, away):
    spec = pl.BlockSpec((1,) + own.shape[1:], lambda i: (i, 0, 0))
    return pl.pallas_call(
        add_kernel,
        out_shape=jax.ShapeDtypeStruct(own.shape, F32),
        grid=(own.shape[0],),
        in_specs=[spec, spec],
        out_specs=spec,
        compiler_params=pltpu.CompilerParams(vmem_limit_bytes=VMEM_BYTES),
        cost_estimate=cost(0, 0),
    )(own, away)


def pick_kernel(extra, transposed, blocks_ref, routes_ref, x_ref, w_ref, *rest):
    outs = rest[-3:]
    rows = x_ref[...]
    experts = w_ref.shape[0]
    width = w_ref.shape[1] if transposed else w_ref.shape[2]
    contract = (((1,), (1 if transposed else 0,)), ((), ()))
    first = jnp.broadcast_to(routes_ref[:, 0:1], (rows.shape[0], width))
    second = jnp.broadcast_to(routes_ref[:, 1:2], (rows.shape[0], width))
    picked = [jnp.zeros((rows.shape[0], width), F32) for _ in range(2)]
    for expert in range(experts):
        product = lax.dot_general(rows, w_ref[expert], contract, preferred_element_type=F32)
        picked[0] = jnp.where(first == expert, product, picked[0])
        picked[1] = jnp.where(second == expert, product, picked[1])
    for place in range(extra):
        picked.append(
            lax.dot_general(rows, rest[0][place], contract, preferred_element_type=F32)
        )
    picked = [item.astype(BF) for item in picked]
    half = len(picked) // 2

    @pl.when(pl.program_id(0) == 0)
    def _():
        for place, item in enumerate(picked):
            outs[0][:, place * width : (place + 1) * width] = item

    @pl.when(pl.program_id(0) == 1)
    def _():
        for place, item in enumerate(picked):
            start = place % half * width
            outs[1 + place // half][:, start : start + width] = item


def pick_matmul(blocks, routes, rows, weight, extra_weight, block_rows, transposed, scale):
    experts = weight.shape[0]
    depth = rows.shape[1]
    width = weight.shape[1] if transposed else weight.shape[2]
    tile = min(256, block_rows)
    tiles = block_rows // tile
    extra = 0 if extra_weight is None else extra_weight.shape[0]
    total = (2 + extra) * width
    in_specs = [
        pl.BlockSpec((tile, 2), lambda b, i, s: (s[b] * tiles + i, 0)),
        pl.BlockSpec((tile, depth), lambda b, i, s: (s[b] * tiles + i, 0)),
        pl.BlockSpec(weight.shape, lambda b, i, s: (0, 0, 0)),
    ]
    operands = [routes, rows, weight]
    if extra:
        in_specs.append(pl.BlockSpec(extra_weight.shape, lambda b, i, s: (0, 0, 0)))
        operands.append(extra_weight)
    flops = 4 * block_rows * depth * width * (experts + extra)
    return pl.pallas_call(
        functools.partial(pick_kernel, extra, transposed),
        out_shape=[jax.ShapeDtypeStruct((block_rows, total), BF)]
        + [jax.ShapeDtypeStruct((block_rows, total // 2), BF)] * 2,
        grid_spec=pltpu.PrefetchScalarGridSpec(
            num_scalar_prefetch=1,
            grid=(2, tiles),
            in_specs=in_specs,
            out_specs=[
                pl.BlockSpec((tile, total), lambda b, i, s: (jnp.where(b == 0, i, tiles - 1), 0)),
            ]
            + [
                pl.BlockSpec((tile, total // 2), lambda b, i, s: (jnp.where(b == 0, 0, i), 0))
            ]
            * 2,
        ),
        compiler_params=pltpu.CompilerParams(vmem_limit_bytes=VMEM_BYTES),
        cost_estimate=cost(
            flops,
            2 * (weight.size + 2 * block_rows * (depth + total)),
            scale,
        ),
    )(blocks, *operands)


def logits_kernel(order_ref, rows_ref, router_ref, *outs):
    product = lax.dot_general(
        router_ref[...], rows_ref[...], (((0,), (1,)), ((), ())), preferred_element_type=F32
    )
    for block, o_ref in enumerate(outs):

        @pl.when(pl.program_id(0) == block)
        def _():
            o_ref[...] = product


def block_logits(order, rows, router, length):
    depth, experts = router.shape
    count = rows.shape[0] // length
    return pl.pallas_call(
        logits_kernel,
        out_shape=[jax.ShapeDtypeStruct((experts, length), F32)] * count,
        grid_spec=pltpu.PrefetchScalarGridSpec(
            num_scalar_prefetch=1,
            grid=(count,),
            in_specs=[
                pl.BlockSpec((length, depth), lambda i, s: (s[i], 0)),
                pl.BlockSpec((depth, experts), lambda i, s: (0, 0)),
            ],
            out_specs=[pl.BlockSpec((experts, length), lambda i, s: (0, 0))] * count,
        ),
        compiler_params=pltpu.CompilerParams(vmem_limit_bytes=VMEM_BYTES),
        cost_estimate=cost(0, 0),
    )(order, rows, router)


def mixed_rows(routes, rows, expert):
    first = (routes[:, 0:1] == expert).astype(F32).astype(BF)
    second = (routes[:, 1:2] == expert).astype(F32).astype(BF)
    return rows[0] * first + rows[1] * second


def merge_kernel(count, extra, transposed, blocks_ref, routes_ref, *refs):
    rows_refs, refs = refs[:count], refs[count:]
    logit_refs, refs = (refs[:count], refs[count:]) if extra else ((), refs)
    w_ref, o_ref, rows_ref = refs[0], refs[-3], refs[-2]
    logits_ref = refs[-1]
    for block in range(count):

        @pl.when(pl.program_id(0) == block)
        def _():
            rows_ref[...] = rows_refs[block][...]
            if extra:
                logits_ref[...] = logit_refs[block][...]

    experts = w_ref.shape[0]
    contract = (((1,), (1 if transposed else 0,)), ((), ()))
    routes = routes_ref[...]
    total = jnp.zeros(o_ref.shape, F32)
    for expert in range(experts):
        mixed = mixed_rows(routes, rows_ref, expert)
        total += lax.dot_general(mixed, w_ref[expert], contract, preferred_element_type=F32)
    if extra:
        pair_ref, router_ref = refs[1:3]
        for place in range(2):
            total += lax.dot_general(
                rows_ref[2 + place], pair_ref[place], contract, preferred_element_type=F32
            )
        total += lax.dot_general(
            logits_ref[...], router_ref[...], contract, preferred_element_type=F32
        )
    o_ref[...] = total.astype(o_ref.dtype)


def merge_matmul(order, routes, blocks, weight, extras, transposed):
    count = len(blocks)
    parts, length, width = blocks[0].shape
    depth = weight.shape[1] if transposed else weight.shape[2]
    tile = min(256, length)
    tiles = length // tile

    def own_tile(place):
        return lambda b, i: jnp.where(b == place, i, jnp.where(b < place, 0, tiles - 1))

    def rows_spec(place):
        index = own_tile(place)
        return pl.BlockSpec((parts, tile, width), lambda b, i, s: (0, index(b, i), 0))

    def logits_spec(place, lanes):
        index = own_tile(place)
        return pl.BlockSpec((tile, lanes), lambda b, i, s: (index(b, i), 0))

    in_specs = [pl.BlockSpec((tile, 2), lambda b, i, s: (s[b] * tiles + i, 0))]
    in_specs += [rows_spec(place) for place in range(count)]
    operands = [routes, *blocks]
    lanes = 128
    if extras:
        logit_blocks, pair, router = extras
        lanes = logit_blocks[0].shape[1]
        in_specs += [logits_spec(place, lanes) for place in range(count)]
        operands += logit_blocks
    in_specs.append(pl.BlockSpec(weight.shape, lambda b, i, s: (0, 0, 0)))
    operands.append(weight)
    if extras:
        in_specs.append(pl.BlockSpec(pair.shape, lambda b, i, s: (0, 0, 0)))
        in_specs.append(pl.BlockSpec(router.shape, lambda b, i, s: (0, 0)))
        operands += [pair, router]
    return pl.pallas_call(
        functools.partial(merge_kernel, count, bool(extras), transposed),
        out_shape=jax.ShapeDtypeStruct((count * length, depth), BF),
        grid_spec=pltpu.PrefetchScalarGridSpec(
            num_scalar_prefetch=1,
            grid=(count, tiles),
            in_specs=in_specs,
            out_specs=pl.BlockSpec((tile, depth), lambda b, i, s: (s[b] * tiles + i, 0)),
            scratch_shapes=[pltpu.VMEM((parts, tile, width), BF), pltpu.VMEM((tile, lanes), BF)],
        ),
        compiler_params=pltpu.CompilerParams(vmem_limit_bytes=VMEM_BYTES),
        cost_estimate=cost(
            2 * count * length * depth * width * (weight.shape[0] + 2 * bool(extras)),
            2 * (weight.size + count * length * (parts * width + depth)),
        ),
    )(order, *operands)


def right_grad_kernel(scalars_ref, routes_ref, left_ref, *refs):
    blocks, o_ref = refs[:-1], refs[-1]
    expert = scalars_ref[len(blocks)] + pl.program_id(0)
    total = None
    for place, block_ref in enumerate(blocks):
        length = block_ref.shape[1]
        span = pl.ds(pl.multiple_of(scalars_ref[place] * length, length), length)
        mixed = mixed_rows(routes_ref[span, :], block_ref, expert)
        product = jnp.dot(left_ref[:, span], mixed, preferred_element_type=F32)
        total = product if total is None else total + product
    o_ref[0] = total.astype(o_ref.dtype)


def left_grad_kernel(scalars_ref, routes_ref, rows_ref, *refs):
    blocks, o_ref = refs[:-1], refs[-1]
    expert = scalars_ref[len(blocks)] + pl.program_id(0)
    total = None
    for place, block_ref in enumerate(blocks):
        length = block_ref.shape[2]
        span = pl.ds(pl.multiple_of(scalars_ref[place] * length, length), length)
        first = (routes_ref[0:1, span] == expert).astype(F32).astype(BF)
        second = (routes_ref[1:2, span] == expert).astype(F32).astype(BF)
        mixed = block_ref[0] * first + block_ref[1] * second
        product = jnp.dot(mixed, rows_ref[span, :], preferred_element_type=F32)
        total = product if total is None else total + product
    o_ref[0] = total.astype(o_ref.dtype)


def expert_grads(kernel, order, base, count, routes, rows, blocks, shape, dtype):
    whole = lambda array: pl.BlockSpec(array.shape, lambda i, s: (0,) * array.ndim)
    scalars = jnp.concatenate([order, base.astype(jnp.int32).reshape(1)])
    tokens = len(blocks) * blocks[0].shape[1]
    return pl.pallas_call(
        kernel,
        out_shape=jax.ShapeDtypeStruct((count,) + shape, dtype),
        grid_spec=pltpu.PrefetchScalarGridSpec(
            num_scalar_prefetch=1,
            grid=(count,),
            in_specs=[whole(routes), whole(rows)]
            + [pl.BlockSpec((2,) + item.shape[1:], lambda i, s: (0, 0, 0)) for item in blocks],
            out_specs=pl.BlockSpec((1,) + shape, lambda i, s: (i, 0, 0)),
        ),
        compiler_params=pltpu.CompilerParams(vmem_limit_bytes=VMEM_BYTES),
        cost_estimate=cost(
            2 * count * shape[0] * shape[1] * tokens,
            2 * rows.size + 4 * tokens * shape[1] + 4 * count * shape[0] * shape[1],
        ),
    )(scalars, routes, rows, *blocks)


def plain_grad_kernel(scalars_ref, left_ref, *refs):
    blocks, o_ref = refs[:-1], refs[-1]
    total = None
    for place, block_ref in enumerate(blocks):
        length = block_ref.shape[1]
        span = pl.ds(pl.multiple_of(scalars_ref[place] * length, length), length)
        if len(o_ref.shape) == 2:
            product = lax.dot_general(
                block_ref[0], left_ref[:, span], (((0,), (1,)), ((), ())),
                preferred_element_type=F32,
            )[: o_ref.shape[0]]
        else:
            product = jnp.dot(left_ref[:, span], block_ref[0], preferred_element_type=F32)
        total = product if total is None else total + product
    o_ref[...] = total.astype(o_ref.dtype).reshape(o_ref.shape)


def plain_grad(order, part, left, blocks, dtype, lines=0):
    depth = left.shape[0]
    _, length, width = blocks[0].shape
    scalars = jnp.concatenate([order, jnp.asarray(part, jnp.int32).reshape(1)])
    count = len(blocks)
    shape = (lines, depth) if lines else (1, depth, width)
    return pl.pallas_call(
        plain_grad_kernel,
        out_shape=jax.ShapeDtypeStruct(shape, dtype),
        grid_spec=pltpu.PrefetchScalarGridSpec(
            num_scalar_prefetch=1,
            grid=(1,),
            in_specs=[pl.BlockSpec(left.shape, lambda i, s: (0, 0))]
            + [pl.BlockSpec((1, length, width), lambda i, s: (s[count], 0, 0)) for _ in blocks],
            out_specs=pl.BlockSpec(shape, lambda i, s: (0,) * len(shape)),
        ),
        compiler_params=pltpu.CompilerParams(vmem_limit_bytes=VMEM_BYTES),
        cost_estimate=cost(
            2 * left.size * width, 2 * (left.size + count * length * width) + 4 * depth * width
        ),
    )(scalars, left, *blocks)


def turn_kernel(*refs):
    count = len(refs) // 2
    for rows_ref, o_ref in zip(refs[:count], refs[count:]):
        o_ref[0] = rows_ref[0].T


def turn(blocks):
    lead, rows, width = blocks[0].shape
    return pl.pallas_call(
        turn_kernel,
        out_shape=[jax.ShapeDtypeStruct((lead, width, rows), item.dtype) for item in blocks],
        grid=(lead,),
        in_specs=[pl.BlockSpec((1, rows, width), lambda i: (i, 0, 0)) for _ in blocks],
        out_specs=[pl.BlockSpec((1, width, rows), lambda i: (i, 0, 0)) for _ in blocks],
        compiler_params=pltpu.CompilerParams(vmem_limit_bytes=VMEM_BYTES),
        cost_estimate=cost(0, 4 * len(blocks) * lead * rows * width),
    )(*blocks)


def spread_kernel(groups, starts_ref, places_ref, rows_ref, *refs):
    outs, totals = refs[: len(groups)], refs[len(groups) :]
    blocks = [bits for group in groups for bits in group]
    tokens = rows_ref.shape[0]
    for total_ref in totals:
        total_ref[...] = jnp.zeros(total_ref.shape, F32)
    slot = lax.broadcasted_iota(jnp.int32, (WINDOW, TILE), 0)
    for index in range(tokens // TILE):
        span = slice(index * TILE, (index + 1) * TILE)
        rows = rows_ref[span, :]
        for bits, total_ref in zip(blocks, totals):
            start = pl.multiple_of(starts_ref[bits, index], 16)
            hot = (slot == places_ref[bits : bits + 1, span] - start).astype(F32).astype(BF)
            product = jnp.dot(hot, rows, preferred_element_type=F32)
            total_ref[pl.ds(start, WINDOW), :] += product
    place = 0
    for group, o_ref in zip(groups, outs):
        for lead in range(len(group)):
            value = totals[place][...].astype(BF)
            if len(group) == 1:
                o_ref[...] = value
            else:
                o_ref[lead] = value
            place += 1


def spread_rows(starts, places, rows, slots, groups):
    tokens, width = rows.shape
    shapes = [
        (slots, width) if len(group) == 1 else (len(group), slots, width) for group in groups
    ]
    count = sum(len(group) for group in groups)
    return pl.pallas_call(
        functools.partial(spread_kernel, groups),
        out_shape=[jax.ShapeDtypeStruct(shape, BF) for shape in shapes],
        grid_spec=pltpu.PrefetchScalarGridSpec(
            num_scalar_prefetch=1,
            grid=(1,),
            in_specs=[
                pl.BlockSpec(places.shape, lambda i, s: (0, 0)),
                pl.BlockSpec((tokens, width), lambda i, s: (0, 0)),
            ],
            out_specs=[
                pl.BlockSpec(shape, lambda i, s, n=len(shape): (0,) * n) for shape in shapes
            ],
            scratch_shapes=[pltpu.VMEM((slots, width), F32) for _ in range(count)],
        ),
        compiler_params=pltpu.CompilerParams(vmem_limit_bytes=VMEM_BYTES),
        cost_estimate=cost(
            4 * count * WINDOW * tokens * width,
            2 * (tokens + count * slots) * width,
        ),
    )(starts, places, rows)


def gather_kernel(tiles, starts_ref, places_ref, *refs):
    o_ref = refs[-1]
    slot = lax.broadcasted_iota(jnp.int32, (TILE, WINDOW), 1)
    for index in range(tiles):
        span = slice(index * TILE, (index + 1) * TILE)
        total = jnp.zeros((TILE, o_ref.shape[1]), F32)
        for block, block_ref in enumerate(refs[:-1]):
            start = pl.multiple_of(starts_ref[block, pl.program_id(0) * tiles + index], 16)
            hot = (slot == places_ref[span, block : block + 1] - start).astype(F32).astype(BF)
            window = pl.ds(start, WINDOW)
            rows = block_ref[0, window, :] if len(block_ref.shape) == 3 else block_ref[window, :]
            total += jnp.dot(hot, rows, preferred_element_type=F32)
        o_ref[span, :] = total.astype(o_ref.dtype)


def gather_slots(starts, places, blocks):
    tokens = places.shape[0]
    lists = [item if isinstance(item, tuple) else (item, None) for item in blocks]
    slots, width = lists[0][0].shape[-2:]
    tiles = 4

    def spec(place):
        if place is None:
            return pl.BlockSpec((slots, width), lambda i, s: (0, 0))
        return pl.BlockSpec((1, slots, width), lambda i, s: (place, 0, 0))

    tile = tiles * TILE
    return pl.pallas_call(
        functools.partial(gather_kernel, tiles),
        out_shape=jax.ShapeDtypeStruct((tokens, width), BF),
        grid_spec=pltpu.PrefetchScalarGridSpec(
            num_scalar_prefetch=1,
            grid=(tokens // tile,),
            in_specs=[pl.BlockSpec((tile, places.shape[1]), lambda i, s: (i, 0))]
            + [spec(place) for _, place in lists],
            out_specs=pl.BlockSpec((tile, width), lambda i, s: (i, 0)),
        ),
        compiler_params=pltpu.CompilerParams(vmem_limit_bytes=VMEM_BYTES),
        cost_estimate=cost(
            4 * WINDOW * tokens * width * len(blocks),
            2 * (tokens + slots * len(blocks)) * width,
        ),
    )(starts, places, *[item for item, _ in lists])


def dots_kernel(transposed, lead, terms, count, stacked, *refs):
    outs = refs[terms * (1 + count) :]
    contract = (((1,), (1 if transposed else 0,)), ((), ()))
    operands = [ref[0] if flag else ref[...] for ref, flag in zip(refs, lead)]
    for place in range(count):
        o_ref = outs[0 if stacked else place]
        total = None
        for term in range(terms):
            right = operands[terms * (1 + place) + term]
            product = lax.dot_general(
                operands[term], right, contract, preferred_element_type=F32
            )
            total = product if total is None else total + product
        if stacked:
            outs[0][place] = total.astype(outs[0].dtype)
        else:
            o_ref[...] = total.astype(o_ref.dtype)


def dots(lefts, right_lists, transposed, dtype, stacked=False):
    operands, specs, lead = [], [], []
    rows = lefts[0][0].shape[1] if isinstance(lefts[0], tuple) else lefts[0].shape[0]
    tile = rows // 2 if rows % 32 == 0 else rows
    flops, size = 0, 0
    for side, items in enumerate([lefts] + list(right_lists)):
        for item in items:
            array, place = item if isinstance(item, tuple) else (item, None)
            shape = array.shape[-2:]
            block = (tile, shape[1]) if side == 0 else shape
            if place is None:
                specs.append(
                    pl.BlockSpec(block, (lambda i: (i, 0)) if side == 0 else (lambda i: (0, 0)))
                )
            elif side == 0:
                specs.append(pl.BlockSpec((1,) + block, lambda i, p=place: (p, i, 0)))
            else:
                specs.append(pl.BlockSpec((1,) + block, lambda i, p=place: (p, 0, 0)))
            operands.append(array)
            lead.append(place is not None)
            size += 2 * shape[0] * shape[1]
            if side:
                flops += 2 * rows * shape[0] * shape[1]
    width = shape[0] if transposed else shape[1]
    count = len(right_lists)
    if stacked:
        out_shape = [jax.ShapeDtypeStruct((count, rows, width), dtype)]
        out_specs = [pl.BlockSpec((count, tile, width), lambda i: (0, i, 0))]
    else:
        out_shape = [jax.ShapeDtypeStruct((rows, width), dtype)] * count
        out_specs = [pl.BlockSpec((tile, width), lambda i: (i, 0))] * count
    return pl.pallas_call(
        functools.partial(dots_kernel, transposed, lead, len(lefts), count, stacked),
        out_shape=out_shape,
        grid=(rows // tile,),
        in_specs=specs,
        out_specs=out_specs,
        compiler_params=pltpu.CompilerParams(vmem_limit_bytes=VMEM_BYTES),
        cost_estimate=cost(
            2 * flops,
            size + 2 * count * rows * width,
        ),
    )(*operands)


def pair_kernel(count, own_ref, other_ref, *refs):
    for place in range(count):
        for lead, left_ref in enumerate((own_ref, other_ref)):

            @pl.when(pl.program_id(0) == 2 * place + lead)
            def _():
                product = jnp.dot(left_ref[...], refs[place][0], preferred_element_type=F32)
                refs[count][0] = product.astype(refs[count].dtype)


def pair_dots(lefts, right_list, scale=COST):
    rows, depth = lefts[0].shape
    width = right_list[0].shape[2]
    count = len(right_list)

    def spec(place):
        return pl.BlockSpec(
            (1, depth, width), lambda i: (jnp.clip(i - 2 * place, 0, 1), 0, 0)
        )

    return pl.pallas_call(
        functools.partial(pair_kernel, count),
        out_shape=jax.ShapeDtypeStruct((2 * count, rows, width), BF),
        grid=(2 * count,),
        in_specs=[pl.BlockSpec((rows, depth), lambda i: (0, 0))] * 2
        + [spec(place) for place in range(count)],
        out_specs=pl.BlockSpec((1, rows, width), lambda i: (i, 0, 0)),
        compiler_params=pltpu.CompilerParams(vmem_limit_bytes=VMEM_BYTES),
        cost_estimate=cost(4 * count * rows * depth * width, 4 * rows * depth, scale),
    )(*lefts, *right_list)


def turned_kernel(pairs, rights, lead, merged, *refs):
    contract = (((0,), (0,)), ((), ()))
    outs = list(refs[2 * pairs + 2 * rights :])
    if merged:
        outs.insert(0, outs[0])
    operands = [ref[0] if flag else ref[...] for ref, flag in zip(refs, lead)]
    for pair in range(pairs):
        for place, o_ref in enumerate(outs):
            total = None
            for batch in (0, 1):
                left = operands[2 * pair + batch]
                right = operands[2 * pairs + 2 * place + batch]
                if len(outs) == 3 and place == 2:
                    left, right = right, left
                product = lax.dot_general(left, right, contract, preferred_element_type=F32)
                total = product if total is None else total + product
            lead = pair
            if merged and place == 1:
                lead += pairs
            o_ref[lead] = total[: o_ref.shape[1]].astype(o_ref.dtype)


def turned_dots(lefts, rights, dtypes, merged=False):
    operands, specs, lead, shapes = [], [], [], []
    for item in [each for pair in list(lefts) + list(rights) for each in pair]:
        array, place = item if isinstance(item, tuple) else (item, None)
        shape = array.shape[-2:]
        if place is None:
            specs.append(pl.BlockSpec(shape, lambda i: (0, 0)))
        else:
            specs.append(pl.BlockSpec((1,) + shape, lambda i, p=place: (p, 0, 0)))
        operands.append(array)
        lead.append(place is not None)
        shapes.append(shape)
    pairs, depth = len(lefts), shapes[0][1]
    outs = []
    flops = 0
    for place, dtype in enumerate(dtypes):
        width = shapes[2 * pairs + 2 * place][1]
        flops += 4 * pairs * shapes[0][0] * depth * width
        shape = (pairs, 8, depth) if place == 2 else (pairs, depth, width)
        if merged and place == 0:
            shape = (2 * pairs, depth, width)
        if not (merged and place == 1):
            outs.append(jax.ShapeDtypeStruct(shape, dtype))
    return pl.pallas_call(
        functools.partial(turned_kernel, pairs, len(rights), lead, merged),
        out_shape=outs,
        grid=(1,),
        in_specs=specs,
        out_specs=[pl.BlockSpec(out.shape, lambda i: (0, 0, 0)) for out in outs],
        compiler_params=pltpu.CompilerParams(vmem_limit_bytes=VMEM_BYTES),
        cost_estimate=cost(flops, flops // 300),
    )(*operands)


def flat(ref):
    return ref[0] if len(ref.shape) == 3 else ref[...]


def expert_kernel(count, owner_ref, other_ref, own_ref, sent_ref, *refs):
    rows_refs, gate_refs = refs[:count], refs[count : 2 * count]
    up_refs, router_refs = refs[2 * count : 3 * count], refs[3 * count : 4 * count]
    act_ref, gate_out, up_out, logit_out = refs[4 * count :]
    gate_pre = up_pre = logits = None
    for index in range(count):
        rows = flat(rows_refs[index])
        gate_part = jnp.dot(rows, flat(gate_refs[index]), preferred_element_type=F32)
        up_part = jnp.dot(rows, flat(up_refs[index]), preferred_element_type=F32)
        logit_part = jnp.dot(rows, router_refs[index][...], preferred_element_type=F32)
        gate_pre = gate_part if index == 0 else gate_pre + gate_part
        up_pre = up_part if index == 0 else up_pre + up_part
        logits = logit_part if index == 0 else logits + logit_part
    lane = lax.broadcasted_iota(jnp.int32, logits.shape, 1)
    signs = (lane == owner_ref[0]).astype(F32) - (lane == other_ref[...]).astype(F32)
    gate = jax.nn.sigmoid(jnp.sum(logits * signs, axis=1, keepdims=True))
    grad_act = own_ref[...] + sent_ref[...].astype(F32)
    sigmoid_gate = jax.nn.sigmoid(gate_pre)
    swish_gate = gate_pre * sigmoid_gate
    activation = swish_gate * up_pre
    act_ref[...] = (activation * gate).astype(BF)
    share = jnp.sum(grad_act * activation, axis=1, keepdims=True) * gate * (1.0 - gate)
    logit_out[...] = (share * signs).astype(BF)
    grad_activation = grad_act * gate
    swish_slope = sigmoid_gate * (1.0 + gate_pre * (1.0 - sigmoid_gate))
    gate_out[...] = (grad_activation * up_pre * swish_slope).astype(BF)
    up_out[...] = (grad_activation * swish_gate).astype(BF)


def expert_forward(owner, other, own, sent, rows, gates, ups, routers):
    slots, depth = own.shape[0], routers[0].shape[0]
    hidden = own.shape[1]
    lanes = routers[0].shape[1]
    tile = slots // 2 if slots % 32 == 0 else slots
    row_spec = lambda width: pl.BlockSpec((tile, width), lambda i, s: (i, 0))

    def rows_spec(item):
        if isinstance(item, tuple):
            return pl.BlockSpec((1, tile, depth), lambda i, s: (item[1], i, 0))
        return row_spec(depth)


    def whole(item):
        if isinstance(item, tuple):
            return pl.BlockSpec((1,) + item[0].shape[1:], lambda i, s: (item[1], 0, 0))
        return pl.BlockSpec(item.shape, lambda i, s: (0, 0))

    weights = list(gates) + list(ups) + list(routers)
    out_shapes = [jax.ShapeDtypeStruct((slots, hidden), BF)] * 3
    out_shapes.append(jax.ShapeDtypeStruct((slots, lanes), BF))
    return pl.pallas_call(
        functools.partial(expert_kernel, len(rows)),
        out_shape=out_shapes,
        grid_spec=pltpu.PrefetchScalarGridSpec(
            num_scalar_prefetch=1,
            grid=(slots // tile,),
            in_specs=[row_spec(1), row_spec(hidden), row_spec(hidden)]
            + [rows_spec(item) for item in rows]
            + [whole(item) for item in weights],
            out_specs=[row_spec(item.shape[1]) for item in out_shapes],
        ),
        compiler_params=pltpu.CompilerParams(vmem_limit_bytes=VMEM_BYTES),
        cost_estimate=cost(
            4 * len(rows) * slots * depth * hidden,
            4 * len(rows) * depth * hidden + 12 * slots * hidden,
        ),
    )(
        owner.reshape(1),
        other,
        own,
        sent,
        *[item[0] if isinstance(item, tuple) else item for item in list(rows) + weights],
    )


def assemble_kernel(order_ref, *refs):
    for block, ref in enumerate(refs[:-1]):

        @pl.when(pl.program_id(0) == block)
        def _():
            refs[-1][0] = flat(ref).astype(F32)


def assemble(order, blocks):
    count = len(blocks)
    arrays = [item[0] if isinstance(item, tuple) else item for item in blocks]
    rows, width = arrays[0].shape[-2:]
    tiles = ASSEMBLE if rows % (16 * ASSEMBLE) == 0 else 1

    def spec(place, item):
        def tile_of(b, i):
            return jnp.where(b == place, i, jnp.where(b < place, 0, tiles - 1))

        if isinstance(item, tuple):
            return pl.BlockSpec(
                (1, rows // tiles, width), lambda b, i, s: (item[1], tile_of(b, i), 0)
            )
        return pl.BlockSpec((rows // tiles, width), lambda b, i, s: (tile_of(b, i), 0))

    return pl.pallas_call(
        assemble_kernel,
        out_shape=jax.ShapeDtypeStruct((count, rows, width), F32),
        grid_spec=pltpu.PrefetchScalarGridSpec(
            num_scalar_prefetch=1,
            grid=(count, tiles),
            in_specs=[spec(place, item) for place, item in enumerate(blocks)],
            out_specs=pl.BlockSpec(
                (1, rows // tiles, width), lambda b, i, s: (s[b], i, 0)
            ),
        ),
        compiler_params=pltpu.CompilerParams(vmem_limit_bytes=VMEM_BYTES),
        cost_estimate=cost(0, 7 * count * rows * width),
    )(order, *arrays)


def allowed_keys(row_segments, column_segments):
    length = row_segments.shape[0]
    query = lax.broadcasted_iota(jnp.int32, (length, length), 0)
    key = lax.broadcasted_iota(jnp.int32, (length, length), 1)
    same = (column_segments == 0) | (column_segments == row_segments)
    return same & (key <= query)


def weights_of(query, key, allowed):
    scores = lax.dot_general(query, key, (((1,), (1,)), ((), ())), preferred_element_type=F32)
    scores = jnp.where(allowed, scores * HD ** (-0.5), NEGATIVE)
    weights = jnp.exp(scores - jnp.max(scores, axis=1, keepdims=True))
    return weights / jnp.sum(weights, axis=1, keepdims=True)


def attend_kernel(
    logits_ref, routes_ref, kept_ref, rows_ref, columns_ref, *refs
):
    parts, refs = refs[:12], refs[12:]
    saved_ref, mixed_ref, gated_ref, side_ref, cos_ref, sin_ref = refs

    @pl.when(pl.program_id(0) == 0)
    def _():
        logits = logits_ref[...]
        label = lax.broadcasted_iota(jnp.int32, logits.shape, 0)
        picked = [
            jnp.sum(jnp.where(label == routes_ref[place : place + 1, :], logits, 0.0), axis=0)
            for place in (0, 1)
        ]
        gates = [
            jax.nn.sigmoid(picked[place] - picked[1 - place])[None, :] for place in (0, 1)
        ]
        lines = [gates[place] * kept_ref[place : place + 1, :] for place in (0, 1)]
        lines.append(gates[0] * gates[1])
        lines += [routes_ref[place : place + 1, :].astype(F32) for place in (0, 1)]
        lines += [kept_ref[place : place + 1, :] for place in (0, 1)]
        lines.append(jnp.zeros((128 - len(lines), logits.shape[1]), F32))
        side_ref[...] = jnp.concatenate(lines, axis=0).T
        cos_ref[...], sin_ref[...] = rope_lines(rows_ref[...], columns_ref[...])

    summed = [
        parts[place][...].astype(F32)
        + parts[4 + place][...].astype(F32)
        + parts[8 + place][...].astype(F32)
        for place in range(4)
    ]
    cosine, sine = cos_ref[...], sin_ref[...]
    turned = [
        (item * cosine + pltpu.roll(item, HD // 2, 1) * sine).astype(BF) for item in summed[:3]
    ]
    turned.append(summed[3].astype(BF))
    for place in range(4):
        saved_ref[place] = turned[place]
    allowed = allowed_keys(rows_ref[...], columns_ref[...])
    for place in range(2):
        probs = weights_of(turned[place], turned[2], allowed).astype(BF)
        mixed = jnp.dot(probs, turned[3], preferred_element_type=F32)
        mixed_ref[place] = mixed
        gated_ref[place] = (mixed * side_ref[:, place : place + 1]).astype(BF)


def head_parts(parts, count, length, heads):
    specs, arrays = [], []
    for part in parts:
        each = count // len(part)
        for place in range(count):
            start = place % each * heads
            specs.append(pl.BlockSpec((length, HD), lambda h, s=start: (0, s + h)))
            arrays.append(part[place // each])
    return specs, arrays


def attend(logits, routes, kept, segments, parts):
    length = logits.shape[1]
    heads = parts[0][0].shape[1] // (4 * HD)
    whole = lambda array: pl.BlockSpec(array.shape, lambda h: (0, 0))
    part_specs, part_arrays = head_parts(parts, 4, length, heads)
    small = [logits, routes, kept, segments.reshape(length, 1), segments.reshape(1, length)]
    return pl.pallas_call(
        attend_kernel,
        out_shape=[
            jax.ShapeDtypeStruct((4, length, heads * HD), BF),
            jax.ShapeDtypeStruct((2, length, heads * HD), F32),
            jax.ShapeDtypeStruct((2, length, heads * HD), BF),
        ]
        + [jax.ShapeDtypeStruct((length, 128), F32)] * 3,
        grid=(heads,),
        in_specs=[whole(item) for item in small] + part_specs,
        out_specs=[
            pl.BlockSpec((count, length, HD), lambda h: (0, 0, h)) for count in (4, 2, 2)
        ]
        + [pl.BlockSpec((length, 128), lambda h: (0, 0))] * 3,
        compiler_params=pltpu.CompilerParams(vmem_limit_bytes=VMEM_BYTES),
        cost_estimate=cost(
            16 * heads * length * length * HD,
            12 * length * heads * HD * 4,
        ),
    )(*small, *part_arrays)


def attend_back_kernel(
    side_ref, rows_ref, columns_ref, cos_ref, sin_ref, saved_ref, mixed_ref, *refs
):
    parts, (out_ref, logit_ref, share_ref) = refs[:6], refs[6:]
    allowed = allowed_keys(rows_ref[...], columns_ref[...])
    key, value = saved_ref[2], saved_ref[3]
    cosine, sine = cos_ref[...], sin_ref[...]
    scale = HD ** (-0.5)
    over_rows = (((0,), (0,)), ((), ()))
    over_last = (((1,), (1,)), ((), ()))

    def unturn(item):
        return (item * cosine - pltpu.roll(item, HD // 2, 1) * sine).astype(BF)

    @pl.when(pl.program_id(0) == 0)
    def _():
        share_ref[...] = jnp.zeros(share_ref.shape, F32)

    lane = lax.broadcasted_iota(jnp.int32, share_ref.shape, 1)
    grad_key = grad_value = 0.0
    for place in range(2):
        grad = (
            parts[place][...].astype(F32)
            + parts[2 + place][...].astype(F32)
            + parts[4 + place][...].astype(F32)
        )
        share = jnp.sum(grad * mixed_ref[place], axis=1, keepdims=True)
        share_ref[...] += jnp.where(lane == place, share, 0.0)
        grad = (grad * side_ref[:, place : place + 1]).astype(BF)
        query = saved_ref[place]
        probs = weights_of(query, key, allowed)
        grad_value += lax.dot_general(
            probs.astype(BF), grad, over_rows, preferred_element_type=F32
        )
        grad_probs = lax.dot_general(grad, value, over_last, preferred_element_type=F32)
        centred = jnp.sum(probs * grad_probs, axis=1, keepdims=True)
        grad_scores = (probs * (grad_probs - centred)).astype(BF)
        grad_query = jnp.dot(grad_scores, key, preferred_element_type=F32) * scale
        out_ref[place] = unturn(grad_query)
        grad_key += lax.dot_general(
            grad_scores, query, over_rows, preferred_element_type=F32
        )
    out_ref[2] = unturn(grad_key * scale)
    out_ref[3] = grad_value.astype(BF)

    @pl.when(pl.program_id(0) == pl.num_programs(0) - 1)
    def _():
        shares = [
            share_ref[:, place : place + 1] * side_ref[:, 5 + place : 6 + place]
            for place in (0, 1)
        ]
        share = (shares[0] - shares[1]) * side_ref[:, 2:3]
        label = lane.astype(F32)
        signs = (label == side_ref[:, 3:4]).astype(F32) - (label == side_ref[:, 4:5]).astype(F32)
        logit_ref[...] = (share * signs).astype(BF)


def attend_back(side, segments, cosine, sine, saved, mixed, parts):
    length = side.shape[0]
    heads = saved.shape[2] // HD
    whole = lambda array: pl.BlockSpec(array.shape, lambda h: (0, 0))
    part_specs, part_arrays = head_parts(parts, 2, length, heads)
    small = [side, segments.reshape(length, 1), segments.reshape(1, length), cosine, sine]
    return pl.pallas_call(
        attend_back_kernel,
        out_shape=[
            jax.ShapeDtypeStruct((4, length, heads * HD), BF),
            jax.ShapeDtypeStruct((length, 128), BF),
        ],
        grid=(heads,),
        in_specs=[whole(item) for item in small]
        + [pl.BlockSpec((count, length, HD), lambda h: (0, 0, h)) for count in (4, 2)]
        + part_specs,
        out_specs=[
            pl.BlockSpec((4, length, HD), lambda h: (0, 0, h)),
            pl.BlockSpec((length, 128), lambda h: (0, 0)),
        ],
        scratch_shapes=[pltpu.VMEM((length, 128), F32)],
        compiler_params=pltpu.CompilerParams(vmem_limit_bytes=VMEM_BYTES),
        cost_estimate=cost(
            40 * heads * length * length * HD,
            20 * length * heads * HD * 4,
        ),
    )(*small, saved, mixed, *part_arrays)


def swap(value, axes, bits, size):
    if bits == 0:
        return value
    return lax.ppermute(value, axes, [(i, i ^ bits) for i in range(size)])


def row_gather(values):
    return lax.all_gather(values, "row", axis=0, tiled=True)


def row_total(values, *waits):
    total = lax.psum_scatter(values, "row", scatter_dimension=0, tiled=True)
    return (after(total, *waits) if waits else total).astype(F32)


def col_total(values):
    return lax.psum(values, "col")


def small_total(value, axes):
    for axis in axes:
        size = lax.axis_size(axis)
        bits = 1
        while bits < size:
            value = value + swap(value, axis, bits, size)
            bits *= 2
    return value


def norm_factor(rows_in):
    squares = col_total(jnp.sum(rows_in * rows_in, axis=1))
    return lax.rsqrt(squares / D + EPSILON)


def norm_backward(rows_in, factor, gain_row, grad_in):
    scaled = grad_in * gain_row
    inner_sum = col_total(jnp.sum(scaled * rows_in, axis=1))[:, None]
    gain_grad = jnp.sum(grad_in * rows_in * factor, axis=0)
    return (factor * scaled - rows_in * factor**3 * inner_sum / D, gain_grad)


def local(
    hidden_in,
    gain_attn,
    router_attn,
    query_weight,
    kv_weight,
    out_weight,
    gain_ffn,
    router_ffn,
    gate_weight,
    up_weight,
    down_weight,
    attn_routes,
    ffn_routes,
    attn_order,
    ffn_order,
    segment_ids,
    d_out,
):
    dp_count, col_count = lax.axis_size("dp"), lax.axis_size("col")
    dp_index, col_index = lax.axis_index("dp"), lax.axis_index("col")
    owners = dp_count * col_count
    owner = dp_index * col_count + col_index
    batch_rows = attn_routes.shape[0]
    group_rows = batch_rows // col_count
    features = hidden_in.shape[1]
    attn_experts = query_weight.shape[0]
    ffn_experts = gate_weight.shape[0]
    half_experts = attn_experts // dp_count
    attn_capacity = 5 * batch_rows // (2 * attn_experts)
    slots = 5 * batch_rows // (2 * ffn_experts)
    head_width = query_weight.shape[2]
    pair_axes = ("dp", "col")

    def cross(pair, *waits):
        received = swap(pair, "col", 2, col_count)
        hop = swap(lead_block(after(received, *waits), 1), "col", 1, col_count)
        return [(received, 0), (hop, 0)]

    def fence(rows, numbers):
        token = swap(tip(rows), "col", 1, col_count)[0, 0]
        return numbers + (token != token).astype(jnp.int32)

    def arrays(blocks):
        return [item[0] if isinstance(item, tuple) else item for item in blocks]

    def flagged(blocks):
        return [(item, 0) for item in blocks]

    offsets = (owner ^ jnp.arange(owners, dtype=jnp.int32)).astype(jnp.int32)
    block_order = (col_index ^ jnp.arange(col_count, dtype=jnp.int32)).astype(jnp.int32)
    hidden_all = row_gather(hidden_in)
    rows_in = hidden_in.astype(F32)
    factor_a = norm_factor(rows_in)
    gate_cross = cross(take_blocks(gate_weight, after(offsets, factor_a), 2, 1, 2))
    factor_a_all = row_gather(factor_a)
    lane_router_f = jnp.pad(
        after(router_ffn, factor_a), ((0, 0), (0, 128 - ffn_experts))
    )
    router_blocks = [swap(lane_router_f, "col", bits, col_count) for bits in range(col_count)]
    owner_rows, owner_starts = token_slots(
        ffn_routes, after(ffn_order, factor_a), offsets, ffn_experts, slots
    )
    (
        hidden_all,
        owner_rows,
        owner_starts,
        offsets,
        block_order,
    ) = lax.optimization_barrier((hidden_all, owner_rows, owner_starts, offsets, block_order))
    grad_out_all = row_gather(after(d_out, hidden_all))

    gain_a = gain_attn.astype(F32)
    normed_all = (hidden_all.astype(F32) * factor_a_all[:, None] * gain_a).astype(BF)

    def col_scatter(rows, weight, extra_weight, transposed, first_waits, near_waits, near_first):
        def part(blocks, scale):
            kept, *sent = pick_matmul(
                blocks, attn_routes, rows, weight, extra_weight, group_rows, transposed, scale
            )
            return kept, [swap(item, "col", 1, col_count) for item in sent]

        near_order = after(block_order[0:2], *first_waits)
        far_order = after(block_order[2:4], *first_waits)
        if near_first:
            near = part(near_order, COST)
            far_order = after(far_order, near[0])
        kept, received = part(far_order, COST)
        far = join_halves(kept, received)
        if not near_first:
            near = part(after(near_order, far, *near_waits), 1)
        return [[near[0]], near[1], far, [swap(far, "col", 2, col_count)]]

    projected = col_scatter(
        normed_all, query_weight, kv_weight, False, [], [gate_cross[0][0]], False
    )

    far_sent = projected[2]
    logits_sent = block_logits(
        after(block_order, far_sent), normed_all, router_attn, group_rows
    )
    attn_kept = kept_pairs(
        attn_routes, after(attn_order, logits_sent[0]), attn_experts, attn_capacity
    )
    segments = segment_ids.reshape(-1)
    kept_a = attn_kept.reshape(2, batch_rows // TILE, TILE)
    kept_a = lax.dynamic_slice_in_dim(
        kept_a, col_index * (group_rows // TILE), group_rows // TILE, 1
    ).reshape(2, group_rows)
    routes_a = lax.dynamic_slice_in_dim(
        after(attn_routes, far_sent), col_index * group_rows, group_rows, 0
    ).T

    up_pair = take_blocks(up_weight, after(offsets, far_sent), 2, 1, 2)
    route_sums = jnp.sum(after(ffn_routes, far_sent), axis=1).astype(BF)
    route_sums = jnp.broadcast_to(route_sums[:, None], (batch_rows, 128))
    near_sums, far_sums = spread_rows(
        after(owner_starts, logits_sent[0]), owner_rows, route_sums, slots, [(0,), (col_count,)]
    )
    far_sums = swap(far_sums[:, 0:8], pair_axes, col_count, owners)
    slot_other = [item[:, 0:1].astype(jnp.int32) - owner for item in (near_sums, far_sums)]
    logits_sent, _ = lax.optimization_barrier(
        (logits_sent, (up_pair, kept_a, routes_a, slot_other))
    )
    logits_a = sum(
        swap(logits_sent[bits], "col", bits, col_count) for bits in range(col_count)
    )
    saved, attended, gated_out, side, cosine, sine_rows = attend(
        logits_a,
        routes_a,
        kept_a,
        segments,
        projected[0:2] + projected[3:],
    )

    half_bits = (0, 1, col_count, col_count + 1)
    grad_groups = spread_rows(
        after(owner_starts, gated_out),
        owner_rows,
        grad_out_all,
        slots,
        [(bits, bits ^ 2) for bits in half_bits],
    )
    grad_far = [swap(grad_groups[place], pair_axes, col_count, owners) for place in (2, 3)]

    lane_router = jnp.pad(
        after(router_attn, gated_out), ((0, 0), (0, 128 - attn_experts))
    )
    down_sent = [
        take_blocks(down_weight, after(offsets, grad_groups[0]), bits, 2, 2) for bits in (0, 1)
    ]

    def col_blocks(block, *waits):
        far = swap(block, "col", 2, col_count)
        near = swap(block, "col", 1, col_count)
        return [block, near, far, swap(after(far, *waits), "col", 1, col_count)]

    gated_blocks = col_blocks(gated_out, lane_router, *down_sent, *router_blocks)
    up_received = swap(after(up_pair, gated_blocks[2]), "col", 2, col_count)
    attn_part = merge_matmul(block_order, attn_routes, gated_blocks, out_weight, (), False)
    down_pairs = [down_sent[0], swap(down_sent[1], "col", 1, col_count)]

    grad_pairs = [grad_groups[0], swap(grad_groups[1], "col", 1, col_count)]

    def grad_act_part(batch, lead, dtype, *waits):
        return dots(
            [(array, lead) for array in grad_pairs[2 * batch : 2 * batch + 2]],
            [[(after(down_pairs[0], *waits), lead), (down_pairs[1], lead)]],
            True,
            dtype,
        )[0]

    grad_act_out = [grad_act_part(0, 1, BF, attn_part)]
    up_side = lead_block(after(up_received, grad_far[0], *grad_act_out), 1)
    up_cross = [(up_received, 0), (swap(up_side, "col", 1, col_count), 0)]
    middle = rows_in + row_total(attn_part, up_cross[1][0])
    gain_f = gain_ffn.astype(F32)
    factor_f = norm_factor(middle)[:, None]
    normed_f = (middle * factor_f * gain_f).astype(BF)
    normed_f_all = row_gather(normed_f)
    gate_near, gate_own = [
        take_blocks(gate_weight, after(offsets, normed_f), bits, 1, 1) for bits in (1, 0)
    ]
    up_near, up_own = [
        take_blocks(up_weight, after(offsets, gate_own), bits, 1, 1) for bits in (1, 0)
    ]
    gate_blocks = flagged([gate_own, swap(gate_near, "col", 1, col_count)]) + gate_cross
    up_blocks = flagged([up_own, swap(up_near, "col", 1, col_count)]) + up_cross

    grad_act_sent = [swap(after(grad_act_out[0], normed_f), "col", 2, col_count)]
    own_early = grad_act_part(0, 0, F32, normed_f)
    grad_hop = after(grad_far[1], own_early, up_own, up_near, grad_act_sent[0])
    grad_pairs += [grad_far[0], swap(grad_hop, "col", 1, col_count)]
    grad_act_out.append(grad_act_part(1, 1, BF, normed_f))
    grad_act_sent.append(swap(grad_act_out[1], "col", 2, col_count))
    send_starts = after(owner_starts, up_own, up_near, own_early, grad_act_out[1])
    order = [(2, 3), (6,), (7,)], [(4,), (5,), (1,), (0,)]
    slots_f = {}
    for part in order:
        blocks = spread_rows(send_starts, owner_rows, normed_f_all, slots, part)
        for group, block in zip(part, blocks):
            received = swap(block, pair_axes, group[0], owners)
            if len(group) == 1:
                slots_f[group[0]] = received
            else:
                slots_f[group[0]] = (received, 0)
                side_block = swap(lead_block(received, 1), "col", 1, col_count)
                slots_f[group[1]] = (side_block, 0)
        send_starts = after(send_starts, *blocks)
    normed_turned = turn([after(normed_all, blocks[0])[None]])[0][0]
    gated_turned = turn([after(gated_blocks[0], blocks[0])] + gated_blocks[1:])
    acts, grad_gates, grad_ups, grad_logits = [], [], [], []
    back_blocks = {}

    def send_back(pair):
        batch = pair[0] // col_count
        blocks = dots(
            [grad_gates[batch], grad_ups[batch], grad_logits[batch]],
            [
                [part[bits % col_count] for part in (gate_blocks, up_blocks, router_blocks)]
                for bits in pair
            ],
            True,
            BF,
            pair[0] == col_count + 2,
        )
        if len(blocks) == 1:
            received = swap(blocks[0], pair_axes, pair[0], owners)
            back_blocks[pair[0]] = (received, 0)
            hop = swap(lead_block(received, 1), "col", 1, col_count)
            back_blocks[pair[1]] = (hop, 0)
        else:
            for bits, block in zip(pair, blocks):
                back_blocks[bits] = swap(block, pair_axes, bits, owners)
        return blocks[0]

    grad_act_own = [own_early, grad_act_part(1, 0, F32, blocks[0])]
    back_sent = after(blocks[0], normed_turned, gated_turned[0])
    for batch in (0, 1):
        act, grad_gate, grad_up, grad_logit = expert_forward(
            owner.astype(jnp.int32),
            after(slot_other[batch], back_sent),
            grad_act_own[batch],
            grad_act_sent[batch],
            [slots_f[batch * col_count + bits] for bits in range(col_count)],
            gate_blocks,
            up_blocks,
            router_blocks,
        )
        acts.append(act)
        grad_gates.append(grad_gate)
        grad_ups.append(grad_up)
        grad_logits.append(grad_logit)
        back_sent = send_back((2, 3) if batch == 0 else (6, 7))
    back_sent = send_back((4, 5))
    grad_logits[0] = after(grad_logits[0], back_sent)
    back_sent = send_back((1, 0))

    def weight_grads(pair, dtype, wait, merged=False):
        return turned_dots(
            [(slots_f[bits], slots_f[bits + col_count]) for bits in pair],
            [grad_gates, grad_ups, (after(grad_logits[0], wait), grad_logits[1])],
            [dtype, dtype, F32],
            merged,
        )

    both_far, router_far = weight_grads((2, 3), BF, back_sent, True)
    grad_normed_f_part = gather_slots(
        after(owner_starts, both_far),
        owner_rows.T,
        [back_blocks[bits] for bits in range(owners)],
    )
    gate_near, up_near, router_near = weight_grads((0,), F32, grad_normed_f_part)
    gate_side, up_side, router_side = weight_grads((1,), BF, router_near)

    act_near = swap(after(acts[0], grad_normed_f_part), "col", 2, col_count)
    grad_normed_f = row_total(grad_normed_f_part, act_near, router_side)

    middle_norm_grad, gain_ffn_grad = norm_backward(middle, factor_f, gain_f, grad_normed_f)
    grad_middle = d_out.astype(F32) + middle_norm_grad
    grad_middle_low = grad_middle.astype(BF)
    grad_middle_all = row_gather(grad_middle_low)
    act_far = swap(after(acts[1], grad_middle_low), "col", 2, col_count)
    act_pairs = [(acts[0], act_near), (acts[1], act_far)]
    gate_near_sent = swap(gate_side, "col", 1, col_count)
    up_near_sent = swap(up_side, "col", 1, col_count)

    down_blocks = {}

    def down_pair(place, sent, start):
        bits = half_bits[place]
        down_blocks[bits], down_blocks[bits ^ 2] = (sent, start), (sent, start + 1)

    near_down = [
        pair_dots(act_pairs[0], [after(down_pairs[place], grad_middle_low)])
        for place in (0, 1)
    ]
    down_pair(0, near_down[0], 0)
    down_pair(1, swap(near_down[1], "col", 1, col_count), 0)

    far_down = pair_dots(
        act_pairs[1], [after(down_pairs[0], near_down[1]), down_pairs[1]]
    )
    far_sent = swap(far_down, pair_axes, col_count, owners)
    down_pair(2, far_sent, 0)
    down_hop = swap(
        take_blocks(far_sent, after(jnp.arange(4, dtype=jnp.int32), far_down), 2, 1, 2),
        "col",
        1,
        col_count,
    )
    down_pair(3, down_hop, 0)
    grad_gated = col_scatter(
        grad_middle_all, out_weight, None, True, [far_down], [], True
    )
    own_base = dp_index * half_experts
    away_base = (1 - dp_index) * half_experts

    def out_grads(base, dtype):
        return expert_grads(
            left_grad_kernel,
            block_order,
            base,
            half_experts,
            attn_routes.T,
            grad_middle_all,
            gated_turned,
            (head_width, features),
            dtype,
        )

    pieces, grad_logits_a = attend_back(
        side,
        segments,
        cosine,
        sine_rows,
        saved,
        attended,
        grad_gated[0:2] + grad_gated[3:],
    )

    out_away = out_grads(after(away_base, pieces), BF)
    ffn_part = gather_slots(
        fence(out_away, owner_starts),
        owner_rows.T,
        [down_blocks[bits] for bits in range(owners)],
    )
    ffn_total = row_total(ffn_part)
    out_away_sent = swap(out_away, "dp", 1, dp_count)

    def down_grad_part(near, dtype, wait):
        lefts = [(after(acts[0], wait), acts[1]), (act_near, act_far)]
        return [
            turned_dots(
                [lefts[lead]],
                [[(grad_pairs[place], lead) for place in (near, 2 + near)]],
                [dtype],
            )[0]
            for lead in (0, 1)
        ]

    down_away = down_grad_part(1, BF, ffn_part)
    logits_back = col_blocks(grad_logits_a)
    pieces_blocks = col_blocks(pieces, *down_away)
    normed_part = merge_matmul(
        block_order,
        attn_routes,
        pieces_blocks,
        query_weight,
        (logits_back, kv_weight, lane_router),
        True,
    )

    def query_grads(base, dtype):
        return expert_grads(
            right_grad_kernel,
            block_order,
            base,
            half_experts,
            attn_routes,
            normed_turned,
            pieces_blocks,
            (features, head_width),
            dtype,
        )

    query_away = query_grads(after(away_base, normed_part), BF)
    kv_away = plain_grad(
        fence(query_away, block_order), 3 - dp_index, normed_turned, pieces_blocks, BF
    )
    query_sent = swap(query_away, "dp", 1, dp_count)
    kv_sent = swap(kv_away, "dp", 1, dp_count)
    query_own = query_grads(after(own_base, kv_away), F32)
    kv_own = plain_grad(
        block_order, after(2 + dp_index, query_own), normed_turned, pieces_blocks, F32
    )
    router_attn_grad = plain_grad(
        block_order,
        after(0 * dp_index, kv_own),
        normed_turned,
        [item[None] for item in logits_back],
        F32,
        attn_experts,
    )
    both_received = swap(after(both_far, pieces_blocks[2], logits_back[2]), "col", 2, col_count)
    tail = after(block_order, router_attn_grad)
    down_sent = [swap(item, "col", 1, col_count) for item in down_away]
    out_own = out_grads(after(own_base, router_attn_grad), F32)
    down_near = down_grad_part(0, F32, out_own)
    down_grad = assemble(
        after(tail, *down_near),
        [(down_near[0], 0), (down_sent[0], 0), (down_near[1], 0), (down_sent[1], 0)],
    )
    out_grad = add_wide(out_own, after(out_away_sent, down_grad))
    both_side = take_blocks(
        both_received,
        after(jnp.arange(4, dtype=jnp.int32), down_grad, out_grad, query_sent),
        1,
        2,
        2,
    )
    both_side = swap(both_side, "col", 1, col_count)
    grad_normed = row_total(normed_part, both_side)
    input_norm_grad, gain_attn_grad = norm_backward(
        rows_in, factor_a[:, None], gain_a, grad_normed
    )
    input_grad = grad_middle + input_norm_grad
    layer_out = (middle + ffn_total).astype(BF)
    small = jnp.concatenate(
        [
            router_attn_grad,
            gain_ffn_grad[None],
            gain_attn_grad[None],
            router_near[0],
            router_side[0],
            router_far[0],
            router_far[1],
        ],
        axis=0,
    )
    small = small_total(small, ("row", "dp"))
    lines = attn_experts + 2
    gain_ffn_grad, gain_attn_grad = small[lines - 2], small[lines - 1]
    router_ffn_grad = sum(
        swap(
            small[lines + bits * ffn_experts : lines + (bits + 1) * ffn_experts],
            "col",
            bits,
            col_count,
        )
        for bits in range(col_count)
    )
    gate_grad, up_grad = [
        assemble(tail, [(near, 0), (sent, 0), (both_received, 2 * place), (both_side, place)])
        for place, (near, sent) in enumerate(
            ((gate_near, gate_near_sent), (up_near, up_near_sent))
        )
    ]
    query_grad = add_wide(query_own, after(query_sent, up_grad))
    kv_grad = add_wide(kv_own, after(kv_sent, up_grad))
    ffn_half = ffn_experts // dp_count
    router_ffn_grad = lax.dynamic_slice_in_dim(
        router_ffn_grad, dp_index * ffn_half, ffn_half, 0
    ).T
    router_attn_grad = lax.dynamic_slice_in_dim(
        small, dp_index * half_experts, half_experts, 0
    ).T
    return (
        layer_out,
        input_grad,
        gain_attn_grad,
        router_attn_grad,
        query_grad,
        kv_grad,
        out_grad,
        gain_ffn_grad,
        router_ffn_grad,
        gate_grad,
        up_grad,
        down_grad,
    )


def solution(mesh):
    in_specs = (
        P(("dp", "row"), "col"),
        P("col"),
        P("col", None),
        P(None, "col", "row"),
        P(None, "col", "row"),
        P(None, "row", "col"),
        P("col"),
        P("col", None),
        P(None, "col", "row"),
        P(None, "col", "row"),
        P(None, "row", "col"),
        P("dp", None),
        P("dp", None),
        P("dp", None),
        P("dp", None),
        P(("dp", "col"), None),
        P(("dp", "row"), "col"),
    )
    out_specs = (
        P(("dp", "row"), "col"),
        P(("dp", "row"), "col"),
        P("col"),
        P("col", "dp"),
        P("dp", "col", "row"),
        P("dp", "col", "row"),
        P("dp", "row", "col"),
        P("col"),
        P("col", "dp"),
        P("dp", "col", "row"),
        P("dp", "col", "row"),
        P("dp", "row", "col"),
    )
    return jax.shard_map(local, mesh=mesh, in_specs=in_specs, out_specs=out_specs, check_vma=False)
```

time: 1270 us -> 953 us (0.75)
  waiting for transfers between devices: 554 us -> 267 us
  Pallas kernels: 386 us -> 514 us
  local copies, waits for them, and re-layouts: 90.5 us -> 30.3 us
  matrix products: 35.7 us -> 0 us
  other arithmetic: 55.3 us -> 26.9 us
  blocking collectives: 65 us -> 40 us
    ppermute x76 -> x75, waiting for transfers between devices: 473 us -> 250 us  [swap(): return lax.ppermute(value, axes, [(i, i ^ bits) for i in range(size)])]
    pallas_call x10 -> x41, Pallas kernels: 98 us -> 222 us  [the longest x7 61.4 us: turned_dots(): pl.pallas_call(functools.partial(turned_kernel, pairs, len(rights), lead,...]
    dot_general x16 -> x0, matrix products: 35.7 us -> none  [the longest x8 22.8 us: local(): jnp.dot(act_pairs[slot // 2][lead], down_pairs[slot % 2][lead], preferred...]
    reduce_scatter x4, waiting for transfers between devices: 34.9 us -> 1.57 us  [row_total(): total = lax.psum_scatter(values, 'row', scatter_dimension=0, tiled=True)]
    all_gather x4, waiting for transfers between devices: 45.8 us -> 14.7 us  [row_gather(): return lax.all_gather(values, 'row', axis=0, tiled=True)]
    psum x4, blocking collectives: 53 us -> 27.5 us  [col_total(): return lax.psum(values, 'col')]
    dynamic_update_slice x12 -> x0, local copies, waits for them, and re-layouts: 21 us -> none  [col_gather(): result = lax.dynamic_update_slice_in_dim(result, blocks[bits], start, axis)]
    squeeze x5 -> x1, local copies, waits for them, and re-layouts: 14.2 us -> 0.01 us  [local(): router_far[1]]
  transfers between devices with their start and end apart: 84 -> 83, of which waited for: 31 -> 38; matrix products, arithmetic and copies ran while one was open for 12% -> 3% of each run, Pallas kernels for 25% -> 50%
where the time goes in v2:
time: 953 us; the launch traced here: 946 us
  Pallas kernels  514 us (54%)
  waiting for transfers between devices  267 us (28%)
  starting transfers between devices  50 us (5%)
  blocking collectives  40 us (4%)
  local copies, waits for them, and re-layouts  30.3 us (3%)
  other arithmetic  26.9 us (3%)
  between operations  17.9 us (2%)
    ppermute x75, waiting for transfers between devices, swap(): return lax.ppermute(value, axes, [(i, i ^ bits) for i in range(size)])  250 us
    pallas_call x7, Pallas kernels, turned_dots(): pl.pallas_call(functools.partial(turned_kernel, pairs, len(rights), lead,...  61.4 us
    pallas_call x8, Pallas kernels, dots(): pl.pallas_call(functools.partial(dots_kernel, transposed, lead, len(lefts...  59.7 us
    ppermute x75, starting transfers between devices, swap(): return lax.ppermute(value, axes, [(i, i ^ bits) for i in range(size)])  48.9 us
    pallas_call x4, Pallas kernels, pick_matmul(): pl.pallas_call(functools.partial(pick_kernel, extra, transposed), out_sha...  44.5 us
    pallas_call x4, Pallas kernels, expert_grads(): pl.pallas_call(kernel, out_shape=jax.ShapeDtypeStruct((count,) + shape, d...  40.1 us
    pallas_call x2, Pallas kernels, expert_forward(): pl.pallas_call(functools.partial(expert_kernel, len(rows)), out_shape=out...  38.1 us
    pallas_call x2, Pallas kernels, merge_matmul(): pl.pallas_call(functools.partial(merge_kernel, count, bool(extras), trans...  38 us
  transfers between devices with their start and end apart: 83, of which 38 were waited for; matrix products, arithmetic and copies ran while one was open for 3% of the time, Pallas kernels for 50%

profile of v2, /device:TPU:0, one launch (start us, length us, event | category | flops | bytes accessed | tf_op | source)
XLA Modules:
  0.0 946.0 jit_solution(3171798528677326076)
XLA Ops:
  9.2 8.3 psum.28
  25.1 6.1 shard_map.256
  31.2 12.5 %all-gather = f32[4,1,512]{2,1,0:T(1,128)S(1)} all-gather(f32[1,1,512]{2,1,0:T(1,128)S(1)} %bitcast.66), channel_id=1, replica_groups=mesh['dp'=2,'row'=4,'col'=4] {'row'}, dimensions={0}, use_global_device_ids=true | all-gather | bytes 10240 | tf_op jit(solution)/shard_map/all_gather | solution.py:1113
  43.7 14.7 %all-gather.6.cloned.1.call-done = bf16[2048,512]{1,0:T(8,128)(2,1)} async-done(((bf16[512,512]{1,0:T(8,128)(2,1)}), bf16[2048,512]{1,0:T(8,128)(2,1)}) %all-gather.6.cloned.1.call-update) | async-done | bytes 2097168 | tf_op jit(solution)/shard_map/all_gather | solution.py:1113
  62.5 12.0 %shard_map.257 = (bf16[512,2048]{1,0:T(8,128)(2,1)}, bf16[512,1024]{1,0:T(8,128)(2,1)}, bf16[512,1024]{1,0:T(8,128)(2,1)}) custom-call(s32[2]{0:T(128)} %get-tuple-element.248.blocks_ref, s32[2048,2]{1,0:T(8,128)} %copy.67.routes_ref, bf16[2048,512]{1,0:T(8,128)(2,1)} %multiply_convert_fusion.x_ref.rows_ref, bf16[8,512,512]{2,1,0:T(8,128)(2,1)} %refs_8_.1, ...), custom_call_target="tpu_custom_call" | custom-call | flops 5120 | bytes 9 | tf_op jit(solution)/shard_map/pallas_call | solution.py:295
  85.7 12.3 %shard_map.264 = (bf16[512,2048]{1,0:T(8,128)(2,1)}, bf16[512,1024]{1,0:T(8,128)(2,1)}, bf16[512,1024]{1,0:T(8,128)(2,1)}) custom-call(s32[2]{0:T(128)} %get-tuple-element.243.blocks_ref, s32[2048,2]{1,0:T(8,128)} %copy.67.routes_ref, bf16[2048,512]{1,0:T(8,128)(2,1)} %multiply_convert_fusion.x_ref.rows_ref, bf16[8,512,512]{2,1,0:T(8,128)(2,1)} %refs_8_.1, ...), custom_call_target="tpu_custom_call" | custom-call | flops 5368709120 | bytes 9437184 | tf_op jit(solution)/shard_map/pallas_call | solution.py:295
  123.8 7.1 collective-permute-done.5
  134.7 17.4 %shard_map.265 = (bf16[4,512,512]{2,1,0:T(8,128)(2,1)}, f32[2,512,512]{2,1,0:T(8,128)}, bf16[2,512,512]{2,1,0:T(8,128)(2,1)}, f32[512,128]{1,0:T(8,128)}, f32[512,128]{1,0:T(8,128)}, /*index=5*/f32[512,128]{1,0:T(8,128)}) custom-call(f32[8,512]{1,0:T(8,128)} %add_add_fusion.logits_ref, s32[2,512]{1,0:T(2,128)} %dynamic-slice_bitcast_fusion.1.routes_ref, ...), custom_call_target="tpu_custom_call" | custom-call | flops 2048 | bytes 12 | tf_op jit(solution)/shard_map/pallas_call | solution.py:998
  157.0 10.5 %shard_map.266 = (bf16[2,640,512]{2,1,0:T(8,128)(2,1)}, bf16[2,640,512]{2,1,0:T(8,128)(2,1)}, bf16[2,640,512]{2,1,0:T(8,128)(2,1)}, bf16[2,640,512]{2,1,0:T(8,128)(2,1)}) custom-call(s32[8,16]{1,0:T(8,128)} %get-tuple-element.229.starts_ref, s32[8,2048]{1,0:T(8,128)} %get-tuple-element.167.places_ref, bf16[2048,512]{1,0:T(8,128)(2,1)} %all-gather.8.cloned.1.call-done.rows_ref), custom_call_target="tpu_custom_call" | custom-call | flops 4608 | bytes 7 | tf_op jit(solution)/shard_map/pallas_call | solution.py:581
  174.9 6.3 collective-permute-done.13.refs_14_.refs_5_
  186.7 16.9 %shard_map.269 = bf16[2048,512]{1,0:T(8,128)(2,1)} custom-call(s32[4]{0:T(128)} %copy-done.56, s32[2048,2]{1,0:T(8,128)} %copy.67.routes_ref, bf16[2,512,512]{2,1,0:T(8,128)(2,1)} %get-tuple-element.254.refs_0_, bf16[2,512,512]{2,1,0:T(8,128)(2,1)} %collective-permute-done.10.refs_1_, bf16[2,512,512]{2,1,0:T(8,128)(2,1)} %collective-permute-done.11.refs_2_, ...), custom_call_target="tpu_custom_call" | custom-call | flops 8192 | bytes 10 | tf_op jit(solution)/shard_map/pallas_call | solution.py:422
  209.8 5.7 shard_map.270
  215.5 19.7 %collective-permute-done.17.refs_0_.refs_3_ = bf16[2,640,512]{2,1,0:T(8,128)(2,1)S(1)} collective-permute-done((bf16[2,640,512]{2,1,0:T(8,128)(2,1)}, bf16[2,640,512]{2,1,0:T(8,128)(2,1)S(1)}, u32[]{:S(2)}, u32[]{:S(2)}) %collective-permute-start.17) | collective-permute-done | bytes 1310752 | tf_op jit(solution)/shard_map/ppermute | solution.py:1109
  235.2 13.2 %collective-permute-done.16.block_ref.refs_10_.refs_4_ = bf16[2,512,1408]{2,1,0:T(8,128)(2,1)} collective-permute-done((bf16[2,512,1408]{2,1,0:T(8,128)(2,1)}, bf16[2,512,1408]{2,1,0:T(8,128)(2,1)}, u32[]{:S(2)}, u32[]{:S(2)}) %collective-permute-start.16) | collective-permute-done | bytes 2883616 | tf_op jit(solution)/shard_map/ppermute | solution.py:1109
  256.1 6.9 psum.29
  267.2 6.1 shard_map.272.own_ref
  283.1 12.6 %collective-permute-done.22 = bf16[2,640,512]{2,1,0:T(8,128)(2,1)S(1)} collective-permute-done((bf16[2,640,512]{2,1,0:T(8,128)(2,1)S(1)}, bf16[2,640,512]{2,1,0:T(8,128)(2,1)S(1)}, u32[]{:S(2)}, u32[]{:S(2)}) %collective-permute-start.22) | collective-permute-done | bytes 1310752 | tf_op jit(solution)/shard_map/ppermute | solution.py:1109
  295.7 9.7 %collective-permute-done.21.sent_ref = bf16[640,1408]{1,0:T(8,128)(2,1)} collective-permute-done((bf16[640,1408]{1,0:T(8,128)(2,1)}, bf16[640,1408]{1,0:T(8,128)(2,1)}, u32[]{:S(2)}, u32[]{:S(2)}) %collective-permute-start.21) | collective-permute-done | bytes 1802272 | tf_op jit(solution)/shard_map/ppermute | solution.py:1109
  309.5 5.4 shard_map.276
  314.9 6.9 shard_map.277
  327.6 6.8 shard_map.278
  334.4 19.3 %collective-permute-done.25.block_ref.refs_2_.refs_0_ = bf16[2,640,512]{2,1,0:T(8,128)(2,1)S(1)} collective-permute-done((bf16[2,640,512]{2,1,0:T(8,128)(2,1)}, bf16[2,640,512]{2,1,0:T(8,128)(2,1)S(1)}, u32[]{:S(2)}, u32[]{:S(2)}) %collective-permute-start.25) | collective-permute-done | bytes 1310752 | tf_op jit(solution)/shard_map/ppermute | solution.py:1109
  362.4 5.7 shard_map.284.own_ref
  368.1 19.1 %shard_map.282 = (bf16[640,1408]{1,0:T(8,128)(2,1)}, bf16[640,1408]{1,0:T(8,128)(2,1)}, bf16[640,1408]{1,0:T(8,128)(2,1)}, bf16[640,128]{1,0:T(8,128)(2,1)}) custom-call(s32[1]{0:T(128)} %bitcast.9.owner_ref, s32[640,1]{1,0:T(8,128)} %convert_subtract_fusion.1.other_ref, f32[640,1408]{1,0:T(8,128)} %shard_map.272.own_ref, ...), custom_call_target="tpu_custom_call" | custom-call | flops 7040 | bytes 21 | tf_op jit(solution)/shard_map/pallas_call | solution.py:855
  387.2 9.1 shard_map.283
  396.4 10.9 %collective-permute-done.33.refs_2_.refs_1_ = bf16[640,512]{1,0:T(8,128)(2,1)S(1)} collective-permute-done((bf16[640,512]{1,0:T(8,128)(2,1)}, bf16[640,512]{1,0:T(8,128)(2,1)S(1)}, u32[]{:S(2)}, u32[]{:S(2)}) %collective-permute-start.33) | collective-permute-done | bytes 655392 | tf_op jit(solution)/shard_map/ppermute | solution.py:1109
  407.3 12.3 %collective-permute-done.34.refs_3_ = bf16[640,512]{1,0:T(8,128)(2,1)S(1)} collective-permute-done((bf16[640,512]{1,0:T(8,128)(2,1)}, bf16[640,512]{1,0:T(8,128)(2,1)S(1)}, u32[]{:S(2)}, u32[]{:S(2)}) %collective-permute-start.34) | collective-permute-done | bytes 655392 | tf_op jit(solution)/shard_map/ppermute | solution.py:1109
  420.4 18.9 %shard_map.285 = (bf16[640,1408]{1,0:T(8,128)(2,1)}, bf16[640,1408]{1,0:T(8,128)(2,1)}, bf16[640,1408]{1,0:T(8,128)(2,1)}, bf16[640,128]{1,0:T(8,128)(2,1)}) custom-call(s32[1]{0:T(128)} %bitcast.9.owner_ref, s32[640,1]{1,0:T(8,128)} %convert_subtract_fusion.other_ref, f32[640,1408]{1,0:T(8,128)} %shard_map.284.own_ref, ...), custom_call_target="tpu_custom_call" | custom-call | flops 7040 | bytes 21 | tf_op jit(solution)/shard_map/pallas_call | solution.py:855
  439.3 9.4 shard_map.289
  450.2 9.1 shard_map.286
  459.3 9.1 shard_map.287
  471.5 10.1 %collective-permute-done.40.block_ref.refs_6_ = bf16[2,640,512]{2,1,0:T(8,128)(2,1)S(1)} collective-permute-done((bf16[2,640,512]{2,1,0:T(8,128)(2,1)}, bf16[2,640,512]{2,1,0:T(8,128)(2,1)S(1)}, u32[]{:S(2)}, u32[]{:S(2)}) %collective-permute-start.40) | collective-permute-done | bytes 1310752 | tf_op jit(solution)/shard_map/ppermute | solution.py:1109
  485.9 16.3 %shard_map.288 = (bf16[4,512,1408]{2,1,0:T(8,128)(2,1)}, f32[2,8,512]{2,1,0:T(8,128)}) custom-call(bf16[2,640,512]{2,1,0:T(8,128)(2,1)} %copy-done.16, bf16[640,512]{1,0:T(8,128)(2,1)} %copy-done.29, bf16[1,640,512]{2,1,0:T(8,128)(2,1)} %collective-permute-done.26.refs_3_.refs_2_, bf16[640,512]{1,0:T(8,128)(2,1)} %copy-done.30, ...), custom_call_target="tpu_custom_call" | custom-call | flops 7360 | bytes 24 | tf_op jit(solution)/shard_map/pallas_call | solution.py:790
  502.3 5.9 collective-permute-done.37.refs_3_
  509.4 9.4 shard_map.291
  521.7 10.1 %shard_map.292 = (f32[1,512,1408]{2,1,0:T(8,128)}, f32[1,512,1408]{2,1,0:T(8,128)}, f32[1,8,512]{2,1,0:T(8,128)}) custom-call(bf16[640,512]{1,0:T(8,128)(2,1)} %get-tuple-element.210.refs_0_, bf16[640,512]{1,0:T(8,128)(2,1)} %copy-done.27, bf16[640,1408]{1,0:T(8,128)(2,1)} %get-tuple-element.212.refs_0_.refs_4_.refs_2_, ...), custom_call_target="tpu_custom_call" | custom-call | flops 3680 | bytes 12 | tf_op jit(solution)/shard_map/pallas_call | solution.py:790
  531.8 9.7 %shard_map.293 = (bf16[1,512,1408]{2,1,0:T(8,128)(2,1)}, bf16[1,512,1408]{2,1,0:T(8,128)(2,1)}, f32[1,8,512]{2,1,0:T(8,128)}) custom-call(bf16[640,512]{1,0:T(8,128)(2,1)} %copy-done.31, bf16[640,512]{1,0:T(8,128)(2,1)} %copy-done.28, bf16[640,1408]{1,0:T(8,128)(2,1)} %get-tuple-element.212.refs_0_.refs_4_.refs_2_, ...), custom_call_target="tpu_custom_call" | custom-call | flops 3680 | bytes 12 | tf_op jit(solution)/shard_map/pallas_call | solution.py:790
  541.5 20.5 %collective-permute-done.42.other_ref.refs_0_ = bf16[640,1408]{1,0:T(8,128)(2,1)} collective-permute-done((bf16[640,1408]{1,0:T(8,128)(2,1)S(1)}, bf16[640,1408]{1,0:T(8,128)(2,1)}, u32[]{:S(2)}, u32[]{:S(2)}) %collective-permute-start.42) | collective-permute-done | bytes 1802272 | tf_op jit(solution)/shard_map/ppermute | solution.py:1109
  565.8 6.4 psum.30
  575.8 5.7 shard_map.294
  581.5 33.6 %collective-permute-done.43.other_ref.refs_1_ = bf16[640,1408]{1,0:T(8,128)(2,1)S(1)} collective-permute-done((bf16[640,1408]{1,0:T(8,128)(2,1)S(1)}, bf16[640,1408]{1,0:T(8,128)(2,1)S(1)}, u32[]{:S(2)}, u32[]{:S(2)}) %collective-permute-start.43) | collective-permute-done | bytes 1802272 | tf_op jit(solution)/shard_map/ppermute | solution.py:1109
  616.3 9.0 shard_map.295
  626.8 10.1 %shard_map.296 = (bf16[512,1024]{1,0:T(8,128)(2,1)}, bf16[512,512]{1,0:T(8,128)(2,1)}, bf16[512,512]{1,0:T(8,128)(2,1)}) custom-call(s32[2]{0:T(128)} %get-tuple-element.243.blocks_ref, s32[2048,2]{1,0:T(8,128)} %copy.67.routes_ref, bf16[2048,512]{1,0:T(8,128)(2,1)} %all-gather.12.cloned.1.call-done.x_ref.rows_ref, bf16[8,512,512]{2,1,0:T(8,128)(2,1)} %w_ref.7), custom_call_target="tpu_custom_call" | custom-call | flops 4096 | bytes 7 | tf_op jit(solution)/shard_map/pallas_call | solution.py:295
  636.9 10.1 %shard_map.297 = (bf16[512,1024]{1,0:T(8,128)(2,1)}, bf16[512,512]{1,0:T(8,128)(2,1)}, bf16[512,512]{1,0:T(8,128)(2,1)}) custom-call(s32[2]{0:T(128)} %get-tuple-element.248.blocks_ref, s32[2048,2]{1,0:T(8,128)} %copy.67.routes_ref, bf16[2048,512]{1,0:T(8,128)(2,1)} %all-gather.12.cloned.1.call-done.x_ref.rows_ref, bf16[8,512,512]{2,1,0:T(8,128)(2,1)} %w_ref.7), custom_call_target="tpu_custom_call" | custom-call | flops 4096 | bytes 7 | tf_op jit(solution)/shard_map/pallas_call | solution.py:295
  658.4 21.4 %collective-permute-done.48.refs_4_.refs_5_ = bf16[512,1024]{1,0:T(8,128)(2,1)S(1)} collective-permute-done((bf16[512,1024]{1,0:T(8,128)(2,1)}, bf16[512,1024]{1,0:T(8,128)(2,1)S(1)}, u32[]{:S(2)}, u32[]{:S(2)}) %collective-permute-start.48) | collective-permute-done | bytes 1048608 | tf_op jit(solution)/shard_map/ppermute | solution.py:1109
  680.8 14.7 %shard_map.299 = (bf16[4,512,512]{2,1,0:T(8,128)(2,1)}, bf16[512,128]{1,0:T(8,128)(2,1)}) custom-call(f32[512,128]{1,0:T(8,128)} %get-tuple-element.194.side_ref, s32[512,1]{1,0:T(8,128)} %copy.64.rows_ref, s32[1,512]{1,0:T(1,128)} %columns_ref.3, f32[512,128]{1,0:T(8,128)} %get-tuple-element.195.cos_ref, f32[512,128]{1,0:T(8,128)} %get-tuple-element.196.sin_ref, ...), custom_call_target="tpu_custom_call" | custom-call | flops 5120 | bytes 20 | tf_op jit(solution)/shard_map/pallas_call | solution.py:1083
  705.3 9.4 shard_map.301.rows_ref
  716.0 5.9 shard_map.303.refs_0_.refs_2_
  721.9 6.1 shard_map.307
  730.9 9.4 shard_map.305
  740.3 5.9 shard_map.306
  747.0 5.2 collective-permute-done.57.refs_6_
  756.4 21.1 %shard_map.308 = bf16[2048,512]{1,0:T(8,128)(2,1)} custom-call(s32[4]{0:T(128)} %copy-done.56, s32[2048,2]{1,0:T(8,128)} %copy.67.routes_ref, bf16[4,512,512]{2,1,0:T(8,128)(2,1)} %get-tuple-element.252.refs_0_, bf16[4,512,512]{2,1,0:T(8,128)(2,1)} %collective-permute-done.53.refs_1_, bf16[4,512,512]{2,1,0:T(8,128)(2,1)} %collective-permute-done.54.refs_2_, ...), custom_call_target="tpu_custom_call" | custom-call | flops 10240 | bytes 14 | tf_op jit(solution)/shard_map/pallas_call | solution.py:422
  782.4 10.6 %shard_map.310.rows_ref = bf16[4,512,512]{2,1,0:T(8,128)(2,1)} custom-call(s32[5]{0:T(128)} %pad_add_fusion.1.scalars_ref, s32[2048,2]{1,0:T(8,128)} %copy.67.routes_ref, bf16[512,2048]{1,0:T(8,128)(2,1)} %bitcast.50, bf16[4,512,512]{2,1,0:T(8,128)(2,1)} %get-tuple-element.252.refs_0_, bf16[4,512,512]{2,1,0:T(8,128)(2,1)} %collective-permute-done.53.refs_1_, ...), custom_call_target="tpu_custom_call" | custom-call | flops 4096 | bytes 10 | tf_op jit(solution)/shard_map/pallas_call | solution.py:472
  805.2 10.5 %shard_map.313.own_ref = f32[4,512,512]{2,1,0:T(8,128)} custom-call(s32[5]{0:T(128)} %pad_add_fusion.3.scalars_ref, s32[2048,2]{1,0:T(8,128)} %copy.67.routes_ref, bf16[512,2048]{1,0:T(8,128)(2,1)} %bitcast.52, bf16[4,512,512]{2,1,0:T(8,128)(2,1)} %get-tuple-element.252.refs_0_, bf16[4,512,512]{2,1,0:T(8,128)(2,1)} %collective-permute-done.53.refs_1_, ...), custom_call_target="tpu_custom_call" | custom-call | flops 4096 | bytes 10 | tf_op jit(solution)/shard_map/pallas_call | solution.py:472
  826.3 6.8 shard_map.318.refs_2_
  833.1 9.6 %shard_map.316.own_ref = f32[4,512,512]{2,1,0:T(8,128)} custom-call(s32[5]{0:T(128)} %pad_add_fusion.6.scalars_ref, s32[2,2048]{1,0:T(2,128)} %bitcast.63, bf16[2048,512]{1,0:T(8,128)(2,1)} %all-gather.12.cloned.1.call-done.x_ref.rows_ref, bf16[2,512,512]{2,1,0:T(8,128)(2,1)} %get-tuple-element.255.refs_0_, bf16[2,512,512]{2,1,0:T(8,128)(2,1)} %get-tuple-element.256.refs_1_, ...), custom_call_target="tpu_custom_call" | custom-call | flops 4096 | bytes 10 | tf_op jit(solution)/shard_map/pallas_call | solution.py:472
  842.7 6.4 shard_map.317.refs_0_
  849.1 11.0 %shard_map.319 = f32[4,1408,512]{2,1,0:T(8,128)} custom-call(s32[4]{0:T(128)} %copy-done.56, f32[1,1408,512]{2,1,0:T(8,128)} %shard_map.317.refs_0_, bf16[1,1408,512]{2,1,0:T(8,128)(2,1)} %collective-permute-done.60.refs_1_, f32[1,1408,512]{2,1,0:T(8,128)} %shard_map.318.refs_2_, bf16[1,1408,512]{2,1,0:T(8,128)(2,1)} %collective-permute-done.61.refs_3_), custom_call_target="tpu_custom_call" | custom-call | bytes 19 | tf_op jit(solution)/shard_map/pallas_call | solution.py:904
  860.1 5.1 shard_map.320
  865.3 8.9 collective-permute-done.63.away_ref
  896.4 5.9 psum.31
  905.9 10.1 %shard_map.322 = f32[4,512,1408]{2,1,0:T(8,128)} custom-call(s32[4]{0:T(128)} %copy-done.56, f32[1,512,1408]{2,1,0:T(8,128)} %get-tuple-element.278.refs_0_, bf16[1,512,1408]{2,1,0:T(8,128)(2,1)} %collective-permute-done.69.refs_1_, bf16[4,512,1408]{2,1,0:T(8,128)(2,1)} %collective-permute-done.64.block_ref.refs_2_, ...), custom_call_target="tpu_custom_call" | custom-call | bytes 19 | tf_op jit(solution)/shard_map/pallas_call | solution.py:904
  923.5 10.1 %shard_map.325 = f32[4,512,1408]{2,1,0:T(8,128)} custom-call(s32[4]{0:T(128)} %copy-done.56, f32[1,512,1408]{2,1,0:T(8,128)} %get-tuple-element.282.refs_0_, bf16[1,512,1408]{2,1,0:T(8,128)(2,1)} %collective-permute-done.74.refs_1_, bf16[4,512,1408]{2,1,0:T(8,128)(2,1)} %collective-permute-done.64.block_ref.refs_2_, ...), custom_call_target="tpu_custom_call" | custom-call | bytes 19 | tf_op jit(solution)/shard_map/pallas_call | solution.py:904
  (409 shorter events, 237.0 us)
Async XLA Ops:
  7.2 51.2 %all-gather.6.cloned.1.call-start = ((), (), s32[]{:S(2)}) async-start(), calls=%async_computation.4 | async-start | bytes 2621440 | tf_op jit(solution)/shard_map/all_gather | solution.py:1113
  7.9 149.1 %all-gather.8.cloned.1.call-start = ((), (), s32[]{:S(2)}) async-start(), calls=%async_computation.5 | async-start | bytes 2621440 | tf_op jit(solution)/shard_map/all_gather | solution.py:1113
  22.6 63.1 %collective-permute-start.6 = (bf16[2,512,1408]{2,1,0:T(8,128)(2,1)}, bf16[2,512,1408]{2,1,0:T(8,128)(2,1)S(1)}, u32[]{:S(2)}, u32[]{:S(2)}) collective-permute-start(bf16[2,512,1408]{2,1,0:T(8,128)(2,1)} %shard_map.263), channel_id=1, source_target_pairs={{0,2},{1,3},{2,0},{3,1},{4,6},{5,7},{6,4},{7,5},{8,10},{9,11},{10,... | collective-permute-start | bytes 8650760 | tf_op jit(solution)/shard_map/ppermute | solution.py:1109
  75.1 179.3 %reduce-scatter.5.cloned.1.call-start = ((), (), s32[]{:S(2)}) async-start(), calls=%async_computation.6 | async-start | bytes 2621440 | tf_op jit(solution)/shard_map/reduce_scatter | solution.py:1117
  83.4 50.0 %collective-permute-start.9 = (bf16[512,2048]{1,0:T(8,128)(2,1)}, bf16[512,2048]{1,0:T(8,128)(2,1)}, u32[]{:S(2)}, u32[]{:S(2)}) collective-permute-start(bf16[512,2048]{1,0:T(8,128)(2,1)} %shard_map.258), channel_id=1, source_target_pairs={{0,2},{1,3},{2,0},{3,1},{4,6},{5,7},{6,4},{7,5},{8,10},{9,11},{10,... | collective-permute-start | bytes 6291464 | tf_op jit(solution)/shard_map/ppermute | solution.py:1109
  98.0 35.3 %collective-permute-start.7 = (bf16[512,1024]{1,0:T(8,128)(2,1)}, bf16[512,1024]{1,0:T(8,128)(2,1)S(1)}, u32[]{:S(2)}, u32[]{:S(2)}) collective-permute-start(bf16[512,1024]{1,0:T(8,128)(2,1)} %get-tuple-element.178), channel_id=1, source_target_pairs={{0,1},{1,0},{2,3},{3,2},{4,5},{5,4},{6,7},{7,6},{8,9},{9,8},{10,11... | collective-permute-start | bytes 3145736 | tf_op jit(solution)/shard_map/ppermute | solution.py:1109
  98.1 35.3 %collective-permute-start.8 = (bf16[512,1024]{1,0:T(8,128)(2,1)}, bf16[512,1024]{1,0:T(8,128)(2,1)S(1)}, u32[]{:S(2)}, u32[]{:S(2)}) collective-permute-start(bf16[512,1024]{1,0:T(8,128)(2,1)} %get-tuple-element.179), channel_id=1, source_target_pairs={{0,1},{1,0},{2,3},{3,2},{4,5},{5,4},{6,7},{7,6},{8,9},{9,8},{10,11... | collective-permute-start | bytes 3145736 | tf_op jit(solution)/shard_map/ppermute | solution.py:1109
  108.8 12.5 %collective-permute-start.2 = (bf16[640,8]{1,0:T(8,128)(2,1)}, bf16[640,8]{1,0:T(8,128)(2,1)S(1)}, u32[]{:S(2)}, u32[]{:S(2)}) collective-permute-start(bf16[640,8]{1,0:T(8,128)(2,1)} %bitcast.77), channel_id=1, source_target_pairs={{0,16},{1,17},{2,18},{3,19},{16,0},{17,1},{18,2},{19,3},{4,20},{5,... | collective-permute-start | bytes 30728 | tf_op jit(solution)/shard_map/ppermute | solution.py:1109
  122.1 8.7 collective-permute-start.5
  123.1 9.6 %collective-permute-start.4 = (f32[8,512]{1,0:T(8,128)S(1)}, f32[8,512]{1,0:T(8,128)S(1)}, u32[]{:S(2)}, u32[]{:S(2)}) collective-permute-start(f32[8,512]{1,0:T(8,128)S(1)} %copy-done.80), channel_id=1, source_target_pairs={{0,2},{1,3},{2,0},{3,1},{4,6},{5,7},{6,4},{7,5},{8,10},{9,11},{10,... | collective-permute-start | bytes 49160 | tf_op jit(solution)/shard_map/ppermute | solution.py:1109
  152.1 30.7 %collective-permute-start.11 = (bf16[2,512,512]{2,1,0:T(8,128)(2,1)}, bf16[2,512,512]{2,1,0:T(8,128)(2,1)}, u32[]{:S(2)}, u32[]{:S(2)}) collective-permute-start(bf16[2,512,512]{2,1,0:T(8,128)(2,1)} %get-tuple-element.254.refs_0_), channel_id=1, source_target_pairs={{0,2},{1,3},{2,0},{3,1},{4,6},{5,7},{6,4},{7,5},{8,10},{9,11},{10,... | collective-permute-start | bytes 3145736 | tf_op jit(solution)/shard_map/ppermute | solution.py:1109
  153.8 21.1 %collective-permute-start.12 = (bf16[512,128]{1,0:T(8,128)(2,1)S(1)}, bf16[512,128]{1,0:T(8,128)(2,1)S(1)}, u32[]{:S(2)}, u32[]{:S(2)}) collective-permute-start(bf16[512,128]{1,0:T(8,128)(2,1)S(1)} %pad.8.refs_12_.refs_5_.refs_8_), channel_id=1, source_target_pairs={{0,1},{1,0},{2,3},{3,2},{4,5},{5,4},{6,7},{7,6},{8,9},{9,8},{10,11... | collective-permute-start | bytes 393224 | tf_op jit(solution)/shard_map/ppermute | solution.py:1109
  153.9 27.2 %collective-permute-start.13 = (bf16[512,128]{1,0:T(8,128)(2,1)S(1)}, bf16[512,128]{1,0:T(8,128)(2,1)S(1)}, u32[]{:S(2)}, u32[]{:S(2)}) collective-permute-start(bf16[512,128]{1,0:T(8,128)(2,1)S(1)} %pad.8.refs_12_.refs_5_.refs_8_), channel_id=1, source_target_pairs={{0,2},{1,3},{2,0},{3,1},{4,6},{5,7},{6,4},{7,5},{8,10},{9,11},{10,... | collective-permute-start | bytes 393224 | tf_op jit(solution)/shard_map/ppermute | solution.py:1109
  154.5 28.2 %collective-permute-start.14 = (bf16[512,128]{1,0:T(8,128)(2,1)S(1)}, bf16[512,128]{1,0:T(8,128)(2,1)S(1)}, u32[]{:S(2)}, u32[]{:S(2)}) collective-permute-start(bf16[512,128]{1,0:T(8,128)(2,1)S(1)} %pad.8.refs_12_.refs_5_.refs_8_), channel_id=1, source_target_pairs={{0,3},{1,2},{2,1},{3,0},{4,7},{5,6},{6,5},{7,4},{8,11},{9,10},{10,... | collective-permute-start | bytes 393224 | tf_op jit(solution)/shard_map/ppermute | solution.py:1109
  155.8 29.0 %collective-permute-start.10 = (bf16[2,512,512]{2,1,0:T(8,128)(2,1)}, bf16[2,512,512]{2,1,0:T(8,128)(2,1)}, u32[]{:S(2)}, u32[]{:S(2)}) collective-permute-start(bf16[2,512,512]{2,1,0:T(8,128)(2,1)} %get-tuple-element.254.refs_0_), channel_id=1, source_target_pairs={{0,1},{1,0},{2,3},{3,2},{4,5},{5,4},{6,7},{7,6},{8,9},{9,8},{10,11... | collective-permute-start | bytes 3145736 | tf_op jit(solution)/shard_map/ppermute | solution.py:1109
  183.2 23.9 %collective-permute-start.19 = (bf16[2,1408,512]{2,1,0:T(8,128)(2,1)}, bf16[2,1408,512]{2,1,0:T(8,128)(2,1)S(1)}, u32[]{:S(2)}, u32[]{:S(2)}) collective-permute-start(bf16[2,1408,512]{2,1,0:T(8,128)(2,1)} %shard_map.268), channel_id=1, source_target_pairs={{0,1},{1,0},{2,3},{3,2},{4,5},{5,4},{6,7},{7,6},{8,9},{9,8},{10,11... | collective-permute-start | bytes 8650760 | tf_op jit(solution)/shard_map/ppermute | solution.py:1109
  183.3 65.1 %collective-permute-start.16 = (bf16[2,512,1408]{2,1,0:T(8,128)(2,1)}, bf16[2,512,1408]{2,1,0:T(8,128)(2,1)}, u32[]{:S(2)}, u32[]{:S(2)}) collective-permute-start(bf16[2,512,1408]{2,1,0:T(8,128)(2,1)} %shard_map.260), channel_id=1, source_target_pairs={{0,2},{1,3},{2,0},{3,1},{4,6},{5,7},{6,4},{7,5},{8,10},{9,11},{10,... | collective-permute-start | bytes 8650760 | tf_op jit(solution)/shard_map/ppermute | solution.py:1109
  203.7 111.2 %all-gather.10.cloned.1.call-start = ((), (), s32[]{:S(2)}) async-start(), calls=%async_computation.7 | async-start | bytes 2621440 | tf_op jit(solution)/shard_map/all_gather | solution.py:1113
  204.2 31.0 %collective-permute-start.17 = (bf16[2,640,512]{2,1,0:T(8,128)(2,1)}, bf16[2,640,512]{2,1,0:T(8,128)(2,1)S(1)}, u32[]{:S(2)}, u32[]{:S(2)}) collective-permute-start(bf16[2,640,512]{2,1,0:T(8,128)(2,1)} %get-tuple-element.189), channel_id=1, source_target_pairs={{0,16},{1,17},{2,18},{3,19},{16,0},{17,1},{18,2},{19,3},{4,20},{5,... | collective-permute-start | bytes 3932168 | tf_op jit(solution)/shard_map/ppermute | solution.py:1109
  265.0 298.5 %reduce-scatter.7.cloned.1.call-start = ((), (), s32[]{:S(2)}) async-start(), calls=%async_computation.8 | async-start | bytes 2621440 | tf_op jit(solution)/shard_map/reduce_scatter | solution.py:1117
  265.1 40.3 %collective-permute-start.21 = (bf16[640,1408]{1,0:T(8,128)(2,1)}, bf16[640,1408]{1,0:T(8,128)(2,1)}, u32[]{:S(2)}, u32[]{:S(2)}) collective-permute-start(bf16[640,1408]{1,0:T(8,128)(2,1)} %shard_map.270), channel_id=1, source_target_pairs={{0,2},{1,3},{2,0},{3,1},{4,6},{5,7},{6,4},{7,5},{8,10},{9,11},{10,... | collective-permute-start | bytes 5406728 | tf_op jit(solution)/shard_map/ppermute | solution.py:1109
  265.7 30.0 %collective-permute-start.22 = (bf16[2,640,512]{2,1,0:T(8,128)(2,1)S(1)}, bf16[2,640,512]{2,1,0:T(8,128)(2,1)S(1)}, u32[]{:S(2)}, u32[]{:S(2)}) collective-permute-start(bf16[2,640,512]{2,1,0:T(8,128)(2,1)S(1)} %copy-done.76), channel_id=1, source_target_pairs={{0,16},{1,17},{2,18},{3,19},{16,0},{17,1},{18,2},{19,3},{4,20},{5,... | collective-permute-start | bytes 3932168 | tf_op jit(solution)/shard_map/ppermute | solution.py:1109
  307.9 48.8 %collective-permute-start.28 = (bf16[1,512,1408]{2,1,0:T(8,128)(2,1)}, bf16[1,512,1408]{2,1,0:T(8,128)(2,1)S(1)}, u32[]{:S(2)}, u32[]{:S(2)}) collective-permute-start(bf16[1,512,1408]{2,1,0:T(8,128)(2,1)} %shard_map.281), channel_id=1, source_target_pairs={{0,1},{1,0},{2,3},{3,2},{4,5},{5,4},{6,7},{7,6},{8,9},{9,8},{10,11... | collective-permute-start | bytes 4325384 | tf_op jit(solution)/shard_map/ppermute | solution.py:1109
  321.8 31.8 %collective-permute-start.25 = (bf16[2,640,512]{2,1,0:T(8,128)(2,1)}, bf16[2,640,512]{2,1,0:T(8,128)(2,1)S(1)}, u32[]{:S(2)}, u32[]{:S(2)}) collective-permute-start(bf16[2,640,512]{2,1,0:T(8,128)(2,1)} %get-tuple-element.206), channel_id=1, source_target_pairs={{0,2},{1,3},{2,0},{3,1},{16,18},{17,19},{18,16},{19,17},{4,6},{5,7... | collective-permute-start | bytes 3932168 | tf_op jit(solution)/shard_map/ppermute | solution.py:1109
  326.5 30.3 %collective-permute-start.27 = (bf16[1,512,1408]{2,1,0:T(8,128)(2,1)}, bf16[1,512,1408]{2,1,0:T(8,128)(2,1)S(1)}, u32[]{:S(2)}, u32[]{:S(2)}) collective-permute-start(bf16[1,512,1408]{2,1,0:T(8,128)(2,1)} %shard_map.280), channel_id=1, source_target_pairs={{0,1},{1,0},{2,3},{3,2},{4,5},{5,4},{6,7},{7,6},{8,9},{9,8},{10,11... | collective-permute-start | bytes 4325384 | tf_op jit(solution)/shard_map/ppermute | solution.py:1109
  326.5 32.7 %collective-permute-start.29 = (bf16[1,512,1408]{2,1,0:T(8,128)(2,1)}, bf16[1,512,1408]{2,1,0:T(8,128)(2,1)S(1)}, u32[]{:S(2)}, u32[]{:S(2)}) collective-permute-start(bf16[1,512,1408]{2,1,0:T(8,128)(2,1)} %shard_map.275), channel_id=1, source_target_pairs={{0,1},{1,0},{2,3},{3,2},{4,5},{5,4},{6,7},{7,6},{8,9},{9,8},{10,11... | collective-permute-start | bytes 4325384 | tf_op jit(solution)/shard_map/ppermute | solution.py:1109
  327.0 92.5 %collective-permute-start.30 = (bf16[640,1408]{1,0:T(8,128)(2,1)}, bf16[640,1408]{1,0:T(8,128)(2,1)}, u32[]{:S(2)}, u32[]{:S(2)}) collective-permute-start(bf16[640,1408]{1,0:T(8,128)(2,1)} %shard_map.276), channel_id=1, source_target_pairs={{0,2},{1,3},{2,0},{3,1},{4,6},{5,7},{6,4},{7,5},{8,10},{9,11},{10,... | collective-permute-start | bytes 5406728 | tf_op jit(solution)/shard_map/ppermute | solution.py:1109
  353.7 6.2 collective-permute-start.24
  356.8 50.5 %collective-permute-start.33 = (bf16[640,512]{1,0:T(8,128)(2,1)}, bf16[640,512]{1,0:T(8,128)(2,1)S(1)}, u32[]{:S(2)}, u32[]{:S(2)}) collective-permute-start(bf16[640,512]{1,0:T(8,128)(2,1)} %get-tuple-element.207), channel_id=1, source_target_pairs={{0,18},{1,19},{2,16},{3,17},{16,2},{17,3},{18,0},{19,1},{4,22},{5,... | collective-permute-start | bytes 1966088 | tf_op jit(solution)/shard_map/ppermute | solution.py:1109
  359.2 37.1 %collective-permute-start.31 = (bf16[640,512]{1,0:T(8,128)(2,1)}, bf16[640,512]{1,0:T(8,128)(2,1)S(1)}, u32[]{:S(2)}, u32[]{:S(2)}) collective-permute-start(bf16[640,512]{1,0:T(8,128)(2,1)} %get-tuple-element.217), channel_id=1, source_target_pairs={{0,16},{1,17},{2,18},{3,19},{16,0},{17,1},{18,2},{19,3},{4,20},{5,... | collective-permute-start | bytes 1966088 | tf_op jit(solution)/shard_map/ppermute | solution.py:1109
  360.7 35.7 %collective-permute-start.32 = (bf16[640,512]{1,0:T(8,128)(2,1)}, bf16[640,512]{1,0:T(8,128)(2,1)S(1)}, u32[]{:S(2)}, u32[]{:S(2)}) collective-permute-start(bf16[640,512]{1,0:T(8,128)(2,1)} %get-tuple-element.219), channel_id=1, source_target_pairs={{0,17},{1,16},{2,19},{3,18},{16,1},{17,0},{18,3},{19,2},{4,21},{5,... | collective-permute-start | bytes 1966088 | tf_op jit(solution)/shard_map/ppermute | solution.py:1109
  361.6 57.9 %collective-permute-start.34 = (bf16[640,512]{1,0:T(8,128)(2,1)}, bf16[640,512]{1,0:T(8,128)(2,1)S(1)}, u32[]{:S(2)}, u32[]{:S(2)}) collective-permute-start(bf16[640,512]{1,0:T(8,128)(2,1)} %get-tuple-element.208), channel_id=1, source_target_pairs={{0,19},{1,18},{2,17},{3,16},{16,3},{17,2},{18,1},{19,0},{4,23},{5,... | collective-permute-start | bytes 1966088 | tf_op jit(solution)/shard_map/ppermute | solution.py:1109
  448.8 32.8 %collective-permute-start.40 = (bf16[2,640,512]{2,1,0:T(8,128)(2,1)}, bf16[2,640,512]{2,1,0:T(8,128)(2,1)S(1)}, u32[]{:S(2)}, u32[]{:S(2)}) collective-permute-start(bf16[2,640,512]{2,1,0:T(8,128)(2,1)} %shard_map.289), channel_id=1, source_target_pairs={{0,18},{1,19},{2,16},{3,17},{16,2},{17,3},{18,0},{19,1},{4,22},{5,... | collective-permute-start | bytes 3932168 | tf_op jit(solution)/shard_map/ppermute | solution.py:1109
  468.4 16.2 %collective-permute-start.35 = (bf16[640,512]{1,0:T(8,128)(2,1)}, bf16[640,512]{1,0:T(8,128)(2,1)S(1)}, u32[]{:S(2)}, u32[]{:S(2)}) collective-permute-start(bf16[640,512]{1,0:T(8,128)(2,1)} %get-tuple-element.226), channel_id=1, source_target_pairs={{0,1},{1,0},{2,3},{3,2},{16,17},{17,16},{18,19},{19,18},{4,5},{5,4... | collective-permute-start | bytes 1966088 | tf_op jit(solution)/shard_map/ppermute | solution.py:1109
  468.9 33.4 %collective-permute-start.36 = (bf16[640,512]{1,0:T(8,128)(2,1)}, bf16[640,512]{1,0:T(8,128)(2,1)S(1)}, u32[]{:S(2)}, u32[]{:S(2)}) collective-permute-start(bf16[640,512]{1,0:T(8,128)(2,1)} %get-tuple-element.215), channel_id=1, source_target_pairs={{0,2},{1,3},{2,0},{3,1},{16,18},{17,19},{18,16},{19,17},{4,6},{5,7... | collective-permute-start | bytes 1966088 | tf_op jit(solution)/shard_map/ppermute | solution.py:1109
  469.4 38.8 %collective-permute-start.38 = (bf16[640,512]{1,0:T(8,128)(2,1)}, bf16[640,512]{1,0:T(8,128)(2,1)S(1)}, u32[]{:S(2)}, u32[]{:S(2)}) collective-permute-start(bf16[640,512]{1,0:T(8,128)(2,1)} %get-tuple-element.224), channel_id=1, source_target_pairs={{0,16},{1,17},{2,18},{3,19},{16,0},{17,1},{18,2},{19,3},{4,20},{5,... | collective-permute-start | bytes 1966088 | tf_op jit(solution)/shard_map/ppermute | solution.py:1109
  470.9 37.3 %collective-permute-start.37 = (bf16[640,512]{1,0:T(8,128)(2,1)}, bf16[640,512]{1,0:T(8,128)(2,1)S(1)}, u32[]{:S(2)}, u32[]{:S(2)}) collective-permute-start(bf16[640,512]{1,0:T(8,128)(2,1)} %get-tuple-element.231), channel_id=1, source_target_pairs={{0,3},{1,2},{2,1},{3,0},{16,19},{17,18},{18,17},{19,16},{4,7},{5,6... | collective-permute-start | bytes 1966088 | tf_op jit(solution)/shard_map/ppermute | solution.py:1109
  481.6 27.8 %collective-permute-start.39 = (bf16[640,512]{1,0:T(8,128)(2,1)}, bf16[640,512]{1,0:T(8,128)(2,1)}, u32[]{:S(2)}, u32[]{:S(2)}) collective-permute-start(bf16[640,512]{1,0:T(8,128)(2,1)} %get-tuple-element.232), channel_id=1, source_target_pairs={{0,17},{1,16},{2,19},{3,18},{16,1},{17,0},{18,3},{19,2},{4,21},{5,... | collective-permute-start | bytes 1966088 | tf_op jit(solution)/shard_map/ppermute | solution.py:1109
  484.6 24.8 %collective-permute-start.41 = (bf16[1,640,512]{2,1,0:T(8,128)(2,1)}, bf16[1,640,512]{2,1,0:T(8,128)(2,1)}, u32[]{:S(2)}, u32[]{:S(2)}) collective-permute-start(bf16[1,640,512]{2,1,0:T(8,128)(2,1)} %shard_map.290), channel_id=1, source_target_pairs={{0,1},{1,0},{2,3},{3,2},{4,5},{5,4},{6,7},{7,6},{8,9},{9,8},{10,11... | collective-permute-start | bytes 1966088 | tf_op jit(solution)/shard_map/ppermute | solution.py:1109
  518.8 108.0 %all-gather.12.cloned.1.call-start = ((), (), s32[]{:S(2)}) async-start(), calls=%async_computation.9 | async-start | bytes 2621440 | tf_op jit(solution)/shard_map/all_gather | solution.py:1113
  520.3 41.7 %collective-permute-start.42 = (bf16[640,1408]{1,0:T(8,128)(2,1)S(1)}, bf16[640,1408]{1,0:T(8,128)(2,1)}, u32[]{:S(2)}, u32[]{:S(2)}) collective-permute-start(bf16[640,1408]{1,0:T(8,128)(2,1)S(1)} %copy-done.5), channel_id=1, source_target_pairs={{0,2},{1,3},{2,0},{3,1},{4,6},{5,7},{6,4},{7,5},{8,10},{9,11},{10,... | collective-permute-start | bytes 5406728 | tf_op jit(solution)/shard_map/ppermute | solution.py:1109
  574.5 308.8 %reduce-scatter.11.cloned.1.call-start = ((), (), s32[]{:S(2)}) async-start(), calls=%async_computation.11 | async-start | bytes 2621440 | tf_op jit(solution)/shard_map/reduce_scatter | solution.py:1117
  574.7 40.4 %collective-permute-start.43 = (bf16[640,1408]{1,0:T(8,128)(2,1)S(1)}, bf16[640,1408]{1,0:T(8,128)(2,1)S(1)}, u32[]{:S(2)}, u32[]{:S(2)}) collective-permute-start(bf16[640,1408]{1,0:T(8,128)(2,1)S(1)} %copy-done.13), channel_id=1, source_target_pairs={{0,2},{1,3},{2,0},{3,1},{4,6},{5,7},{6,4},{7,5},{8,10},{9,11},{10,... | collective-permute-start | bytes 5406728 | tf_op jit(solution)/shard_map/ppermute | solution.py:1109
  625.3 72.2 %collective-permute-start.51 = (bf16[4,640,512]{2,1,0:T(8,128)(2,1)}, bf16[4,640,512]{2,1,0:T(8,128)(2,1)}, u32[]{:S(2)}, u32[]{:S(2)}) collective-permute-start(bf16[4,640,512]{2,1,0:T(8,128)(2,1)} %shard_map.295), channel_id=1, source_target_pairs={{0,16},{1,17},{2,18},{3,19},{16,0},{17,1},{18,2},{19,3},{4,20},{5,... | collective-permute-start | bytes 7864328 | tf_op jit(solution)/shard_map/ppermute | solution.py:1109
  654.4 25.4 %collective-permute-start.48 = (bf16[512,1024]{1,0:T(8,128)(2,1)}, bf16[512,1024]{1,0:T(8,128)(2,1)S(1)}, u32[]{:S(2)}, u32[]{:S(2)}) collective-permute-start(bf16[512,1024]{1,0:T(8,128)(2,1)} %shard_map.298), channel_id=1, source_target_pairs={{0,2},{1,3},{2,0},{3,1},{4,6},{5,7},{6,4},{7,5},{8,10},{9,11},{10,... | collective-permute-start | bytes 3145736 | tf_op jit(solution)/shard_map/ppermute | solution.py:1109
  695.5 50.8 %collective-permute-start.54 = (bf16[4,512,512]{2,1,0:T(8,128)(2,1)}, bf16[4,512,512]{2,1,0:T(8,128)(2,1)}, u32[]{:S(2)}, u32[]{:S(2)}) collective-permute-start(bf16[4,512,512]{2,1,0:T(8,128)(2,1)} %get-tuple-element.252.refs_0_), channel_id=1, source_target_pairs={{0,2},{1,3},{2,0},{3,1},{4,6},{5,7},{6,4},{7,5},{8,10},{9,11},{10,... | collective-permute-start | bytes 6291464 | tf_op jit(solution)/shard_map/ppermute | solution.py:1109
  696.9 34.0 %collective-permute-start.50 = (bf16[2,640,512]{2,1,0:T(8,128)(2,1)}, bf16[2,640,512]{2,1,0:T(8,128)(2,1)}, u32[]{:S(2)}, u32[]{:S(2)}) collective-permute-start(bf16[2,640,512]{2,1,0:T(8,128)(2,1)} %shard_map.294), channel_id=1, source_target_pairs={{0,1},{1,0},{2,3},{3,2},{4,5},{5,4},{6,7},{7,6},{8,9},{9,8},{10,11... | collective-permute-start | bytes 3932168 | tf_op jit(solution)/shard_map/ppermute | solution.py:1109
  700.3 30.6 %collective-permute-start.52 = (bf16[2,640,512]{2,1,0:T(8,128)(2,1)}, bf16[2,640,512]{2,1,0:T(8,128)(2,1)}, u32[]{:S(2)}, u32[]{:S(2)}) collective-permute-start(bf16[2,640,512]{2,1,0:T(8,128)(2,1)} %shard_map.304), channel_id=1, source_target_pairs={{0,1},{1,0},{2,3},{3,2},{4,5},{5,4},{6,7},{7,6},{8,9},{9,8},{10,11... | collective-permute-start | bytes 3932168 | tf_op jit(solution)/shard_map/ppermute | solution.py:1109
  715.9 12.5 %collective-permute-start.49 = (bf16[16,128]{1,0:T(8,128)(2,1)}, bf16[16,128]{1,0:T(8,128)(2,1)S(1)}, u32[]{:S(2)}, u32[]{:S(2)}) collective-permute-start(bf16[16,128]{1,0:T(8,128)(2,1)} %shard_map.302), channel_id=1, source_target_pairs={{0,1},{1,0},{2,3},{3,2},{4,5},{5,4},{6,7},{7,6},{8,9},{9,8},{10,11... | collective-permute-start | bytes 12296 | tf_op jit(solution)/shard_map/ppermute | solution.py:1109
  728.0 26.4 %collective-permute-start.53 = (bf16[4,512,512]{2,1,0:T(8,128)(2,1)S(1)}, bf16[4,512,512]{2,1,0:T(8,128)(2,1)}, u32[]{:S(2)}, u32[]{:S(2)}) collective-permute-start(bf16[4,512,512]{2,1,0:T(8,128)(2,1)S(1)} %copy-done.2), channel_id=1, source_target_pairs={{0,1},{1,0},{2,3},{3,2},{4,5},{5,4},{6,7},{7,6},{8,9},{9,8},{10,11... | collective-permute-start | bytes 6291464 | tf_op jit(solution)/shard_map/ppermute | solution.py:1109
  746.3 8.1 collective-permute-start.55
  746.3 5.9 collective-permute-start.57
  752.2 126.1 %collective-permute-start.64 = (bf16[4,512,1408]{2,1,0:T(8,128)(2,1)}, bf16[4,512,1408]{2,1,0:T(8,128)(2,1)}, u32[]{:S(2)}, u32[]{:S(2)}) collective-permute-start(bf16[4,512,1408]{2,1,0:T(8,128)(2,1)} %get-tuple-element.275), channel_id=1, source_target_pairs={{0,2},{1,3},{2,0},{3,1},{4,6},{5,7},{6,4},{7,5},{8,10},{9,11},{10,... | collective-permute-start | bytes 17301512 | tf_op jit(solution)/shard_map/ppermute | solution.py:1109
  777.5 125.6 %reduce-scatter.9.cloned.1.call-start = ((), (), s32[]{:S(2)}) async-start(), calls=%async_computation.10 | async-start | bytes 2621440 | tf_op jit(solution)/shard_map/reduce_scatter | solution.py:1117
  781.3 78.9 %collective-permute-start.62 = (bf16[4,512,512]{2,1,0:T(8,128)(2,1)S(1)}, bf16[4,512,512]{2,1,0:T(8,128)(2,1)}, u32[]{:S(2)}, u32[]{:S(2)}) collective-permute-start(bf16[4,512,512]{2,1,0:T(8,128)(2,1)S(1)} %copy-done.17), channel_id=1, source_target_pairs={{0,16},{16,0},{1,17},{17,1},{2,18},{18,2},{3,19},{19,3},{4,20},{20... | collective-permute-start | bytes 6291464 | tf_op jit(solution)/shard_map/ppermute | solution.py:1109
  793.0 81.2 %collective-permute-start.63 = (bf16[4,512,512]{2,1,0:T(8,128)(2,1)}, bf16[4,512,512]{2,1,0:T(8,128)(2,1)}, u32[]{:S(2)}, u32[]{:S(2)}) collective-permute-start(bf16[4,512,512]{2,1,0:T(8,128)(2,1)} %shard_map.310.rows_ref), channel_id=1, source_target_pairs={{0,16},{16,0},{1,17},{17,1},{2,18},{18,2},{3,19},{19,3},{4,20},{20... | collective-permute-start | bytes 6291464 | tf_op jit(solution)/shard_map/ppermute | solution.py:1109
  795.8 53.3 %collective-permute-start.61 = (bf16[1,1408,512]{2,1,0:T(8,128)(2,1)}, bf16[1,1408,512]{2,1,0:T(8,128)(2,1)}, u32[]{:S(2)}, u32[]{:S(2)}) collective-permute-start(bf16[1,1408,512]{2,1,0:T(8,128)(2,1)} %shard_map.307), channel_id=1, source_target_pairs={{0,1},{1,0},{2,3},{3,2},{4,5},{5,4},{6,7},{7,6},{8,9},{9,8},{10,11... | collective-permute-start | bytes 4325384 | tf_op jit(solution)/shard_map/ppermute | solution.py:1109
  797.1 51.9 %collective-permute-start.60 = (bf16[1,1408,512]{2,1,0:T(8,128)(2,1)}, bf16[1,1408,512]{2,1,0:T(8,128)(2,1)}, u32[]{:S(2)}, u32[]{:S(2)}) collective-permute-start(bf16[1,1408,512]{2,1,0:T(8,128)(2,1)} %shard_map.306), channel_id=1, source_target_pairs={{0,1},{1,0},{2,3},{3,2},{4,5},{5,4},{6,7},{7,6},{8,9},{9,8},{10,11... | collective-permute-start | bytes 4325384 | tf_op jit(solution)/shard_map/ppermute | solution.py:1109
  882.1 5.6 collective-permute-start.65
  882.1 23.8 %collective-permute-start.69 = (bf16[1,512,1408]{2,1,0:T(8,128)(2,1)}, bf16[1,512,1408]{2,1,0:T(8,128)(2,1)}, u32[]{:S(2)}, u32[]{:S(2)}) collective-permute-start(bf16[1,512,1408]{2,1,0:T(8,128)(2,1)} %get-tuple-element.279), channel_id=1, source_target_pairs={{0,1},{1,0},{2,3},{3,2},{4,5},{5,4},{6,7},{7,6},{8,9},{9,8},{10,11... | collective-permute-start | bytes 4325384 | tf_op jit(solution)/shard_map/ppermute | solution.py:1109
  882.6 40.9 %collective-permute-start.74 = (bf16[1,512,1408]{2,1,0:T(8,128)(2,1)}, bf16[1,512,1408]{2,1,0:T(8,128)(2,1)}, u32[]{:S(2)}, u32[]{:S(2)}) collective-permute-start(bf16[1,512,1408]{2,1,0:T(8,128)(2,1)} %get-tuple-element.283), channel_id=1, source_target_pairs={{0,1},{1,0},{2,3},{3,2},{4,5},{5,4},{6,7},{7,6},{8,9},{9,8},{10,11... | collective-permute-start | bytes 4325384 | tf_op jit(solution)/shard_map/ppermute | solution.py:1109
  882.7 38.4 %collective-permute-start.70 = (bf16[1,512,512]{2,1,0:T(8,128)(2,1)S(1)}, bf16[1,512,512]{2,1,0:T(8,128)(2,1)}, u32[]{:S(2)}, u32[]{:S(2)}) collective-permute-start(bf16[1,512,512]{2,1,0:T(8,128)(2,1)S(1)} %copy-done.45), channel_id=1, source_target_pairs={{0,16},{16,0},{1,17},{17,1},{2,18},{18,2},{3,19},{19,3},{4,20},{20... | collective-permute-start | bytes 1572872 | tf_op jit(solution)/shard_map/ppermute | solution.py:1109
  894.6 7.7 collective-permute-start.67
  902.4 31.2 %collective-permute-start.68 = (f32[42,512]{1,0:T(8,128)S(1)}, f32[42,512]{1,0:T(8,128)S(1)}, u32[]{:S(2)}, u32[]{:S(2)}) collective-permute-start(f32[42,512]{1,0:T(8,128)S(1)} %add.109), channel_id=1, source_target_pairs={{0,16},{16,0},{1,17},{17,1},{2,18},{18,2},{3,19},{19,3},{4,20},{20... | collective-permute-start | bytes 258056 | tf_op jit(solution)/shard_map/ppermute | solution.py:1109
  (101 other events, 1033.3 us)
Sparse Core Ops, SparseCore 0:
  9.6 48.7 all-gather.5
  75.2 44.7 all-gather.7
  203.8 44.7 reduce-scatter.4
  265.1 45.8 all-gather.9
  518.9 44.5 reduce-scatter.6
  574.6 44.7 all-gather.11
  777.6 42.2 reduce-scatter.10
  822.3 43.1 reduce-scatter.8

commit v3 on v2

--- a/solution.py
+++ b/solution.py
@@ -745,8 +745,6 @@
 def turned_kernel(pairs, rights, lead, merged, *refs):
     contract = (((0,), (0,)), ((), ()))
     outs = list(refs[2 * pairs + 2 * rights :])
-    if merged:
-        outs.insert(0, outs[0])
     operands = [ref[0] if flag else ref[...] for ref, flag in zip(refs, lead)]
     for pair in range(pairs):
         for place, o_ref in enumerate(outs):
@@ -760,7 +758,7 @@
                 total = product if total is None else total + product
             lead = pair
             if merged and place == 1:
-                lead += pairs
+                o_ref, lead = (outs[0], pairs) if pair else (o_ref, 0)
             o_ref[lead] = total[: o_ref.shape[1]].astype(o_ref.dtype)
 
 
@@ -783,10 +781,9 @@
         width = shapes[2 * pairs + 2 * place][1]
         flops += 4 * pairs * shapes[0][0] * depth * width
         shape = (pairs, 8, depth) if place == 2 else (pairs, depth, width)
-        if merged and place == 0:
-            shape = (2 * pairs, depth, width)
-        if not (merged and place == 1):
-            outs.append(jax.ShapeDtypeStruct(shape, dtype))
+        if merged and place < 2:
+            shape = (1 if place else pairs + 1, depth, width)
+        outs.append(jax.ShapeDtypeStruct(shape, dtype))
     return pl.pallas_call(
         functools.partial(turned_kernel, pairs, len(rights), lead, merged),
         out_shape=outs,
@@ -877,16 +874,17 @@
     )
 
 
-def assemble_kernel(order_ref, *refs):
-    for block, ref in enumerate(refs[:-1]):
+def assemble_kernel(chained, order_ref, *refs):
+    for block, ref in enumerate(refs[1:-1] if chained else refs[:-1]):
 
         @pl.when(pl.program_id(0) == block)
         def _():
             refs[-1][0] = flat(ref).astype(F32)
 
 
-def assemble(order, blocks):
+def assemble(order, start, total, blocks, before=None):
     count = len(blocks)
+    chained = before is not None
     arrays = [item[0] if isinstance(item, tuple) else item for item in blocks]
     rows, width = arrays[0].shape[-2:]
     tiles = ASSEMBLE if rows % (16 * ASSEMBLE) == 0 else 1
@@ -902,19 +900,21 @@
         return pl.BlockSpec((rows // tiles, width), lambda b, i, s: (tile_of(b, i), 0))
 
     return pl.pallas_call(
-        assemble_kernel,
-        out_shape=jax.ShapeDtypeStruct((count, rows, width), F32),
+        functools.partial(assemble_kernel, chained),
+        out_shape=jax.ShapeDtypeStruct((total, rows, width), F32),
+        input_output_aliases={1: 0} if chained else {},
         grid_spec=pltpu.PrefetchScalarGridSpec(
             num_scalar_prefetch=1,
             grid=(count, tiles),
-            in_specs=[spec(place, item) for place, item in enumerate(blocks)],
+            in_specs=[pl.BlockSpec(memory_space=pl.ANY)] * chained
+            + [spec(place, item) for place, item in enumerate(blocks)],
             out_specs=pl.BlockSpec(
-                (1, rows // tiles, width), lambda b, i, s: (s[b], i, 0)
+                (1, rows // tiles, width), lambda b, i, s: (s[start + b], i, 0)
             ),
         ),
         compiler_params=pltpu.CompilerParams(vmem_limit_bytes=VMEM_BYTES),
         cost_estimate=cost(0, 7 * count * rows * width),
-    )(order, *arrays)
+    )(order, *([before] if chained else []), *arrays)
 
 
 def allowed_keys(row_segments, column_segments):
@@ -1137,9 +1137,10 @@
     return lax.rsqrt(squares / D + EPSILON)
 
 
-def norm_backward(rows_in, factor, gain_row, grad_in):
+def norm_backward(rows_in, factor, gain_row, grad_in, *waits):
     scaled = grad_in * gain_row
-    inner_sum = col_total(jnp.sum(scaled * rows_in, axis=1))[:, None]
+    inner_sum = jnp.sum(scaled * rows_in, axis=1)
+    inner_sum = col_total(after(inner_sum, *waits) if waits else inner_sum)[:, None]
     gain_grad = jnp.sum(grad_in * rows_in * factor, axis=0)
     return (factor * scaled - rows_in * factor**3 * inner_sum / D, gain_grad)
 
@@ -1183,8 +1184,11 @@
         hop = swap(lead_block(after(received, *waits), 1), "col", 1, col_count)
         return [(received, 0), (hop, 0)]
 
-    def fence(rows, numbers):
-        token = swap(tip(rows), "col", 1, col_count)[0, 0]
+    def fence(rows, numbers, times=1):
+        token = tip(rows)
+        for _ in range(times):
+            token = swap(token, "col", 1, col_count)
+        token = token[0, 0]
         return numbers + (token != token).astype(jnp.int32)
 
     def arrays(blocks):
@@ -1219,7 +1223,9 @@
     gain_a = gain_attn.astype(F32)
     normed_all = (hidden_all.astype(F32) * factor_a_all[:, None] * gain_a).astype(BF)
 
-    def col_scatter(rows, weight, extra_weight, transposed, first_waits, near_waits, near_first):
+    def col_scatter(
+        rows, weight, extra_weight, transposed, first_waits, near_waits, near_first, *far_waits
+    ):
         def part(blocks, scale):
             kept, *sent = pick_matmul(
                 blocks, attn_routes, rows, weight, extra_weight, group_rows, transposed, scale
@@ -1232,7 +1238,7 @@
             near = part(near_order, COST)
             far_order = after(far_order, near[0])
         kept, received = part(far_order, COST)
-        far = join_halves(kept, received)
+        far = join_halves(after(kept, *far_waits) if far_waits else kept, received)
         if not near_first:
             near = part(after(near_order, far, *near_waits), 1)
         return [[near[0]], near[1], far, [swap(far, "col", 2, col_count)]]
@@ -1410,7 +1416,7 @@
             merged,
         )
 
-    both_far, router_far = weight_grads((2, 3), BF, back_sent, True)
+    both_far, up_far, router_far = weight_grads((2, 3), BF, back_sent, True)
     grad_normed_f_part = gather_slots(
         after(owner_starts, both_far),
         owner_rows.T,
@@ -1444,8 +1450,14 @@
     down_pair(0, near_down[0], 0)
     down_pair(1, swap(near_down[1], "col", 1, col_count), 0)
 
+    gate_early = assemble(
+        after(block_order, grad_middle_low),
+        0,
+        col_count,
+        [(gate_near, 0), (gate_near_sent, 0)],
+    )
     far_down = pair_dots(
-        act_pairs[1], [after(down_pairs[0], near_down[1]), down_pairs[1]]
+        act_pairs[1], [after(down_pairs[0], near_down[1], gate_early), down_pairs[1]]
     )
     far_sent = swap(far_down, pair_axes, col_count, owners)
     down_pair(2, far_sent, 0)
@@ -1456,16 +1468,19 @@
         col_count,
     )
     down_pair(3, down_hop, 0)
+    up_received = swap(after(up_far, grad_middle_low), "col", 2, col_count)
     grad_gated = col_scatter(
-        grad_middle_all, out_weight, None, True, [far_down], [], True
+        grad_middle_all, out_weight, None, True, [far_down], [], True, up_received
     )
     own_base = dp_index * half_experts
     away_base = (1 - dp_index) * half_experts
+
+    grad_order = fence(grad_gated[2], block_order)
 
     def out_grads(base, dtype):
         return expert_grads(
             left_grad_kernel,
-            block_order,
+            grad_order,
             base,
             half_experts,
             attn_routes.T,
@@ -1475,8 +1490,10 @@
             dtype,
         )
 
+    out_away = out_grads(away_base, BF)
+    out_own = out_grads(own_base, F32)
     pieces, grad_logits_a = attend_back(
-        side,
+        after(side, out_away, out_own),
         segments,
         cosine,
         sine_rows,
@@ -1485,9 +1502,8 @@
         grad_gated[0:2] + grad_gated[3:],
     )
 
-    out_away = out_grads(after(away_base, pieces), BF)
     ffn_part = gather_slots(
-        fence(out_away, owner_starts),
+        after(owner_starts, pieces),
         owner_rows.T,
         [down_blocks[bits] for bits in range(owners)],
     )
@@ -1506,8 +1522,9 @@
         ]
 
     down_away = down_grad_part(1, BF, ffn_part)
+    down_near = down_grad_part(0, F32, down_away[0])
     logits_back = col_blocks(grad_logits_a)
-    pieces_blocks = col_blocks(pieces, *down_away)
+    pieces_blocks = col_blocks(pieces, out_away_sent, *down_away, *down_near)
     normed_part = merge_matmul(
         block_order,
         attn_routes,
@@ -1551,27 +1568,23 @@
     both_received = swap(after(both_far, pieces_blocks[2], logits_back[2]), "col", 2, col_count)
     tail = after(block_order, router_attn_grad)
     down_sent = [swap(item, "col", 1, col_count) for item in down_away]
-    out_own = out_grads(after(own_base, router_attn_grad), F32)
-    down_near = down_grad_part(0, F32, out_own)
     down_grad = assemble(
         after(tail, *down_near),
+        0,
+        col_count,
         [(down_near[0], 0), (down_sent[0], 0), (down_near[1], 0), (down_sent[1], 0)],
     )
+    up_early = assemble(
+        after(tail, down_grad),
+        0,
+        col_count,
+        [(up_near, 0), (up_near_sent, 0), (up_received, 0)],
+    )
     out_grad = add_wide(out_own, after(out_away_sent, down_grad))
-    both_side = take_blocks(
-        both_received,
-        after(jnp.arange(4, dtype=jnp.int32), down_grad, out_grad, query_sent),
-        1,
-        2,
-        2,
-    )
-    both_side = swap(both_side, "col", 1, col_count)
-    grad_normed = row_total(normed_part, both_side)
-    input_norm_grad, gain_attn_grad = norm_backward(
-        rows_in, factor_a[:, None], gain_a, grad_normed
-    )
-    input_grad = grad_middle + input_norm_grad
-    layer_out = (middle + ffn_total).astype(BF)
+    query_grad = add_wide(query_own, after(query_sent, out_grad))
+    kv_grad = add_wide(kv_own, after(kv_sent, out_grad))
+    grad_normed = row_total(normed_part, router_attn_grad)
+    gain_attn_grad = jnp.sum(grad_normed * rows_in * factor_a[:, None], axis=0)
     small = jnp.concatenate(
         [
             router_attn_grad,
@@ -1585,6 +1598,18 @@
         axis=0,
     )
     small = small_total(small, ("row", "dp"))
+    both_received = after(
+        both_received, gate_early, up_early, out_grad, query_grad, kv_grad, small
+    )
+    both_side = take_blocks(
+        both_received, fence(both_received, jnp.arange(4, dtype=jnp.int32)), 1, 1, 2
+    )
+    both_side = swap(both_side, "col", 1, col_count)
+    input_norm_grad, _ = norm_backward(
+        rows_in, factor_a[:, None], gain_a, grad_normed, both_side
+    )
+    input_grad = grad_middle + input_norm_grad
+    layer_out = (middle + ffn_total).astype(BF)
     lines = attn_experts + 2
     gain_ffn_grad, gain_attn_grad = small[lines - 2], small[lines - 1]
     router_ffn_grad = sum(
@@ -1596,14 +1621,10 @@
         )
         for bits in range(col_count)
     )
-    gate_grad, up_grad = [
-        assemble(tail, [(near, 0), (sent, 0), (both_received, 2 * place), (both_side, place)])
-        for place, (near, sent) in enumerate(
-            ((gate_near, gate_near_sent), (up_near, up_near_sent))
-        )
-    ]
-    query_grad = add_wide(query_own, after(query_sent, up_grad))
-    kv_grad = add_wide(kv_own, after(kv_sent, up_grad))
+    gate_grad = assemble(
+        tail, 2, col_count, [(both_received, 0), (both_side, 0)], gate_early
+    )
+    up_grad = assemble(tail, 3, col_count, [(both_side, 1)], up_early)
     ffn_half = ffn_experts // dp_count
     router_ffn_grad = lax.dynamic_slice_in_dim(
         router_ffn_grad, dp_index * ffn_half, ffn_half, 0

time: 953 us -> 928 us (0.974)
  waiting for transfers between devices: 267 us -> 230 us
    ppermute x75 -> x77, waiting for transfers between devices: 250 us -> 213 us  [swap(): return lax.ppermute(value, axes, [(i, i ^ bits) for i in range(size)])]
    unnamed x168 -> x170, local copies, waits for them, and re-layouts: 19.5 us -> 23.8 us
    pallas_call x3 -> x5, Pallas kernels: 31.1 us -> 34.5 us  [assemble(): pl.pallas_call(functools.partial(assemble_kernel, chained), out_shape=jax...]
    ppermute x75 -> x77, starting transfers between devices: 48.9 us -> 49.4 us  [swap(): return lax.ppermute(value, axes, [(i, i ^ bits) for i in range(size)])]
  transfers between devices with their start and end apart: 83 -> 85, of which waited for: 38 -> 34; matrix products, arithmetic and copies ran while one was open for 3% -> 3% of each run, Pallas kernels for 50% -> 50%
where the time goes in v3:
time: 928 us; the launch traced here: 920 us
  Pallas kernels  518 us (56%)
  waiting for transfers between devices  230 us (25%)
  starting transfers between devices  50.5 us (5%)
  blocking collectives  40.2 us (4%)
  local copies, waits for them, and re-layouts  35.2 us (4%)
  other arithmetic  26.3 us (3%)
  between operations  19.3 us (2%)
    ppermute x77, waiting for transfers between devices, swap(): return lax.ppermute(value, axes, [(i, i ^ bits) for i in range(size)])  213 us
    pallas_call x7, Pallas kernels, turned_dots(): pl.pallas_call(functools.partial(turned_kernel, pairs, len(rights), lead,...  60.5 us
    pallas_call x8, Pallas kernels, dots(): pl.pallas_call(functools.partial(dots_kernel, transposed, lead, len(lefts...  59.7 us
    ppermute x77, starting transfers between devices, swap(): return lax.ppermute(value, axes, [(i, i ^ bits) for i in range(size)])  49.4 us
    pallas_call x4, Pallas kernels, pick_matmul(): pl.pallas_call(functools.partial(pick_kernel, extra, transposed), out_sha...  44.5 us
    pallas_call x4, Pallas kernels, expert_grads(): pl.pallas_call(kernel, out_shape=jax.ShapeDtypeStruct((count,) + shape, d...  40.1 us
    pallas_call x2, Pallas kernels, expert_forward(): pl.pallas_call(functools.partial(expert_kernel, len(rows)), out_shape=out...  38.1 us
    pallas_call x2, Pallas kernels, merge_matmul(): pl.pallas_call(functools.partial(merge_kernel, count, bool(extras), trans...  38.1 us
  transfers between devices with their start and end apart: 85, of which 34 were waited for; matrix products, arithmetic and copies ran while one was open for 3% of the time, Pallas kernels for 50%

profile of v3, /device:TPU:0, one launch (start us, length us, event | category | flops | bytes accessed | tf_op | source)
XLA Modules:
  0.0 919.8 jit_solution(6682988068024247990)
XLA Ops:
  9.2 8.3 psum.28
  25.1 6.1 shard_map.256
  31.2 12.5 %all-gather = f32[4,1,512]{2,1,0:T(1,128)S(1)} all-gather(f32[1,1,512]{2,1,0:T(1,128)S(1)} %bitcast.67), channel_id=1, replica_groups=mesh['dp'=2,'row'=4,'col'=4] {'row'}, dimensions={0}, use_global_device_ids=true | all-gather | bytes 10240 | tf_op jit(solution)/shard_map/all_gather | solution.py:1113
  43.8 14.7 %all-gather.6.cloned.1.call-done = bf16[2048,512]{1,0:T(8,128)(2,1)} async-done(((bf16[512,512]{1,0:T(8,128)(2,1)}), bf16[2048,512]{1,0:T(8,128)(2,1)}) %all-gather.6.cloned.1.call-update) | async-done | bytes 2097168 | tf_op jit(solution)/shard_map/all_gather | solution.py:1113
  62.6 12.0 %shard_map.257 = (bf16[512,2048]{1,0:T(8,128)(2,1)}, bf16[512,1024]{1,0:T(8,128)(2,1)}, bf16[512,1024]{1,0:T(8,128)(2,1)}) custom-call(s32[2]{0:T(128)} %get-tuple-element.251.blocks_ref, s32[2048,2]{1,0:T(8,128)} %copy.69.routes_ref, bf16[2048,512]{1,0:T(8,128)(2,1)} %multiply_convert_fusion.x_ref.rows_ref, bf16[8,512,512]{2,1,0:T(8,128)(2,1)} %refs_8_.1, ...), custom_call_target="tpu_custom_call" | custom-call | flops 5120 | bytes 9 | tf_op jit(solution)/shard_map/pallas_call | solution.py:295
  85.7 12.3 %shard_map.264 = (bf16[512,2048]{1,0:T(8,128)(2,1)}, bf16[512,1024]{1,0:T(8,128)(2,1)}, bf16[512,1024]{1,0:T(8,128)(2,1)}) custom-call(s32[2]{0:T(128)} %get-tuple-element.249.blocks_ref, s32[2048,2]{1,0:T(8,128)} %copy.69.routes_ref, bf16[2048,512]{1,0:T(8,128)(2,1)} %multiply_convert_fusion.x_ref.rows_ref, bf16[8,512,512]{2,1,0:T(8,128)(2,1)} %refs_8_.1, ...), custom_call_target="tpu_custom_call" | custom-call | flops 5368709120 | bytes 9437184 | tf_op jit(solution)/shard_map/pallas_call | solution.py:295
  123.7 7.2 collective-permute-done.5
  134.7 17.4 %shard_map.265 = (bf16[4,512,512]{2,1,0:T(8,128)(2,1)}, f32[2,512,512]{2,1,0:T(8,128)}, bf16[2,512,512]{2,1,0:T(8,128)(2,1)}, f32[512,128]{1,0:T(8,128)}, f32[512,128]{1,0:T(8,128)}, /*index=5*/f32[512,128]{1,0:T(8,128)}) custom-call(f32[8,512]{1,0:T(8,128)} %add_add_fusion.logits_ref, s32[2,512]{1,0:T(2,128)} %dynamic-slice_bitcast_fusion.1.routes_ref, ...), custom_call_target="tpu_custom_call" | custom-call | flops 2048 | bytes 12 | tf_op jit(solution)/shard_map/pallas_call | solution.py:998
  157.0 10.6 %shard_map.266 = (bf16[2,640,512]{2,1,0:T(8,128)(2,1)}, bf16[2,640,512]{2,1,0:T(8,128)(2,1)}, bf16[2,640,512]{2,1,0:T(8,128)(2,1)}, bf16[2,640,512]{2,1,0:T(8,128)(2,1)}) custom-call(s32[8,16]{1,0:T(8,128)} %get-tuple-element.271.starts_ref, s32[8,2048]{1,0:T(8,128)} %get-tuple-element.173.places_ref, bf16[2048,512]{1,0:T(8,128)(2,1)} %all-gather.8.cloned.1.call-done.rows_ref), custom_call_target="tpu_custom_call" | custom-call | flops 4608 | bytes 7 | tf_op jit(solution)/shard_map/pallas_call | solution.py:581
  174.9 6.2 collective-permute-done.13.refs_14_.refs_5_
  186.7 16.9 %shard_map.269 = bf16[2048,512]{1,0:T(8,128)(2,1)} custom-call(s32[4]{0:T(128)} %copy-done.58, s32[2048,2]{1,0:T(8,128)} %copy.69.routes_ref, bf16[2,512,512]{2,1,0:T(8,128)(2,1)} %get-tuple-element.258.refs_0_, bf16[2,512,512]{2,1,0:T(8,128)(2,1)} %collective-permute-done.10.refs_1_, bf16[2,512,512]{2,1,0:T(8,128)(2,1)} %collective-permute-done.11.refs_2_, ...), custom_call_target="tpu_custom_call" | custom-call | flops 8192 | bytes 10 | tf_op jit(solution)/shard_map/pallas_call | solution.py:422
  209.7 5.8 shard_map.270
  215.5 19.7 %collective-permute-done.17.refs_0_.refs_3_ = bf16[2,640,512]{2,1,0:T(8,128)(2,1)S(1)} collective-permute-done((bf16[2,640,512]{2,1,0:T(8,128)(2,1)}, bf16[2,640,512]{2,1,0:T(8,128)(2,1)S(1)}, u32[]{:S(2)}, u32[]{:S(2)}) %collective-permute-start.17) | collective-permute-done | bytes 1310752 | tf_op jit(solution)/shard_map/ppermute | solution.py:1109
  235.2 13.2 %collective-permute-done.16.block_ref.refs_10_.refs_4_ = bf16[2,512,1408]{2,1,0:T(8,128)(2,1)} collective-permute-done((bf16[2,512,1408]{2,1,0:T(8,128)(2,1)}, bf16[2,512,1408]{2,1,0:T(8,128)(2,1)}, u32[]{:S(2)}, u32[]{:S(2)}) %collective-permute-start.16) | collective-permute-done | bytes 2883616 | tf_op jit(solution)/shard_map/ppermute | solution.py:1109
  256.1 6.9 psum.29
  267.2 6.1 shard_map.272.own_ref
  283.1 12.6 %collective-permute-done.22 = bf16[2,640,512]{2,1,0:T(8,128)(2,1)S(1)} collective-permute-done((bf16[2,640,512]{2,1,0:T(8,128)(2,1)S(1)}, bf16[2,640,512]{2,1,0:T(8,128)(2,1)S(1)}, u32[]{:S(2)}, u32[]{:S(2)}) %collective-permute-start.22) | collective-permute-done | bytes 1310752 | tf_op jit(solution)/shard_map/ppermute | solution.py:1109
  295.7 9.7 %collective-permute-done.21.sent_ref = bf16[640,1408]{1,0:T(8,128)(2,1)} collective-permute-done((bf16[640,1408]{1,0:T(8,128)(2,1)}, bf16[640,1408]{1,0:T(8,128)(2,1)}, u32[]{:S(2)}, u32[]{:S(2)}) %collective-permute-start.21) | collective-permute-done | bytes 1802272 | tf_op jit(solution)/shard_map/ppermute | solution.py:1109
  309.6 5.4 shard_map.276
  315.0 6.8 shard_map.277
  327.6 6.9 shard_map.278
  334.5 19.2 %collective-permute-done.25.block_ref.refs_2_.refs_0_ = bf16[2,640,512]{2,1,0:T(8,128)(2,1)S(1)} collective-permute-done((bf16[2,640,512]{2,1,0:T(8,128)(2,1)}, bf16[2,640,512]{2,1,0:T(8,128)(2,1)S(1)}, u32[]{:S(2)}, u32[]{:S(2)}) %collective-permute-start.25) | collective-permute-done | bytes 1310752 | tf_op jit(solution)/shard_map/ppermute | solution.py:1109
  362.4 5.7 shard_map.284.own_ref
  368.1 19.2 %shard_map.282 = (bf16[640,1408]{1,0:T(8,128)(2,1)}, bf16[640,1408]{1,0:T(8,128)(2,1)}, bf16[640,1408]{1,0:T(8,128)(2,1)}, bf16[640,128]{1,0:T(8,128)(2,1)}) custom-call(s32[1]{0:T(128)} %bitcast.9.owner_ref, s32[640,1]{1,0:T(8,128)} %convert_subtract_fusion.1.other_ref, f32[640,1408]{1,0:T(8,128)} %shard_map.272.own_ref, ...), custom_call_target="tpu_custom_call" | custom-call | flops 7040 | bytes 21 | tf_op jit(solution)/shard_map/pallas_call | solution.py:852
  387.3 9.1 shard_map.283
  396.5 10.8 %collective-permute-done.33.refs_2_.refs_1_ = bf16[640,512]{1,0:T(8,128)(2,1)S(1)} collective-permute-done((bf16[640,512]{1,0:T(8,128)(2,1)}, bf16[640,512]{1,0:T(8,128)(2,1)S(1)}, u32[]{:S(2)}, u32[]{:S(2)}) %collective-permute-start.33) | collective-permute-done | bytes 655392 | tf_op jit(solution)/shard_map/ppermute | solution.py:1109
  407.3 12.1 %collective-permute-done.34.refs_3_ = bf16[640,512]{1,0:T(8,128)(2,1)S(1)} collective-permute-done((bf16[640,512]{1,0:T(8,128)(2,1)}, bf16[640,512]{1,0:T(8,128)(2,1)S(1)}, u32[]{:S(2)}, u32[]{:S(2)}) %collective-permute-start.34) | collective-permute-done | bytes 655392 | tf_op jit(solution)/shard_map/ppermute | solution.py:1109
  420.3 18.9 %shard_map.285 = (bf16[640,1408]{1,0:T(8,128)(2,1)}, bf16[640,1408]{1,0:T(8,128)(2,1)}, bf16[640,1408]{1,0:T(8,128)(2,1)}, bf16[640,128]{1,0:T(8,128)(2,1)}) custom-call(s32[1]{0:T(128)} %bitcast.9.owner_ref, s32[640,1]{1,0:T(8,128)} %convert_subtract_fusion.other_ref, f32[640,1408]{1,0:T(8,128)} %shard_map.284.own_ref, ...), custom_call_target="tpu_custom_call" | custom-call | flops 7040 | bytes 21 | tf_op jit(solution)/shard_map/pallas_call | solution.py:852
  439.2 9.4 %shard_map.289 = bf16[2,640,512]{2,1,0:T(8,128)(2,1)} custom-call(bf16[640,1408]{1,0:T(8,128)(2,1)} %get-tuple-element.223.refs_0_.refs_5_.refs_3_, bf16[640,1408]{1,0:T(8,128)(2,1)} %get-tuple-element.224.refs_1_.refs_7_.refs_5_, bf16[640,128]{1,0:T(8,128)(2,1)} %get-tuple-element.225.refs_2_.refs_9_.refs_7_, bf16[2,512,1408]{2,1,0:T(8,128)(2,1)} %copy-done.1, ...), custom_call_target="tpu_custom_call" | custom-call | flops 7360 | bytes 10 | tf_op jit(solution)/shard_map/pallas_call | solution.py:699
  450.1 9.1 shard_map.286
  459.1 9.1 shard_map.287
  471.4 10.1 %collective-permute-done.40.block_ref.refs_6_ = bf16[2,640,512]{2,1,0:T(8,128)(2,1)S(1)} collective-permute-done((bf16[2,640,512]{2,1,0:T(8,128)(2,1)}, bf16[2,640,512]{2,1,0:T(8,128)(2,1)S(1)}, u32[]{:S(2)}, u32[]{:S(2)}) %collective-permute-start.40) | collective-permute-done | bytes 1310752 | tf_op jit(solution)/shard_map/ppermute | solution.py:1109
  485.8 15.9 %shard_map.288 = (bf16[3,512,1408]{2,1,0:T(8,128)(2,1)}, bf16[1,512,1408]{2,1,0:T(8,128)(2,1)}, f32[2,8,512]{2,1,0:T(8,128)}) custom-call(bf16[2,640,512]{2,1,0:T(8,128)(2,1)} %copy-done.16, bf16[640,512]{1,0:T(8,128)(2,1)} %copy-done.31, bf16[1,640,512]{2,1,0:T(8,128)(2,1)} %collective-permute-done.26.refs_3_.refs_2_, bf16[640,512]{1,0:T(8,128)(2,1)} %copy-done.32, ...), custom_call_target="tpu_custom_call" | custom-call | flops 7360 | bytes 24 | tf_op jit(solution)/shard_map/pallas_call | solution.py:787
  501.7 6.5 collective-permute-done.37.refs_3_
  509.3 9.4 %shard_map.291 = bf16[2048,512]{1,0:T(8,128)(2,1)} custom-call(s32[8,16]{1,0:T(8,128)} %get-tuple-element.271.starts_ref, s32[2048,8]{1,0:T(8,128)} %bitcast.57, bf16[640,512]{1,0:T(8,128)(2,1)} %get-tuple-element.232.refs_0_, bf16[640,512]{1,0:T(8,128)(2,1)} %copy-done.41, bf16[640,512]{1,0:T(8,128)(2,1)} %copy-done.42, bf16[640,512]{1,0:T(8,128)(2,1)} %copy-done.44, ...), custom_call_target="tpu_custom_call" | custom-call | flops 4608 | bytes 7 | tf_op jit(solution)/shard_map/pallas_call | solution.py:631
  521.6 10.0 %shard_map.292 = (f32[1,512,1408]{2,1,0:T(8,128)}, f32[1,512,1408]{2,1,0:T(8,128)}, f32[1,8,512]{2,1,0:T(8,128)}) custom-call(bf16[640,512]{1,0:T(8,128)(2,1)} %get-tuple-element.212.refs_0_, bf16[640,512]{1,0:T(8,128)(2,1)} %copy-done.29, bf16[640,1408]{1,0:T(8,128)(2,1)} %get-tuple-element.214.refs_0_.refs_4_.refs_2_, ...), custom_call_target="tpu_custom_call" | custom-call | flops 3680 | bytes 12 | tf_op jit(solution)/shard_map/pallas_call | solution.py:787
  531.6 9.7 %shard_map.293 = (bf16[1,512,1408]{2,1,0:T(8,128)(2,1)}, bf16[1,512,1408]{2,1,0:T(8,128)(2,1)}, f32[1,8,512]{2,1,0:T(8,128)}) custom-call(bf16[640,512]{1,0:T(8,128)(2,1)} %copy-done.33, bf16[640,512]{1,0:T(8,128)(2,1)} %copy-done.30, bf16[640,1408]{1,0:T(8,128)(2,1)} %get-tuple-element.214.refs_0_.refs_4_.refs_2_, ...), custom_call_target="tpu_custom_call" | custom-call | flops 3680 | bytes 12 | tf_op jit(solution)/shard_map/pallas_call | solution.py:787
  541.4 20.5 %collective-permute-done.42.other_ref.refs_0_ = bf16[640,1408]{1,0:T(8,128)(2,1)} collective-permute-done((bf16[640,1408]{1,0:T(8,128)(2,1)S(1)}, bf16[640,1408]{1,0:T(8,128)(2,1)}, u32[]{:S(2)}, u32[]{:S(2)}) %collective-permute-start.42) | collective-permute-done | bytes 1802272 | tf_op jit(solution)/shard_map/ppermute | solution.py:1109
  565.8 6.4 psum.30
  576.8 5.7 shard_map.294
  583.6 6.0 shard_map.295.refs_0_
  589.6 27.4 %collective-permute-done.43.other_ref.refs_1_ = bf16[640,1408]{1,0:T(8,128)(2,1)S(1)} collective-permute-done((bf16[640,1408]{1,0:T(8,128)(2,1)S(1)}, bf16[640,1408]{1,0:T(8,128)(2,1)S(1)}, u32[]{:S(2)}, u32[]{:S(2)}) %collective-permute-start.43) | collective-permute-done | bytes 1802272 | tf_op jit(solution)/shard_map/ppermute | solution.py:1109
  618.2 9.0 shard_map.296
  628.7 10.1 %shard_map.297 = (bf16[512,1024]{1,0:T(8,128)(2,1)}, bf16[512,512]{1,0:T(8,128)(2,1)}, bf16[512,512]{1,0:T(8,128)(2,1)}) custom-call(s32[2]{0:T(128)} %get-tuple-element.249.blocks_ref, s32[2048,2]{1,0:T(8,128)} %copy.69.routes_ref, bf16[2048,512]{1,0:T(8,128)(2,1)} %all-gather.12.cloned.1.call-done.x_ref.rows_ref, bf16[8,512,512]{2,1,0:T(8,128)(2,1)} %w_ref.7), custom_call_target="tpu_custom_call" | custom-call | flops 4096 | bytes 7 | tf_op jit(solution)/shard_map/pallas_call | solution.py:295
  638.8 10.1 %shard_map.298 = (bf16[512,1024]{1,0:T(8,128)(2,1)}, bf16[512,512]{1,0:T(8,128)(2,1)}, bf16[512,512]{1,0:T(8,128)(2,1)}) custom-call(s32[2]{0:T(128)} %get-tuple-element.251.blocks_ref, s32[2048,2]{1,0:T(8,128)} %copy.69.routes_ref, bf16[2048,512]{1,0:T(8,128)(2,1)} %all-gather.12.cloned.1.call-done.x_ref.rows_ref, bf16[8,512,512]{2,1,0:T(8,128)(2,1)} %w_ref.7), custom_call_target="tpu_custom_call" | custom-call | flops 4096 | bytes 7 | tf_op jit(solution)/shard_map/pallas_call | solution.py:295
  665.2 9.4 %shard_map.302 = bf16[4,512,512]{2,1,0:T(8,128)(2,1)} custom-call(s32[5]{0:T(128)} %get-tuple-element.315.scalars_ref, s32[2,2048]{1,0:T(2,128)} %bitcast.63, bf16[2048,512]{1,0:T(8,128)(2,1)} %all-gather.12.cloned.1.call-done.x_ref.rows_ref, bf16[2,512,512]{2,1,0:T(8,128)(2,1)} %get-tuple-element.259.refs_0_, ...), custom_call_target="tpu_custom_call" | custom-call | flops 4096 | bytes 10 | tf_op jit(solution)/shard_map/pallas_call | solution.py:472
  675.2 9.6 %shard_map.303.own_ref = f32[4,512,512]{2,1,0:T(8,128)} custom-call(s32[5]{0:T(128)} %get-tuple-element.314.scalars_ref, s32[2,2048]{1,0:T(2,128)} %bitcast.64, bf16[2048,512]{1,0:T(8,128)(2,1)} %all-gather.12.cloned.1.call-done.x_ref.rows_ref, bf16[2,512,512]{2,1,0:T(8,128)(2,1)} %get-tuple-element.259.refs_0_, ...), custom_call_target="tpu_custom_call" | custom-call | flops 4096 | bytes 10 | tf_op jit(solution)/shard_map/pallas_call | solution.py:472
  686.1 15.1 %shard_map.304 = (bf16[4,512,512]{2,1,0:T(8,128)(2,1)}, bf16[512,128]{1,0:T(8,128)(2,1)}) custom-call(f32[512,128]{1,0:T(8,128)} %get-tuple-element.263.side_ref, s32[512,1]{1,0:T(8,128)} %copy.66.rows_ref, s32[1,512]{1,0:T(1,128)} %columns_ref.3, f32[512,128]{1,0:T(8,128)} %get-tuple-element.264.cos_ref, f32[512,128]{1,0:T(8,128)} %get-tuple-element.265.sin_ref, ...), custom_call_target="tpu_custom_call" | custom-call | flops 5120 | bytes 20 | tf_op jit(solution)/shard_map/pallas_call | solution.py:1083
  706.2 5.7 shard_map.305.refs_0_.refs_2_
  711.9 5.9 shard_map.309
  717.9 6.5 shard_map.311.refs_2_
  726.6 9.6 %shard_map.307 = bf16[2048,512]{1,0:T(8,128)(2,1)} custom-call(s32[8,16]{1,0:T(8,128)} %get-tuple-element.271.starts_ref, s32[2048,8]{1,0:T(8,128)} %bitcast.58, bf16[2,640,512]{2,1,0:T(8,128)(2,1)} %shard_map.305.refs_0_.refs_2_, bf16[2,640,512]{2,1,0:T(8,128)(2,1)} %copy-done.18, bf16[2,640,512]{2,1,0:T(8,128)(2,1)} %shard_map.305.refs_0_.refs_2_, ...), custom_call_target="tpu_custom_call" | custom-call | flops 4608 | bytes 7 | tf_op jit(solution)/shard_map/pallas_call | solution.py:631
  736.2 6.0 shard_map.308
  742.2 6.4 shard_map.310.refs_0_
  758.6 21.1 %shard_map.312 = bf16[2048,512]{1,0:T(8,128)(2,1)} custom-call(s32[4]{0:T(128)} %copy-done.58, s32[2048,2]{1,0:T(8,128)} %copy.69.routes_ref, bf16[4,512,512]{2,1,0:T(8,128)(2,1)} %get-tuple-element.270.refs_0_, bf16[4,512,512]{2,1,0:T(8,128)(2,1)} %collective-permute-done.55.refs_1_, bf16[4,512,512]{2,1,0:T(8,128)(2,1)} %collective-permute-done.56.refs_2_, ...), custom_call_target="tpu_custom_call" | custom-call | flops 10240 | bytes 14 | tf_op jit(solution)/shard_map/pallas_call | solution.py:422
  785.0 10.7 %shard_map.314.rows_ref = bf16[4,512,512]{2,1,0:T(8,128)(2,1)} custom-call(s32[5]{0:T(128)} %pad_add_fusion.2.scalars_ref, s32[2048,2]{1,0:T(8,128)} %copy.69.routes_ref, bf16[512,2048]{1,0:T(8,128)(2,1)} %bitcast.51, bf16[4,512,512]{2,1,0:T(8,128)(2,1)} %get-tuple-element.270.refs_0_, bf16[4,512,512]{2,1,0:T(8,128)(2,1)} %collective-permute-done.55.refs_1_, ...), custom_call_target="tpu_custom_call" | custom-call | flops 4096 | bytes 10 | tf_op jit(solution)/shard_map/pallas_call | solution.py:472
  808.0 10.5 %shard_map.317.own_ref = f32[4,512,512]{2,1,0:T(8,128)} custom-call(s32[5]{0:T(128)} %pad_add_fusion.4.scalars_ref, s32[2048,2]{1,0:T(8,128)} %copy.69.routes_ref, bf16[512,2048]{1,0:T(8,128)(2,1)} %bitcast.53, bf16[4,512,512]{2,1,0:T(8,128)(2,1)} %get-tuple-element.270.refs_0_, bf16[4,512,512]{2,1,0:T(8,128)(2,1)} %collective-permute-done.55.refs_1_, ...), custom_call_target="tpu_custom_call" | custom-call | flops 4096 | bytes 10 | tf_op jit(solution)/shard_map/pallas_call | solution.py:472
  838.5 6.2 collective-permute-done.70
  846.8 11.1 %shard_map.320 = f32[4,1408,512]{2,1,0:T(8,128)} custom-call(s32[4]{0:T(128)} %copy-done.58, f32[1,1408,512]{2,1,0:T(8,128)} %shard_map.310.refs_0_, bf16[1,1408,512]{2,1,0:T(8,128)(2,1)} %collective-permute-done.64.refs_1_, f32[1,1408,512]{2,1,0:T(8,128)} %shard_map.311.refs_2_, bf16[1,1408,512]{2,1,0:T(8,128)(2,1)} %collective-permute-done.65.refs_3_), custom_call_target="tpu_custom_call" | custom-call | bytes 19 | tf_op jit(solution)/shard_map/pallas_call | solution.py:902
  857.9 5.1 shard_map.322
  863.0 8.0 shard_map.321.refs_0_
  874.3 5.1 shard_map.323
  894.1 5.8 shard_map.327
  903.5 6.1 psum.31
  (418 shorter events, 239.8 us)
Async XLA Ops:
  7.2 51.2 %all-gather.6.cloned.1.call-start = ((), (), s32[]{:S(2)}) async-start(), calls=%async_computation.4 | async-start | bytes 2621440 | tf_op jit(solution)/shard_map/all_gather | solution.py:1113
  7.9 149.1 %all-gather.8.cloned.1.call-start = ((), (), s32[]{:S(2)}) async-start(), calls=%async_computation.5 | async-start | bytes 2621440 | tf_op jit(solution)/shard_map/all_gather | solution.py:1113
  22.6 63.1 %collective-permute-start.6 = (bf16[2,512,1408]{2,1,0:T(8,128)(2,1)}, bf16[2,512,1408]{2,1,0:T(8,128)(2,1)S(1)}, u32[]{:S(2)}, u32[]{:S(2)}) collective-permute-start(bf16[2,512,1408]{2,1,0:T(8,128)(2,1)} %shard_map.263), channel_id=1, source_target_pairs={{0,2},{1,3},{2,0},{3,1},{4,6},{5,7},{6,4},{7,5},{8,10},{9,11},{10,... | collective-permute-start | bytes 8650760 | tf_op jit(solution)/shard_map/ppermute | solution.py:1109
  75.1 179.3 %reduce-scatter.5.cloned.1.call-start = ((), (), s32[]{:S(2)}) async-start(), calls=%async_computation.6 | async-start | bytes 2621440 | tf_op jit(solution)/shard_map/reduce_scatter | solution.py:1117
  83.4 50.0 %collective-permute-start.9 = (bf16[512,2048]{1,0:T(8,128)(2,1)}, bf16[512,2048]{1,0:T(8,128)(2,1)}, u32[]{:S(2)}, u32[]{:S(2)}) collective-permute-start(bf16[512,2048]{1,0:T(8,128)(2,1)} %shard_map.258), channel_id=1, source_target_pairs={{0,2},{1,3},{2,0},{3,1},{4,6},{5,7},{6,4},{7,5},{8,10},{9,11},{10,... | collective-permute-start | bytes 6291464 | tf_op jit(solution)/shard_map/ppermute | solution.py:1109
  98.0 35.3 %collective-permute-start.7 = (bf16[512,1024]{1,0:T(8,128)(2,1)}, bf16[512,1024]{1,0:T(8,128)(2,1)S(1)}, u32[]{:S(2)}, u32[]{:S(2)}) collective-permute-start(bf16[512,1024]{1,0:T(8,128)(2,1)} %get-tuple-element.184), channel_id=1, source_target_pairs={{0,1},{1,0},{2,3},{3,2},{4,5},{5,4},{6,7},{7,6},{8,9},{9,8},{10,11... | collective-permute-start | bytes 3145736 | tf_op jit(solution)/shard_map/ppermute | solution.py:1109
  98.1 35.3 %collective-permute-start.8 = (bf16[512,1024]{1,0:T(8,128)(2,1)}, bf16[512,1024]{1,0:T(8,128)(2,1)S(1)}, u32[]{:S(2)}, u32[]{:S(2)}) collective-permute-start(bf16[512,1024]{1,0:T(8,128)(2,1)} %get-tuple-element.185), channel_id=1, source_target_pairs={{0,1},{1,0},{2,3},{3,2},{4,5},{5,4},{6,7},{7,6},{8,9},{9,8},{10,11... | collective-permute-start | bytes 3145736 | tf_op jit(solution)/shard_map/ppermute | solution.py:1109
  108.8 12.5 %collective-permute-start.2 = (bf16[640,8]{1,0:T(8,128)(2,1)}, bf16[640,8]{1,0:T(8,128)(2,1)S(1)}, u32[]{:S(2)}, u32[]{:S(2)}) collective-permute-start(bf16[640,8]{1,0:T(8,128)(2,1)} %bitcast.78), channel_id=1, source_target_pairs={{0,16},{1,17},{2,18},{3,19},{16,0},{17,1},{18,2},{19,3},{4,20},{5,... | collective-permute-start | bytes 30728 | tf_op jit(solution)/shard_map/ppermute | solution.py:1109
  122.1 8.8 collective-permute-start.5
  123.0 9.7 %collective-permute-start.4 = (f32[8,512]{1,0:T(8,128)S(1)}, f32[8,512]{1,0:T(8,128)S(1)}, u32[]{:S(2)}, u32[]{:S(2)}) collective-permute-start(f32[8,512]{1,0:T(8,128)S(1)} %copy-done.81), channel_id=1, source_target_pairs={{0,2},{1,3},{2,0},{3,1},{4,6},{5,7},{6,4},{7,5},{8,10},{9,11},{10,... | collective-permute-start | bytes 49160 | tf_op jit(solution)/shard_map/ppermute | solution.py:1109
  152.1 30.7 %collective-permute-start.11 = (bf16[2,512,512]{2,1,0:T(8,128)(2,1)}, bf16[2,512,512]{2,1,0:T(8,128)(2,1)}, u32[]{:S(2)}, u32[]{:S(2)}) collective-permute-start(bf16[2,512,512]{2,1,0:T(8,128)(2,1)} %get-tuple-element.258.refs_0_), channel_id=1, source_target_pairs={{0,2},{1,3},{2,0},{3,1},{4,6},{5,7},{6,4},{7,5},{8,10},{9,11},{10,... | collective-permute-start | bytes 3145736 | tf_op jit(solution)/shard_map/ppermute | solution.py:1109
  153.8 21.1 %collective-permute-start.12 = (bf16[512,128]{1,0:T(8,128)(2,1)S(1)}, bf16[512,128]{1,0:T(8,128)(2,1)S(1)}, u32[]{:S(2)}, u32[]{:S(2)}) collective-permute-start(bf16[512,128]{1,0:T(8,128)(2,1)S(1)} %pad.8.refs_12_.refs_5_.refs_8_), channel_id=1, source_target_pairs={{0,1},{1,0},{2,3},{3,2},{4,5},{5,4},{6,7},{7,6},{8,9},{9,8},{10,11... | collective-permute-start | bytes 393224 | tf_op jit(solution)/shard_map/ppermute | solution.py:1109
  153.9 27.2 %collective-permute-start.13 = (bf16[512,128]{1,0:T(8,128)(2,1)S(1)}, bf16[512,128]{1,0:T(8,128)(2,1)S(1)}, u32[]{:S(2)}, u32[]{:S(2)}) collective-permute-start(bf16[512,128]{1,0:T(8,128)(2,1)S(1)} %pad.8.refs_12_.refs_5_.refs_8_), channel_id=1, source_target_pairs={{0,2},{1,3},{2,0},{3,1},{4,6},{5,7},{6,4},{7,5},{8,10},{9,11},{10,... | collective-permute-start | bytes 393224 | tf_op jit(solution)/shard_map/ppermute | solution.py:1109
  154.5 28.2 %collective-permute-start.14 = (bf16[512,128]{1,0:T(8,128)(2,1)S(1)}, bf16[512,128]{1,0:T(8,128)(2,1)S(1)}, u32[]{:S(2)}, u32[]{:S(2)}) collective-permute-start(bf16[512,128]{1,0:T(8,128)(2,1)S(1)} %pad.8.refs_12_.refs_5_.refs_8_), channel_id=1, source_target_pairs={{0,3},{1,2},{2,1},{3,0},{4,7},{5,6},{6,5},{7,4},{8,11},{9,10},{10,... | collective-permute-start | bytes 393224 | tf_op jit(solution)/shard_map/ppermute | solution.py:1109
  155.8 29.0 %collective-permute-start.10 = (bf16[2,512,512]{2,1,0:T(8,128)(2,1)}, bf16[2,512,512]{2,1,0:T(8,128)(2,1)}, u32[]{:S(2)}, u32[]{:S(2)}) collective-permute-start(bf16[2,512,512]{2,1,0:T(8,128)(2,1)} %get-tuple-element.258.refs_0_), channel_id=1, source_target_pairs={{0,1},{1,0},{2,3},{3,2},{4,5},{5,4},{6,7},{7,6},{8,9},{9,8},{10,11... | collective-permute-start | bytes 3145736 | tf_op jit(solution)/shard_map/ppermute | solution.py:1109
  183.2 23.9 %collective-permute-start.19 = (bf16[2,1408,512]{2,1,0:T(8,128)(2,1)}, bf16[2,1408,512]{2,1,0:T(8,128)(2,1)S(1)}, u32[]{:S(2)}, u32[]{:S(2)}) collective-permute-start(bf16[2,1408,512]{2,1,0:T(8,128)(2,1)} %shard_map.268), channel_id=1, source_target_pairs={{0,1},{1,0},{2,3},{3,2},{4,5},{5,4},{6,7},{7,6},{8,9},{9,8},{10,11... | collective-permute-start | bytes 8650760 | tf_op jit(solution)/shard_map/ppermute | solution.py:1109
  183.3 65.1 %collective-permute-start.16 = (bf16[2,512,1408]{2,1,0:T(8,128)(2,1)}, bf16[2,512,1408]{2,1,0:T(8,128)(2,1)}, u32[]{:S(2)}, u32[]{:S(2)}) collective-permute-start(bf16[2,512,1408]{2,1,0:T(8,128)(2,1)} %shard_map.260), channel_id=1, source_target_pairs={{0,2},{1,3},{2,0},{3,1},{4,6},{5,7},{6,4},{7,5},{8,10},{9,11},{10,... | collective-permute-start | bytes 8650760 | tf_op jit(solution)/shard_map/ppermute | solution.py:1109
  203.7 111.4 %all-gather.10.cloned.1.call-start = ((), (), s32[]{:S(2)}) async-start(), calls=%async_computation.7 | async-start | bytes 2621440 | tf_op jit(solution)/shard_map/all_gather | solution.py:1113
  204.2 31.0 %collective-permute-start.17 = (bf16[2,640,512]{2,1,0:T(8,128)(2,1)}, bf16[2,640,512]{2,1,0:T(8,128)(2,1)S(1)}, u32[]{:S(2)}, u32[]{:S(2)}) collective-permute-start(bf16[2,640,512]{2,1,0:T(8,128)(2,1)} %get-tuple-element.195), channel_id=1, source_target_pairs={{0,16},{1,17},{2,18},{3,19},{16,0},{17,1},{18,2},{19,3},{4,20},{5,... | collective-permute-start | bytes 3932168 | tf_op jit(solution)/shard_map/ppermute | solution.py:1109
  265.0 298.5 %reduce-scatter.7.cloned.1.call-start = ((), (), s32[]{:S(2)}) async-start(), calls=%async_computation.8 | async-start | bytes 2621440 | tf_op jit(solution)/shard_map/reduce_scatter | solution.py:1117
  265.1 40.3 %collective-permute-start.21 = (bf16[640,1408]{1,0:T(8,128)(2,1)}, bf16[640,1408]{1,0:T(8,128)(2,1)}, u32[]{:S(2)}, u32[]{:S(2)}) collective-permute-start(bf16[640,1408]{1,0:T(8,128)(2,1)} %shard_map.270), channel_id=1, source_target_pairs={{0,2},{1,3},{2,0},{3,1},{4,6},{5,7},{6,4},{7,5},{8,10},{9,11},{10,... | collective-permute-start | bytes 5406728 | tf_op jit(solution)/shard_map/ppermute | solution.py:1109
  265.7 30.0 %collective-permute-start.22 = (bf16[2,640,512]{2,1,0:T(8,128)(2,1)S(1)}, bf16[2,640,512]{2,1,0:T(8,128)(2,1)S(1)}, u32[]{:S(2)}, u32[]{:S(2)}) collective-permute-start(bf16[2,640,512]{2,1,0:T(8,128)(2,1)S(1)} %copy-done.79), channel_id=1, source_target_pairs={{0,16},{1,17},{2,18},{3,19},{16,0},{17,1},{18,2},{19,3},{4,20},{5,... | collective-permute-start | bytes 3932168 | tf_op jit(solution)/shard_map/ppermute | solution.py:1109
  308.0 48.7 %collective-permute-start.28 = (bf16[1,512,1408]{2,1,0:T(8,128)(2,1)}, bf16[1,512,1408]{2,1,0:T(8,128)(2,1)S(1)}, u32[]{:S(2)}, u32[]{:S(2)}) collective-permute-start(bf16[1,512,1408]{2,1,0:T(8,128)(2,1)} %shard_map.281), channel_id=1, source_target_pairs={{0,1},{1,0},{2,3},{3,2},{4,5},{5,4},{6,7},{7,6},{8,9},{9,8},{10,11... | collective-permute-start | bytes 4325384 | tf_op jit(solution)/shard_map/ppermute | solution.py:1109
  321.9 31.9 %collective-permute-start.25 = (bf16[2,640,512]{2,1,0:T(8,128)(2,1)}, bf16[2,640,512]{2,1,0:T(8,128)(2,1)S(1)}, u32[]{:S(2)}, u32[]{:S(2)}) collective-permute-start(bf16[2,640,512]{2,1,0:T(8,128)(2,1)} %get-tuple-element.208), channel_id=1, source_target_pairs={{0,2},{1,3},{2,0},{3,1},{16,18},{17,19},{18,16},{19,17},{4,6},{5,7... | collective-permute-start | bytes 3932168 | tf_op jit(solution)/shard_map/ppermute | solution.py:1109
  326.6 30.2 %collective-permute-start.27 = (bf16[1,512,1408]{2,1,0:T(8,128)(2,1)}, bf16[1,512,1408]{2,1,0:T(8,128)(2,1)S(1)}, u32[]{:S(2)}, u32[]{:S(2)}) collective-permute-start(bf16[1,512,1408]{2,1,0:T(8,128)(2,1)} %shard_map.280), channel_id=1, source_target_pairs={{0,1},{1,0},{2,3},{3,2},{4,5},{5,4},{6,7},{7,6},{8,9},{9,8},{10,11... | collective-permute-start | bytes 4325384 | tf_op jit(solution)/shard_map/ppermute | solution.py:1109
  326.6 32.6 %collective-permute-start.29 = (bf16[1,512,1408]{2,1,0:T(8,128)(2,1)}, bf16[1,512,1408]{2,1,0:T(8,128)(2,1)S(1)}, u32[]{:S(2)}, u32[]{:S(2)}) collective-permute-start(bf16[1,512,1408]{2,1,0:T(8,128)(2,1)} %shard_map.275), channel_id=1, source_target_pairs={{0,1},{1,0},{2,3},{3,2},{4,5},{5,4},{6,7},{7,6},{8,9},{9,8},{10,11... | collective-permute-start | bytes 4325384 | tf_op jit(solution)/shard_map/ppermute | solution.py:1109
  327.1 92.4 %collective-permute-start.30 = (bf16[640,1408]{1,0:T(8,128)(2,1)}, bf16[640,1408]{1,0:T(8,128)(2,1)}, u32[]{:S(2)}, u32[]{:S(2)}) collective-permute-start(bf16[640,1408]{1,0:T(8,128)(2,1)} %shard_map.276), channel_id=1, source_target_pairs={{0,2},{1,3},{2,0},{3,1},{4,6},{5,7},{6,4},{7,5},{8,10},{9,11},{10,... | collective-permute-start | bytes 5406728 | tf_op jit(solution)/shard_map/ppermute | solution.py:1109
  353.7 6.1 collective-permute-start.24
  356.8 50.5 %collective-permute-start.33 = (bf16[640,512]{1,0:T(8,128)(2,1)}, bf16[640,512]{1,0:T(8,128)(2,1)S(1)}, u32[]{:S(2)}, u32[]{:S(2)}) collective-permute-start(bf16[640,512]{1,0:T(8,128)(2,1)} %get-tuple-element.209), channel_id=1, source_target_pairs={{0,18},{1,19},{2,16},{3,17},{16,2},{17,3},{18,0},{19,1},{4,22},{5,... | collective-permute-start | bytes 1966088 | tf_op jit(solution)/shard_map/ppermute | solution.py:1109
  359.2 37.2 %collective-permute-start.31 = (bf16[640,512]{1,0:T(8,128)(2,1)}, bf16[640,512]{1,0:T(8,128)(2,1)S(1)}, u32[]{:S(2)}, u32[]{:S(2)}) collective-permute-start(bf16[640,512]{1,0:T(8,128)(2,1)} %get-tuple-element.219), channel_id=1, source_target_pairs={{0,16},{1,17},{2,18},{3,19},{16,0},{17,1},{18,2},{19,3},{4,20},{5,... | collective-permute-start | bytes 1966088 | tf_op jit(solution)/shard_map/ppermute | solution.py:1109
  360.6 35.8 %collective-permute-start.32 = (bf16[640,512]{1,0:T(8,128)(2,1)}, bf16[640,512]{1,0:T(8,128)(2,1)S(1)}, u32[]{:S(2)}, u32[]{:S(2)}) collective-permute-start(bf16[640,512]{1,0:T(8,128)(2,1)} %get-tuple-element.221), channel_id=1, source_target_pairs={{0,17},{1,16},{2,19},{3,18},{16,1},{17,0},{18,3},{19,2},{4,21},{5,... | collective-permute-start | bytes 1966088 | tf_op jit(solution)/shard_map/ppermute | solution.py:1109
  361.6 57.9 %collective-permute-start.34 = (bf16[640,512]{1,0:T(8,128)(2,1)}, bf16[640,512]{1,0:T(8,128)(2,1)S(1)}, u32[]{:S(2)}, u32[]{:S(2)}) collective-permute-start(bf16[640,512]{1,0:T(8,128)(2,1)} %get-tuple-element.210), channel_id=1, source_target_pairs={{0,19},{1,18},{2,17},{3,16},{16,3},{17,2},{18,1},{19,0},{4,23},{5,... | collective-permute-start | bytes 1966088 | tf_op jit(solution)/shard_map/ppermute | solution.py:1109
  448.6 32.8 %collective-permute-start.40 = (bf16[2,640,512]{2,1,0:T(8,128)(2,1)}, bf16[2,640,512]{2,1,0:T(8,128)(2,1)S(1)}, u32[]{:S(2)}, u32[]{:S(2)}) collective-permute-start(bf16[2,640,512]{2,1,0:T(8,128)(2,1)} %shard_map.289), channel_id=1, source_target_pairs={{0,18},{1,19},{2,16},{3,17},{16,2},{17,3},{18,0},{19,1},{4,22},{5,... | collective-permute-start | bytes 3932168 | tf_op jit(solution)/shard_map/ppermute | solution.py:1109
  468.3 16.2 %collective-permute-start.35 = (bf16[640,512]{1,0:T(8,128)(2,1)}, bf16[640,512]{1,0:T(8,128)(2,1)S(1)}, u32[]{:S(2)}, u32[]{:S(2)}) collective-permute-start(bf16[640,512]{1,0:T(8,128)(2,1)} %get-tuple-element.228), channel_id=1, source_target_pairs={{0,1},{1,0},{2,3},{3,2},{16,17},{17,16},{18,19},{19,18},{4,5},{5,4... | collective-permute-start | bytes 1966088 | tf_op jit(solution)/shard_map/ppermute | solution.py:1109
  468.8 32.9 %collective-permute-start.36 = (bf16[640,512]{1,0:T(8,128)(2,1)}, bf16[640,512]{1,0:T(8,128)(2,1)S(1)}, u32[]{:S(2)}, u32[]{:S(2)}) collective-permute-start(bf16[640,512]{1,0:T(8,128)(2,1)} %get-tuple-element.217), channel_id=1, source_target_pairs={{0,2},{1,3},{2,0},{3,1},{16,18},{17,19},{18,16},{19,17},{4,6},{5,7... | collective-permute-start | bytes 1966088 | tf_op jit(solution)/shard_map/ppermute | solution.py:1109
  469.3 38.8 %collective-permute-start.38 = (bf16[640,512]{1,0:T(8,128)(2,1)}, bf16[640,512]{1,0:T(8,128)(2,1)S(1)}, u32[]{:S(2)}, u32[]{:S(2)}) collective-permute-start(bf16[640,512]{1,0:T(8,128)(2,1)} %get-tuple-element.226), channel_id=1, source_target_pairs={{0,16},{1,17},{2,18},{3,19},{16,0},{17,1},{18,2},{19,3},{4,20},{5,... | collective-permute-start | bytes 1966088 | tf_op jit(solution)/shard_map/ppermute | solution.py:1109
  470.8 37.3 %collective-permute-start.37 = (bf16[640,512]{1,0:T(8,128)(2,1)}, bf16[640,512]{1,0:T(8,128)(2,1)S(1)}, u32[]{:S(2)}, u32[]{:S(2)}) collective-permute-start(bf16[640,512]{1,0:T(8,128)(2,1)} %get-tuple-element.233), channel_id=1, source_target_pairs={{0,3},{1,2},{2,1},{3,0},{16,19},{17,18},{18,17},{19,16},{4,7},{5,6... | collective-permute-start | bytes 1966088 | tf_op jit(solution)/shard_map/ppermute | solution.py:1109
  481.4 27.9 %collective-permute-start.39 = (bf16[640,512]{1,0:T(8,128)(2,1)}, bf16[640,512]{1,0:T(8,128)(2,1)}, u32[]{:S(2)}, u32[]{:S(2)}) collective-permute-start(bf16[640,512]{1,0:T(8,128)(2,1)} %get-tuple-element.234), channel_id=1, source_target_pairs={{0,17},{1,16},{2,19},{3,18},{16,1},{17,0},{18,3},{19,2},{4,21},{5,... | collective-permute-start | bytes 1966088 | tf_op jit(solution)/shard_map/ppermute | solution.py:1109
  484.4 24.8 %collective-permute-start.41 = (bf16[1,640,512]{2,1,0:T(8,128)(2,1)}, bf16[1,640,512]{2,1,0:T(8,128)(2,1)}, u32[]{:S(2)}, u32[]{:S(2)}) collective-permute-start(bf16[1,640,512]{2,1,0:T(8,128)(2,1)} %shard_map.290), channel_id=1, source_target_pairs={{0,1},{1,0},{2,3},{3,2},{4,5},{5,4},{6,7},{7,6},{8,9},{9,8},{10,11... | collective-permute-start | bytes 1966088 | tf_op jit(solution)/shard_map/ppermute | solution.py:1109
  518.7 109.9 %all-gather.12.cloned.1.call-start = ((), (), s32[]{:S(2)}) async-start(), calls=%async_computation.9 | async-start | bytes 2621440 | tf_op jit(solution)/shard_map/all_gather | solution.py:1113
  520.2 41.7 %collective-permute-start.42 = (bf16[640,1408]{1,0:T(8,128)(2,1)S(1)}, bf16[640,1408]{1,0:T(8,128)(2,1)}, u32[]{:S(2)}, u32[]{:S(2)}) collective-permute-start(bf16[640,1408]{1,0:T(8,128)(2,1)S(1)} %copy-done.5), channel_id=1, source_target_pairs={{0,2},{1,3},{2,0},{3,1},{4,6},{5,7},{6,4},{7,5},{8,10},{9,11},{10,... | collective-permute-start | bytes 5406728 | tf_op jit(solution)/shard_map/ppermute | solution.py:1109
  574.4 254.2 %reduce-scatter.11.cloned.1.call-start = ((), (), s32[]{:S(2)}) async-start(), calls=%async_computation.11 | async-start | bytes 2621440 | tf_op jit(solution)/shard_map/reduce_scatter | solution.py:1117
  574.7 42.3 %collective-permute-start.43 = (bf16[640,1408]{1,0:T(8,128)(2,1)S(1)}, bf16[640,1408]{1,0:T(8,128)(2,1)S(1)}, u32[]{:S(2)}, u32[]{:S(2)}) collective-permute-start(bf16[640,1408]{1,0:T(8,128)(2,1)S(1)} %copy-done.13), channel_id=1, source_target_pairs={{0,2},{1,3},{2,0},{3,1},{4,6},{5,7},{6,4},{7,5},{8,10},{9,11},{10,... | collective-permute-start | bytes 5406728 | tf_op jit(solution)/shard_map/ppermute | solution.py:1109
  575.7 6.8 collective-permute-start.44
  575.7 73.6 %collective-permute-start.45 = (bf16[1,512,1408]{2,1,0:T(8,128)(2,1)}, bf16[1,512,1408]{2,1,0:T(8,128)(2,1)}, u32[]{:S(2)}, u32[]{:S(2)}) collective-permute-start(bf16[1,512,1408]{2,1,0:T(8,128)(2,1)} %get-tuple-element.254), channel_id=1, source_target_pairs={{0,2},{1,3},{2,0},{3,1},{4,6},{5,7},{6,4},{7,5},{8,10},{9,11},{10,... | collective-permute-start | bytes 4325384 | tf_op jit(solution)/shard_map/ppermute | solution.py:1109
  627.2 75.6 %collective-permute-start.53 = (bf16[4,640,512]{2,1,0:T(8,128)(2,1)}, bf16[4,640,512]{2,1,0:T(8,128)(2,1)}, u32[]{:S(2)}, u32[]{:S(2)}) collective-permute-start(bf16[4,640,512]{2,1,0:T(8,128)(2,1)} %shard_map.296), channel_id=1, source_target_pairs={{0,16},{1,17},{2,18},{3,19},{16,0},{17,1},{18,2},{19,3},{4,20},{5,... | collective-permute-start | bytes 7864328 | tf_op jit(solution)/shard_map/ppermute | solution.py:1109
  656.2 28.6 %collective-permute-start.51 = (bf16[512,1024]{1,0:T(8,128)(2,1)}, bf16[512,1024]{1,0:T(8,128)(2,1)S(1)}, u32[]{:S(2)}, u32[]{:S(2)}) collective-permute-start(bf16[512,1024]{1,0:T(8,128)(2,1)} %shard_map.299.rows_ref), channel_id=1, source_target_pairs={{0,2},{1,3},{2,0},{3,1},{4,6},{5,7},{6,4},{7,5},{8,10},{9,11},{10,... | collective-permute-start | bytes 3145736 | tf_op jit(solution)/shard_map/ppermute | solution.py:1109
  657.2 27.6 %collective-permute-start.49 = (bf16[512,512]{1,0:T(8,128)(2,1)}, bf16[512,512]{1,0:T(8,128)(2,1)S(1)}, u32[]{:S(2)}, u32[]{:S(2)}) collective-permute-start(bf16[512,512]{1,0:T(8,128)(2,1)} %get-tuple-element.268), channel_id=1, source_target_pairs={{0,1},{1,0},{2,3},{3,2},{4,5},{5,4},{6,7},{7,6},{8,9},{9,8},{10,11... | collective-permute-start | bytes 1572872 | tf_op jit(solution)/shard_map/ppermute | solution.py:1109
  657.2 27.6 %collective-permute-start.50 = (bf16[512,512]{1,0:T(8,128)(2,1)}, bf16[512,512]{1,0:T(8,128)(2,1)S(1)}, u32[]{:S(2)}, u32[]{:S(2)}) collective-permute-start(bf16[512,512]{1,0:T(8,128)(2,1)} %get-tuple-element.269), channel_id=1, source_target_pairs={{0,1},{1,0},{2,3},{3,2},{4,5},{5,4},{6,7},{7,6},{8,9},{9,8},{10,11... | collective-permute-start | bytes 1572872 | tf_op jit(solution)/shard_map/ppermute | solution.py:1109
  674.6 74.0 %collective-permute-start.57 = (bf16[4,512,512]{2,1,0:T(8,128)(2,1)}, bf16[4,512,512]{2,1,0:T(8,128)(2,1)}, u32[]{:S(2)}, u32[]{:S(2)}) collective-permute-start(bf16[4,512,512]{2,1,0:T(8,128)(2,1)} %shard_map.302), channel_id=1, source_target_pairs={{0,16},{16,0},{1,17},{17,1},{2,18},{18,2},{3,19},{19,3},{4,20},{20... | collective-permute-start | bytes 6291464 | tf_op jit(solution)/shard_map/ppermute | solution.py:1109
  701.2 48.1 %collective-permute-start.56 = (bf16[4,512,512]{2,1,0:T(8,128)(2,1)}, bf16[4,512,512]{2,1,0:T(8,128)(2,1)}, u32[]{:S(2)}, u32[]{:S(2)}) collective-permute-start(bf16[4,512,512]{2,1,0:T(8,128)(2,1)} %get-tuple-element.270.refs_0_), channel_id=1, source_target_pairs={{0,2},{1,3},{2,0},{3,1},{4,6},{5,7},{6,4},{7,5},{8,10},{9,11},{10,... | collective-permute-start | bytes 6291464 | tf_op jit(solution)/shard_map/ppermute | solution.py:1109
  702.3 22.1 %collective-permute-start.52 = (bf16[2,640,512]{2,1,0:T(8,128)(2,1)S(1)}, bf16[2,640,512]{2,1,0:T(8,128)(2,1)S(1)}, u32[]{:S(2)}, u32[]{:S(2)}) collective-permute-start(bf16[2,640,512]{2,1,0:T(8,128)(2,1)S(1)} %copy-done.40), channel_id=1, source_target_pairs={{0,1},{1,0},{2,3},{3,2},{4,5},{5,4},{6,7},{7,6},{8,9},{9,8},{10,11... | collective-permute-start | bytes 3932168 | tf_op jit(solution)/shard_map/ppermute | solution.py:1109
  705.7 18.7 %collective-permute-start.54 = (bf16[2,640,512]{2,1,0:T(8,128)(2,1)}, bf16[2,640,512]{2,1,0:T(8,128)(2,1)S(1)}, u32[]{:S(2)}, u32[]{:S(2)}) collective-permute-start(bf16[2,640,512]{2,1,0:T(8,128)(2,1)} %shard_map.306), channel_id=1, source_target_pairs={{0,1},{1,0},{2,3},{3,2},{4,5},{5,4},{6,7},{7,6},{8,9},{9,8},{10,11... | collective-permute-start | bytes 3932168 | tf_op jit(solution)/shard_map/ppermute | solution.py:1109
  724.4 32.2 %collective-permute-start.55 = (bf16[4,512,512]{2,1,0:T(8,128)(2,1)S(1)}, bf16[4,512,512]{2,1,0:T(8,128)(2,1)}, u32[]{:S(2)}, u32[]{:S(2)}) collective-permute-start(bf16[4,512,512]{2,1,0:T(8,128)(2,1)S(1)} %copy-done.2), channel_id=1, source_target_pairs={{0,1},{1,0},{2,3},{3,2},{4,5},{5,4},{6,7},{7,6},{8,9},{9,8},{10,11... | collective-permute-start | bytes 6291464 | tf_op jit(solution)/shard_map/ppermute | solution.py:1109
  749.3 7.3 collective-permute-start.58
  779.7 129.9 %reduce-scatter.9.cloned.1.call-start = ((), (), s32[]{:S(2)}) async-start(), calls=%async_computation.10 | async-start | bytes 2621440 | tf_op jit(solution)/shard_map/reduce_scatter | solution.py:1117
  779.8 99.6 %collective-permute-start.63 = (bf16[3,512,1408]{2,1,0:T(8,128)(2,1)}, bf16[3,512,1408]{2,1,0:T(8,128)(2,1)}, u32[]{:S(2)}, u32[]{:S(2)}) collective-permute-start(bf16[3,512,1408]{2,1,0:T(8,128)(2,1)} %get-tuple-element.284), channel_id=1, source_target_pairs={{0,2},{1,3},{2,0},{3,1},{4,6},{5,7},{6,4},{7,5},{8,10},{9,11},{10,... | collective-permute-start | bytes 12976136 | tf_op jit(solution)/shard_map/ppermute | solution.py:1109
  800.7 35.5 %collective-permute-start.65 = (bf16[1,1408,512]{2,1,0:T(8,128)(2,1)}, bf16[1,1408,512]{2,1,0:T(8,128)(2,1)}, u32[]{:S(2)}, u32[]{:S(2)}) collective-permute-start(bf16[1,1408,512]{2,1,0:T(8,128)(2,1)} %shard_map.309), channel_id=1, source_target_pairs={{0,1},{1,0},{2,3},{3,2},{4,5},{5,4},{6,7},{7,6},{8,9},{9,8},{10,11... | collective-permute-start | bytes 4325384 | tf_op jit(solution)/shard_map/ppermute | solution.py:1109
  806.5 67.8 %collective-permute-start.67 = (bf16[4,512,512]{2,1,0:T(8,128)(2,1)S(1)}, bf16[4,512,512]{2,1,0:T(8,128)(2,1)}, u32[]{:S(2)}, u32[]{:S(2)}) collective-permute-start(bf16[4,512,512]{2,1,0:T(8,128)(2,1)S(1)} %copy-done.17), channel_id=1, source_target_pairs={{0,16},{16,0},{1,17},{17,1},{2,18},{18,2},{3,19},{19,3},{4,20},{20... | collective-permute-start | bytes 6291464 | tf_op jit(solution)/shard_map/ppermute | solution.py:1109
  831.4 13.6 %collective-permute-start.64 = (bf16[1,1408,512]{2,1,0:T(8,128)(2,1)}, bf16[1,1408,512]{2,1,0:T(8,128)(2,1)}, u32[]{:S(2)}, u32[]{:S(2)}) collective-permute-start(bf16[1,1408,512]{2,1,0:T(8,128)(2,1)} %shard_map.308), channel_id=1, source_target_pairs={{0,1},{1,0},{2,3},{3,2},{4,5},{5,4},{6,7},{7,6},{8,9},{9,8},{10,11... | collective-permute-start | bytes 4325384 | tf_op jit(solution)/shard_map/ppermute | solution.py:1109
  836.2 26.8 %collective-permute-start.66 = (bf16[1,512,1408]{2,1,0:T(8,128)(2,1)}, bf16[1,512,1408]{2,1,0:T(8,128)(2,1)}, u32[]{:S(2)}, u32[]{:S(2)}) collective-permute-start(bf16[1,512,1408]{2,1,0:T(8,128)(2,1)} %get-tuple-element.289), channel_id=1, source_target_pairs={{0,1},{1,0},{2,3},{3,2},{4,5},{5,4},{6,7},{7,6},{8,9},{9,8},{10,11... | collective-permute-start | bytes 4325384 | tf_op jit(solution)/shard_map/ppermute | solution.py:1109
  836.2 8.4 collective-permute-start.70
  844.7 26.4 %collective-permute-start.68 = (bf16[1,512,512]{2,1,0:T(8,128)(2,1)}, bf16[1,512,512]{2,1,0:T(8,128)(2,1)S(1)}, u32[]{:S(2)}, u32[]{:S(2)}) collective-permute-start(bf16[1,512,512]{2,1,0:T(8,128)(2,1)} %shard_map.316), channel_id=1, source_target_pairs={{0,16},{16,0},{1,17},{17,1},{2,18},{18,2},{3,19},{19,3},{4,20},{20... | collective-permute-start | bytes 1572872 | tf_op jit(solution)/shard_map/ppermute | solution.py:1109
  845.0 34.4 %collective-permute-start.71 = (f32[42,512]{1,0:T(8,128)S(1)}, f32[42,512]{1,0:T(8,128)S(1)}, u32[]{:S(2)}, u32[]{:S(2)}) collective-permute-start(f32[42,512]{1,0:T(8,128)S(1)} %add.114), channel_id=1, source_target_pairs={{0,16},{16,0},{1,17},{17,1},{2,18},{18,2},{3,19},{19,3},{4,20},{20... | collective-permute-start | bytes 258056 | tf_op jit(solution)/shard_map/ppermute | solution.py:1109
  (104 other events, 898.7 us)
Sparse Core Ops, SparseCore 0:
  9.6 48.7 all-gather.5
  75.2 44.7 all-gather.7
  203.7 44.7 reduce-scatter.4
  265.1 45.8 all-gather.9
  518.8 44.6 reduce-scatter.6
  574.6 44.7 all-gather.11
  779.8 43.1 reduce-scatter.10
  836.3 42.6 reduce-scatter.8
